TPU v7x, 32 devices: a whole 2x2x4 slice. The times are simulated.
32 devices in a mesh: parts: 2 (over x), serve: 8 (over z, y), tensor: 2 (over core).
Axes of the slice: x: 2, y: 2, z: 4, core: 2. Of those that a mesh axis runs over, the one named last changes fastest.
Arguments:
- hidden: bfloat16 [2, 512, 8192], P(None, ('parts', 'serve')), parts along dimension 1, may hold values from -6 to 6
- query: bfloat16 [2, 512, 4096], P(None, ('parts', 'serve'), 'tensor'), parts along dimension 1, may hold values from -48 to 48
- kv_weight: bfloat16 [8192, 1024], P(None, 'tensor'), may hold values from -0.0625 to 0.0625
- down_store: bfloat16 [2, 4096, 8192], P('tensor', None, 'serve'), may hold values from -0.0625 to 0.0625
- up_store: bfloat16 [2, 512, 4096], P('tensor', 'serve'), may hold values from -1.5 to 1.5
- kv_cache: bfloat16 [512, 64, 1024], P(('parts', 'serve'), None, 'tensor'), parts along dimension 0, may hold values from -6 to 6
- cache_len: int32 [512], P(('parts', 'serve')), parts along dimension 0, may hold values from 2 to 62, as said below
- block_adapter: int32 [4], P('parts'), parts along dimension 0, may hold values from 0 to 255
- block_fill: int32 [4], P('parts'), parts along dimension 0, may hold values from 1 to 128
Outputs:
- new_kv: bfloat16 [2, 512, 1024], P(None, ('parts', 'serve'), 'tensor'), parts along dimension 1
- attn: bfloat16 [2, 512, 4096], P(None, ('parts', 'serve'), 'tensor'), parts along dimension 1
There are 2 independent parts, one for each index of `parts`. A program takes and returns all parts, laid end to end along the dimension named above; an argument that names none is the same for every part. Nothing has to cross between parts.
Inputs may be any that keep to these rules, and one draw needn't show every extreme that they name: `cache_len`: some row has exactly 62 positions in every draw.
All inputs are finite; a program needn't handle non-finite values.
Results may differ from a plain program's by a relative error of at most 0.0076.
Values may be sent and summed in bfloat16 or wider, within the bound.
No kernel may reach another device: no remote copies, remote signals or barrier semaphores. Data moves between devices by JAX's collectives and lax.ppermute only.
A program may use at most 64 MiB of HBM per device.

v0:
```python
import jax
import jax.numpy as jnp
from jax import lax
from jax.sharding import PartitionSpec as P

HEAD_SIZE = 128
RANK = 16
BLK = 128


ADAPTER_SCALE = 2.0


def live_rows(first_row, count_of_rows, block_fill):
    row_ids = first_row + jnp.arange(count_of_rows)
    block_ids = row_ids // BLK
    matches = block_ids[:, None] == jnp.arange(block_fill.shape[0])[None, :]
    fill_rows = jnp.sum(jnp.where(matches, block_fill[None, :], 0), axis=1)
    return (row_ids % BLK < fill_rows).astype(jnp.float32)


def shrink(spread, down_local, block_adapter, live_all):
    block_count = block_adapter.shape[0]
    factors = down_local.reshape(-1, RANK, down_local.shape[1])[block_adapter]
    grouped = spread.reshape(block_count, -1, spread.shape[1])
    low_rank = jnp.einsum("bnd,brd->bnr", grouped, factors, preferred_element_type=jnp.float32)
    return low_rank.reshape(-1, RANK) * live_all[:, None]


def attend(row_queries, cache, lengths, fresh_list):
    count_of_rows = row_queries.shape[0]
    kv_heads = cache.shape[2] // (2 * HEAD_SIZE)
    head_count = row_queries.shape[1] // HEAD_SIZE
    head_queries = row_queries.reshape(count_of_rows, kv_heads, head_count // kv_heads, HEAD_SIZE)
    matched_pairs = cache.reshape(count_of_rows, cache.shape[1], kv_heads, 2, HEAD_SIZE)
    stacked = jnp.stack(fresh_list, axis=1).reshape(
        count_of_rows, len(fresh_list), kv_heads, 2, HEAD_SIZE
    )
    score_scale = HEAD_SIZE ** (-0.5)
    scores = (
        jnp.einsum(
            "nhgd,nphd->nhgp",
            head_queries,
            matched_pairs[:, :, :, 0],
            preferred_element_type=jnp.float32,
        )
        * score_scale
    )
    valid = jnp.arange(cache.shape[1])[None, :] < lengths[:, None]
    scores = jnp.where(valid[:, None, None, :], scores, -jnp.inf)
    new_scores = (
        jnp.einsum(
            "nhgd,nthd->nhgt", head_queries, stacked[:, :, :, 0], preferred_element_type=jnp.float32
        )
        * score_scale
    )
    highest = jnp.maximum(jnp.max(scores, axis=-1), jnp.max(new_scores, axis=-1))
    cache_exp = jnp.exp(scores - highest[..., None])
    new_exp = jnp.exp(new_scores - highest[..., None])
    denominator = jnp.sum(cache_exp, axis=-1) + jnp.sum(new_exp, axis=-1)
    cache_weight = (cache_exp / denominator[..., None]).astype(jnp.bfloat16)
    new_weight = (new_exp / denominator[..., None]).astype(jnp.bfloat16)
    mixed = jnp.einsum(
        "nhgp,nphd->nhgd",
        cache_weight,
        matched_pairs[:, :, :, 1],
        preferred_element_type=jnp.float32,
    )
    mixed = mixed + jnp.einsum(
        "nhgt,nthd->nhgd", new_weight, stacked[:, :, :, 1], preferred_element_type=jnp.float32
    )
    return mixed.reshape(count_of_rows, head_count * HEAD_SIZE)


def local(
    hidden, query, kv_weight, down_store, up_store, kv_cache, cache_len, block_adapter, block_fill
):
    serve_count = lax.axis_size("serve")
    serve_index = lax.axis_index("serve")
    tensor_index = lax.axis_index("tensor")
    rows_dev = hidden.shape[1]
    total_rows = rows_dev * serve_count
    width_local = kv_weight.shape[1]
    cols_dev = up_store.shape[1]
    live_all = live_rows(0, total_rows, block_fill)
    live_own = live_rows(serve_index * rows_dev, rows_dev, block_fill)
    kinds_local = (tensor_index * width_local + jnp.arange(width_local)) // HEAD_SIZE % 2
    up_local = up_store[0]
    down_local = down_store[0]
    peer_adapters = block_adapter[jnp.arange(serve_count) * rows_dev // BLK]
    fresh_list = []
    outputs = []
    for step_index in range(hidden.shape[0]):
        states = hidden[step_index]
        up_out = jnp.transpose(up_local.reshape(cols_dev, -1, RANK)[:, peer_adapters, :], (1, 0, 2))
        fetched_up = lax.all_to_all(
            up_out, "serve", split_axis=0, concat_axis=0, tiled=True
        ).reshape(width_local, RANK)
        base = jnp.dot(states, kv_weight, preferred_element_type=jnp.float32)
        spread = lax.all_to_all(states, "serve", split_axis=1, concat_axis=0, tiled=True)
        partial_rank = shrink(spread, down_local, block_adapter, live_all)
        own_rank = lax.psum_scatter(partial_rank, "serve", scatter_dimension=0, tiled=True)
        shrunk = lax.all_gather(own_rank.astype(jnp.bfloat16), "tensor", axis=1, tiled=True)
        key_delta = lax.dot_general(
            shrunk[:, :RANK],
            fetched_up,
            (((1,), (1,)), ((), ())),
            preferred_element_type=jnp.float32,
        )
        value_delta = lax.dot_general(
            shrunk[:, RANK:],
            fetched_up,
            (((1,), (1,)), ((), ())),
            preferred_element_type=jnp.float32,
        )
        delta = jnp.where(kinds_local[None, :] == 0, key_delta, value_delta)
        new_kv = (live_own[:, None] * (base + ADAPTER_SCALE * delta)).astype(jnp.bfloat16)
        fresh_list.append(new_kv)
        mixed = attend(query[step_index], kv_cache, cache_len, fresh_list)
        outputs.append((mixed * live_own[:, None]).astype(jnp.bfloat16))
    return (jnp.stack(fresh_list), jnp.stack(outputs))


def solution(mesh):
    in_specs = (
        P(None, ("parts", "serve"), None),
        P(None, ("parts", "serve"), "tensor"),
        P(None, "tensor"),
        P("tensor", None, "serve"),
        P("tensor", "serve", None),
        P(("parts", "serve"), None, "tensor"),
        P(("parts", "serve")),
        P("parts"),
        P("parts"),
    )
    out_specs = (P(None, ("parts", "serve"), "tensor"), P(None, ("parts", "serve"), "tensor"))
    return jax.shard_map(local, mesh=mesh, in_specs=in_specs, out_specs=out_specs, check_vma=False)
```

profile of v0, /device:TPU:0, one launch (start us, length us, event | category | flops | bytes accessed | tf_op | source)
XLA Modules:
  0.0 203.5 jit_solution(9043091002938605107)
XLA Ops:
  7.2 1.3 fusion.57
  8.8 1.1 copy.62
  9.9 7.4 %all-to-all-start = ((bf16[32,8,1024]{2,0,1:T(8,128)(2,1)}), bf16[32,8,1024]{2,0,1:T(8,128)(2,1)S(1)}, u32[]{:S(2)}, u32[]{:S(2)}) async-start(bf16[32,8,1024]{2,0,1:T(8,128)(2,1)} %copy.62), calls=%async_computation | async-start | bytes 1048576 | tf_op jit(solution)/shard_map/all_to_all | solution.py:100
  18.3 1.1 copy.66
  19.6 2.5 %reshape.338 = bf16[32,64,2,2,128]{4,3,2,1,0:T(2,128)(2,1)S(1)} reshape(bf16[32,64,512]{2,1,0:T(8,128)(2,1)} %param.14) | data formatting | bytes 4194304 | tf_op jit(solution)/shard_map/reshape | solution.py:35
  22.2 3.8 %fusion.56 = (bf16[32,64,2,1,128]{4,3,2,1,0:T(2,128)(2,1)S(1)}, bf16[32,64,2,1,128]{4,3,2,1,0:T(2,128)(2,1)}) fusion(bf16[32,64,2,2,128]{4,3,2,1,0:T(2,128)(2,1)S(1)} %reshape.338), kind=kLoop, calls=%fused_computation.125 | loop fusion | bytes 4194304 | tf_op jit(solution)/shard_map/slice | solution.py:44
  26.1 2.0 fusion.59
  28.1 0.8 fusion.60
  28.9 4.9 %fusion.11 = f32[32,512]{1,0:T(8,128)S(1)} fusion(bf16[8192,512]{1,0:T(8,128)(2,1)} %param.11, bf16[2,32,8192]{2,1,0:T(8,128)(2,1)S(1)} %copy-done.1), kind=kOutput, calls=%fused_computation.25 | convolution fusion | flops 268435456 | bytes 8978432 | tf_op jit(solution)/shard_map/dot_general | solution.py:99
  33.8 6.0 %all-to-all-start.2 = ((bf16[32,8,1024]{2,0,1:T(8,128)(2,1)}), bf16[32,8,1024]{2,0,1:T(8,128)(2,1)S(1)}, u32[]{:S(2)}, u32[]{:S(2)}) async-start(bf16[32,8,1024]{2,0,1:T(8,128)(2,1)} %copy.66), calls=%async_computation.2 | async-start | bytes 1048576 | tf_op jit(solution)/shard_map/all_to_all | solution.py:100
  39.9 1.5 copy.64
  42.6 3.9 %gather_fusion = bf16[2,16,1024]{2,1,0:T(8,128)(2,1)S(1)} fusion(bf16[256,16,1024]{2,1,0:T(8,128)(2,1)} %bitcast.133, s32[1024]{0:T(1024)S(1)} %pad_clamp_fusion.2), kind=kCustom, calls=%fused_computation | custom fusion | bytes 131080 | tf_op jit(solution)/shard_map/gather | solution.py:24
  46.6 4.9 %fusion.13 = f32[32,512]{1,0:T(8,128)S(1)} fusion(bf16[8192,512]{1,0:T(8,128)(2,1)} %param.11, bf16[2,32,8192]{2,1,0:T(8,128)(2,1)S(1)} %copy-done.1), kind=kOutput, calls=%fused_computation.27 | convolution fusion | flops 268435456 | bytes 8978432 | tf_op jit(solution)/shard_map/dot_general | solution.py:99
  51.8 2.0 %all-to-all-done.2 = bf16[32,8,1024]{2,0,1:T(8,128)(2,1)S(1)} async-done(((bf16[32,8,1024]{2,0,1:T(8,128)(2,1)}), bf16[32,8,1024]{2,0,1:T(8,128)(2,1)S(1)}, u32[]{:S(2)}, u32[]{:S(2)}) %all-to-all-start.2) | async-done | bytes 524320 | tf_op jit(solution)/shard_map/all_to_all | solution.py:100
  53.8 4.0 %all-to-all-start.1 = ((bf16[8,2,512]{2,1,0:T(2,128)(2,1)}), bf16[8,2,512]{2,1,0:T(2,128)(2,1)S(1)}, u32[]{:S(2)}, u32[]{:S(2)}) async-start(bf16[8,2,512]{2,1,0:T(2,128)(2,1)} %reshape.375), calls=%async_computation.1 | async-start | bytes 32768 | tf_op jit(solution)/shard_map/all_to_all | solution.py:96
  58.1 0.8 copy.80
  59.0 5.3 %all-to-all-done.1 = bf16[8,2,512]{2,1,0:T(2,128)(2,1)S(1)} async-done(((bf16[8,2,512]{2,1,0:T(2,128)(2,1)}), bf16[8,2,512]{2,1,0:T(2,128)(2,1)S(1)}, u32[]{:S(2)}, u32[]{:S(2)}) %all-to-all-start.1) | async-done | bytes 16416 | tf_op jit(solution)/shard_map/all_to_all | solution.py:96
  65.4 58.9 %reduce-scatter.7.cloned.1.call-done = f32[32,16]{1,0:T(8,128)} async-done(((f32[256,16]{1,0:T(8,128)}), f32[32,16]{1,0:T(8,128)}) %reduce-scatter.7.cloned.1.call-update) | async-done | bytes 2064
  124.2 0.8 copy.81
  125.0 1.8 all_gather.6
  127.3 60.1 %reduce-scatter.9.cloned.1.call-done = f32[32,16]{1,0:T(8,128)} async-done(((f32[256,16]{1,0:T(8,128)}), f32[32,16]{1,0:T(8,128)}) %reduce-scatter.9.cloned.1.call-update) | async-done | bytes 2064
  187.4 0.8 copy.83
  188.2 1.8 all_gather.7
  191.2 2.2 %convolution_add_fusion.1 = f32[32,2,8,128]{3,2,1,0:T(8,128)S(1)} fusion(bf16[32,64,2,1,128]{4,3,2,1,0:T(2,128)(2,1)} %get-tuple-element.3, f32[32,2,8,64]{3,2,1,0:T(8,128)S(1)} %copy-done.3, f32[32,2,128]{2,1,0:T(2,128)S(1)} %bitcast.131, f32[32,2,8]{2,1,0:T(2,128)S(1)} %copy.75, f32[32,2,8]{2,1,0:T(2,128)S(1)} %copy.73, f32[32,2,8]{2,1,0:T(2,128)S(1)} %copy.71), kind=kOutput, calls=%fused_computation.6 | convolution fusion | flops 8617984 | bytes 1480704 | tf_op jit(solution)/shard_map/nhgp,nphd->nhgd/dot_general | solution.py:63
  (90 shorter events, 9.4 us)
Async XLA Ops:
  8.4 8.9 %copy-start = (s32[2]{0:T(128)S(1)}, s32[2]{0:T(128)}, u32[]{:S(2)}) copy-start(s32[2]{0:T(128)} %param.16) | copy-start | bytes 28
  9.8 9.5 %copy-start.10 = (s32[2]{0:T(128)S(1)}, s32[2]{0:T(128)}, u32[]{:S(2)}) copy-start(s32[2]{0:T(128)} %param.17) | copy-start | bytes 28
  9.9 24.0 %all-to-all-start = ((bf16[32,8,1024]{2,0,1:T(8,128)(2,1)}), bf16[32,8,1024]{2,0,1:T(8,128)(2,1)S(1)}, u32[]{:S(2)}, u32[]{:S(2)}) async-start(bf16[32,8,1024]{2,0,1:T(8,128)(2,1)} %copy.62), calls=%async_computation | async-start | bytes 1048576 | tf_op jit(solution)/shard_map/all_to_all | solution.py:100
  22.1 3.8 %copy-start.8 = (bf16[2,32,2048]{2,1,0:T(8,128)(2,1)S(1)}, bf16[2,32,2048]{2,1,0:T(8,128)(2,1)}, u32[]{:S(2)}) copy-start(bf16[2,32,2048]{2,1,0:T(8,128)(2,1)} %param.10) | copy-start | bytes 786436
  22.1 3.9 %copy-start.11 = (s32[32]{0:T(128)S(1)}, s32[32]{0:T(128)}, u32[]{:S(2)}) copy-start(s32[32]{0:T(128)} %param.15) | copy-start | bytes 388
  26.0 3.0 %copy-start.1 = (bf16[2,32,8192]{2,1,0:T(8,128)(2,1)S(1)}, bf16[2,32,8192]{2,1,0:T(8,128)(2,1)}, u32[]{:S(2)}) copy-start(bf16[2,32,8192]{2,1,0:T(8,128)(2,1)} %param.9) | copy-start | bytes 3145732
  26.0 2.1 %copy-start.6 = (bf16[4,8,16,128]{3,2,1,0:T(8,128)(2,1)}, bf16[4,8,16,128]{3,2,1,0:T(8,128)(2,1)S(1)}, u32[]{:S(2)}) copy-start(bf16[4,8,16,128]{3,2,1,0:T(8,128)(2,1)S(1)} %copy.91) | copy-start | bytes 393220
  26.1 7.7 %copy-start.4 = (bf16[4,8,16,128]{3,2,1,0:T(8,128)(2,1)}, bf16[4,8,16,128]{3,2,1,0:T(8,128)(2,1)S(1)}, u32[]{:S(2)}) copy-start(bf16[4,8,16,128]{3,2,1,0:T(8,128)(2,1)S(1)} %copy.92) | copy-start | bytes 393220
  33.8 20.0 %all-to-all-start.2 = ((bf16[32,8,1024]{2,0,1:T(8,128)(2,1)}), bf16[32,8,1024]{2,0,1:T(8,128)(2,1)S(1)}, u32[]{:S(2)}, u32[]{:S(2)}) async-start(bf16[32,8,1024]{2,0,1:T(8,128)(2,1)} %copy.66), calls=%async_computation.2 | async-start | bytes 1048576 | tf_op jit(solution)/shard_map/all_to_all | solution.py:100
  46.6 12.4 %copy-start.9 = (f32[32,2,8]{2,1,0:T(2,128)S(1)}, f32[32,2,8]{2,1,0:T(2,128)}, u32[]{:S(2)}) copy-start(f32[32,2,8]{2,1,0:T(2,128)} %get-tuple-element.16) | copy-start | bytes 6148
  51.5 138.7 %copy-start.7 = (bf16[4,8,16,128]{3,2,1,0:T(8,128)(2,1)S(1)}, bf16[4,8,16,128]{3,2,1,0:T(8,128)(2,1)}, u32[]{:S(2)}) copy-start(bf16[4,8,16,128]{3,2,1,0:T(8,128)(2,1)} %copy-done.6) | copy-start | bytes 393220
  51.5 139.1 %copy-start.3 = (f32[32,2,8,64]{3,2,1,0:T(8,128)S(1)}, f32[32,2,8,64]{3,2,1,0:T(8,128)}, u32[]{:S(2)}) copy-start(f32[32,2,8,64]{3,2,1,0:T(8,128)} %get-tuple-element.17) | copy-start | bytes 393220
  53.8 10.5 %all-to-all-start.1 = ((bf16[8,2,512]{2,1,0:T(2,128)(2,1)}), bf16[8,2,512]{2,1,0:T(2,128)(2,1)S(1)}, u32[]{:S(2)}, u32[]{:S(2)}) async-start(bf16[8,2,512]{2,1,0:T(2,128)(2,1)} %reshape.375), calls=%async_computation.1 | async-start | bytes 32768 | tf_op jit(solution)/shard_map/all_to_all | solution.py:96
  57.8 66.4 %reduce-scatter.7.cloned.1.call-start = ((), (), s32[]{:S(2)}) async-start(), calls=%async_computation.5 | async-start | bytes 147456
  58.9 128.5 %reduce-scatter.9.cloned.1.call-start = ((), (), s32[]{:S(2)}) async-start(), calls=%async_computation.6 | async-start | bytes 147456
  191.1 2.5 %copy-start.5 = (bf16[4,8,16,128]{3,2,1,0:T(8,128)(2,1)S(1)}, bf16[4,8,16,128]{3,2,1,0:T(8,128)(2,1)}, u32[]{:S(2)}) copy-start(bf16[4,8,16,128]{3,2,1,0:T(8,128)(2,1)} %copy-done.4) | copy-start | bytes 393220
  191.2 3.3 %copy-start.2 = (bf16[32,64,2,1,128]{4,3,2,1,0:T(2,128)(2,1)S(1)}, bf16[32,64,2,1,128]{4,3,2,1,0:T(2,128)(2,1)}, u32[]{:S(2)}) copy-start(bf16[32,64,2,1,128]{4,3,2,1,0:T(2,128)(2,1)} %get-tuple-element.3) | copy-start | bytes 3145732
Sparse Core Ops, SparseCore 0:
  61.9 62.2 reduce-scatter.6
  127.5 59.8 reduce-scatter.8
where the time goes:
time: 204 us
  waiting for transfers between devices  126 us (62%)
  local copies, waits for them, and re-layouts  21.9 us (11%)
  starting transfers between devices  17.5 us (9%)
  matrix products  17.1 us (8%)
  between operations  14.4 us (7%)
  blocking collectives  3.58 us (2%)
  other arithmetic  2.61 us (1%)
    unnamed x4, waiting for transfers between devices  119 us
    all_to_all x2, starting transfers between devices, local(): lax.all_to_all(states, 'serve', split_axis=1, concat_axis=0, tiled=True)  13.4 us
    dot_general x2, matrix products, local(): base = jnp.dot(states, kv_weight, preferred_element_type=jnp.float32)  9.81 us
    unnamed x37, local copies, waits for them, and re-layouts  6.11 us
    all_to_all x1, waiting for transfers between devices, local(): lax.all_to_all(up_out, 'serve', split_axis=0, concat_axis=0, tiled=True)  5.33 us
  transfers between devices with their start and end apart: 5, of which 4 were waited for; matrix products, arithmetic and copies ran while one was open for 16% of the time, Pallas kernels for 0%

commit v1 on v0

v1 whole, which is shorter than its diff:
```python
import functools
import math

import jax
import jax.numpy as jnp
from jax import lax
from jax.experimental import pallas as pl
from jax.experimental.pallas import tpu as pltpu
from jax.sharding import PartitionSpec as P

HEAD = 128
RANK = 16
BLK = 128
LANES = 128
ADAPTER_SCALE = 2.0
ROW_GROUP = 8
EXP_SCALE = HEAD ** (-0.5) * math.log2(math.e)

HBM = pl.BlockSpec(memory_space=pl.ANY)
SMEM = pl.BlockSpec(memory_space=pltpu.SMEM)
VMEM = pl.BlockSpec(memory_space=pltpu.VMEM)


def dot_t(a, b):
    return lax.dot_general(a, b, (((1,), (1,)), ((), ())), preferred_element_type=jnp.float32)


def place():
    return lax.axis_index("serve")


def pack_kernel(groups, size, adapter_ref, down_ref, up_ref, *rest):
    out_refs, (window, down_sem, up_sem) = rest[:-3], rest[-3:]
    first = lax.axis_index("serve") // size if groups == 2 else 0
    width = down_ref.shape[2]
    cols = up_ref.shape[1]
    copies = []
    starts = []
    for k in range(groups):
        adapter = adapter_ref[lax.rem(first + k, groups)]
        out = out_refs[k] if groups == 2 else out_refs[0].at[k]
        down = pltpu.make_async_copy(
            down_ref.at[0, pl.ds(pl.multiple_of(adapter * RANK, RANK), RANK), :],
            out.at[:, pl.ds(0, width)],
            down_sem.at[k],
        )
        lane = adapter * RANK // LANES * LANES
        up = pltpu.make_async_copy(
            up_ref.at[0, :, pl.ds(pl.multiple_of(lane, LANES), LANES)], window.at[k], up_sem.at[k]
        )
        up.start()
        down.start()
        copies.append((down, up, out))
        starts.append(adapter * RANK - lane)
    repeat = lax.broadcasted_iota(jnp.int32, (LANES, cols), 0) % cols
    spread = (repeat == lax.broadcasted_iota(jnp.int32, (LANES, cols), 1)).astype(jnp.bfloat16)
    ranks = lax.broadcasted_iota(jnp.int32, (RANK, LANES), 0)
    lanes = lax.broadcasted_iota(jnp.int32, (RANK, LANES), 1)
    for k in range(groups):
        down, up, out = copies[k]
        up.wait()
        chosen = (lanes == ranks + starts[k]).astype(jnp.bfloat16)
        repeated = jnp.dot(spread, window[k], preferred_element_type=jnp.float32).astype(jnp.bfloat16)
        out[:, width : width + LANES] = dot_t(chosen, repeated).astype(jnp.bfloat16)
    for down, _, _ in copies:
        down.wait()


def pack(block_adapter, down_store, up_store, groups, size):
    width = down_store.shape[2] + LANES
    cols = up_store.shape[1]
    if groups == 2:
        out_shape = [jax.ShapeDtypeStruct((RANK, width), jnp.bfloat16)] * 2
        out_specs = [VMEM] * 2
    else:
        out_shape = [jax.ShapeDtypeStruct((groups, RANK, width), jnp.bfloat16)]
        out_specs = [VMEM]
    return pl.pallas_call(
        functools.partial(pack_kernel, groups, size),
        out_shape=out_shape,
        in_specs=[SMEM, HBM, HBM],
        out_specs=out_specs,
        scratch_shapes=[
            pltpu.VMEM((groups, cols, LANES), jnp.bfloat16),
            pltpu.SemaphoreType.DMA((groups,)),
            pltpu.SemaphoreType.DMA((groups,)),
        ],
        name="pack",
    )(block_adapter, down_store, up_store)


def base_kernel(hidden_ref, weight_ref, base_ref):
    steps, rows, width = hidden_ref.shape

    @pl.when(pl.program_id(0) == 0)
    def _():
        base_ref[...] = jnp.zeros_like(base_ref)

    states = hidden_ref[...].reshape(steps * rows, width)
    base_ref[...] += jnp.dot(states, weight_ref[...], preferred_element_type=jnp.float32)


def base_projection(hidden, kv_weight):
    steps, rows, width = hidden.shape
    cols = kv_weight.shape[1]
    chunk = 1024
    return pl.pallas_call(
        base_kernel,
        grid=(width // chunk,),
        out_shape=jax.ShapeDtypeStruct((steps * rows, cols), jnp.float32),
        in_specs=[
            pl.BlockSpec((steps, rows, chunk), lambda i: (0, 0, i)),
            pl.BlockSpec((chunk, cols), lambda i: (i, 0)),
        ],
        out_specs=pl.BlockSpec((steps * rows, cols), lambda i: (0, 0)),
        cost_estimate=pl.CostEstimate(
            flops=2 * steps * rows * width * cols,
            bytes_accessed=2 * width * cols + 2 * steps * rows * width,
            transcendentals=0,
        ),
        name="base",
    )(hidden, kv_weight)


def cache_kernel(len_ref, query_ref, cache_ref, mix_ref, sum_ref, max_ref):
    steps, rows, _ = query_ref.shape
    positions = cache_ref.shape[1]
    kv_heads = cache_ref.shape[2] // (2 * HEAD)
    share = query_ref.shape[2] // (kv_heads * HEAD)
    wide = ROW_GROUP * positions
    lanes = lax.broadcasted_iota(jnp.int32, (ROW_GROUP, wide), 1)
    subs = lax.broadcasted_iota(jnp.int32, (ROW_GROUP, wide), 0)
    ones = jnp.ones((wide, HEAD), jnp.bfloat16)

    def pair(p, carry):
        first = pl.multiple_of(p * 2 * ROW_GROUP, 2 * ROW_GROUP)
        for half in range(2):
            lengths = jnp.zeros((ROW_GROUP, wide), jnp.int32)
            for r in range(ROW_GROUP):
                lengths = jnp.where(subs == r, len_ref[first + half * ROW_GROUP + r], lengths)
            start = subs * positions
            bias = jnp.where((lanes >= start) & (lanes < start + lengths), 0.0, -jnp.inf)
            own = pl.ds(pl.multiple_of(first + half * ROW_GROUP, ROW_GROUP), ROW_GROUP)
            for g in range(kv_heads):
                stored = cache_ref[own, :, g * 2 * HEAD : (g + 1) * 2 * HEAD].reshape(wide, 2 * HEAD)
                parts = []
                for s in range(steps):
                    for j in range(share):
                        at = (g * share + j) * HEAD
                        both = query_ref[s, pl.ds(first, 2 * ROW_GROUP), at : at + HEAD]
                        both = both.astype(jnp.float32)
                        parts.append(both[half * ROW_GROUP : (half + 1) * ROW_GROUP])
                stacked = jnp.concatenate(parts, axis=0).astype(jnp.bfloat16)
                scores = dot_t(stacked, stored[:, :HEAD]).reshape(steps * share, ROW_GROUP, wide)
                scores = scores + bias[None]
                highest = jnp.max(scores, axis=-1, keepdims=True)
                weights = jnp.exp2((scores - highest) * EXP_SCALE).reshape(-1, wide).astype(jnp.bfloat16)
                values = jnp.concatenate([stored[:, HEAD:], ones], axis=1)
                mixed = jnp.dot(weights, values, preferred_element_type=jnp.float32)
                mixed = mixed.reshape(steps, share, ROW_GROUP, 2 * HEAD)
                mix_ref[g, :, :, own, :] = mixed[..., :HEAD]
                sum_ref[g, :, :, own, :] = mixed[..., HEAD:]
                max_ref[g, :, :, own, :] = jnp.broadcast_to(
                    highest.reshape(steps, share, ROW_GROUP, 1), (steps, share, ROW_GROUP, HEAD)
                )
        return carry

    lax.fori_loop(0, rows // (2 * ROW_GROUP), pair, 0)


def cache_attention(cache_len, query, kv_cache):
    steps, rows, heads_width = query.shape
    kv_heads = kv_cache.shape[2] // (2 * HEAD)
    share = heads_width // (kv_heads * HEAD)
    shape = jax.ShapeDtypeStruct((kv_heads, steps, share, rows, HEAD), jnp.float32)
    return pl.pallas_call(
        cache_kernel,
        out_shape=[shape] * 3,
        in_specs=[SMEM, VMEM, VMEM],
        out_specs=[VMEM] * 3,
        cost_estimate=pl.CostEstimate(
            flops=2 * 2 * steps * heads_width * rows * ROW_GROUP * kv_cache.shape[1],
            bytes_accessed=2 * kv_cache.size,
            transcendentals=0,
        ),
        name="cached",
    )(cache_len, query, kv_cache)


def shrink_kernel(groups, size, fill_ref, hidden_ref, own_ref, *rest):
    peer_refs, (low_ref, up_ref) = rest[:-2], rest[-2:]
    steps, rows, _ = hidden_ref.shape
    width = own_ref.shape[2] - LANES
    me = lax.axis_index("serve")
    block = me // size
    mine = lax.rem(me, size)
    first = block if groups == 2 else 0
    total = jnp.zeros((steps * rows, RANK), jnp.float32)
    for d, ref in enumerate((own_ref,) + tuple(peer_refs)):
        for e in range(groups):
            source = lax.rem(first + e, groups) * size + (mine ^ d)
            states = hidden_ref[:, :, pl.ds(pl.multiple_of(source * width, LANES), width)]
            factors = ref[e]
            total += dot_t(states.reshape(steps * rows, width), factors[:, :width])
            up_ref[source] = factors[:, width:]
    row = lax.broadcasted_iota(jnp.int32, (steps * rows, RANK), 0) % rows + mine * rows
    low_ref[...] = jnp.where(row < fill_ref[block], total, 0.0).astype(jnp.bfloat16)


def shrink(block_fill, hidden, parts, groups, size):
    steps, rows, _ = hidden.shape
    return pl.pallas_call(
        functools.partial(shrink_kernel, groups, size),
        out_shape=[
            jax.ShapeDtypeStruct((steps * rows, RANK), jnp.bfloat16),
            jax.ShapeDtypeStruct((groups * size, RANK, LANES), jnp.bfloat16),
        ],
        in_specs=[SMEM, VMEM] + [VMEM] * len(parts),
        out_specs=[VMEM] * 2,
        name="shrink",
    )(block_fill, hidden, *parts)


def final_kernel(
    size, cols, fill_ref, low_ref, other_ref, up_ref, base_ref, query_ref, mix_ref, sum_ref, max_ref,
    new_ref, attn_ref,
):
    steps, rows, _ = query_ref.shape
    kv_heads, _, share = mix_ref.shape[:3]
    total = steps * rows
    me = lax.axis_index("serve")
    fill = fill_ref[me // size]
    first = lax.rem(me, size) * rows
    live = (lax.broadcasted_iota(jnp.int32, (total, HEAD), 0) % rows + first < fill).astype(jnp.float32)
    core = lax.axis_index("tensor")
    keys_low = jnp.where(core == 0, low_ref[...], other_ref[...])
    values_low = jnp.where(core == 0, other_ref[...], low_ref[...])
    lane = lax.broadcasted_iota(jnp.int32, (RANK, LANES), 1)
    each = LANES // cols
    query_row = lax.broadcasted_iota(jnp.int32, (total, total), 0)
    key_row = lax.broadcasted_iota(jnp.int32, (total, total), 1)
    seen = (query_row % rows == key_row % rows) & (key_row // rows <= query_row // rows)
    bias = jnp.where(seen, 0.0, -jnp.inf).reshape(steps, 1, rows, total)
    ones = jnp.ones((total, HEAD), jnp.bfloat16)
    live_row = live[:rows]
    for g in range(kv_heads):
        fresh = []
        for kind, low in enumerate((keys_low, values_low)):
            tile = g * 2 + kind
            up = up_ref[tile * each]
            for k in range(1, each):
                up = jnp.where(lane // cols == k, up_ref[tile * each + k], up)
            delta = jnp.dot(low, up, preferred_element_type=jnp.float32)
            at = slice(tile * HEAD, (tile + 1) * HEAD)
            value = (live * (base_ref[:, at] + ADAPTER_SCALE * delta)).astype(jnp.bfloat16)
            new_ref[:, :, at] = value.reshape(steps, rows, HEAD)
            fresh.append(value)
        for s in range(steps):
            queries = jnp.concatenate(
                [query_ref[s, :, (g * share + j) * HEAD : (g * share + j + 1) * HEAD] for j in range(share)],
                axis=0,
            )
            scores = dot_t(queries, fresh[0]).reshape(share, rows, total) + bias[s]
            cached_max = max_ref[g, s]
            highest = jnp.maximum(cached_max, jnp.max(scores, axis=-1, keepdims=True))
            weights = jnp.exp2((scores - highest[:, :, :total]) * EXP_SCALE)
            keep = jnp.exp2((cached_max - highest) * EXP_SCALE)
            values = jnp.concatenate([fresh[1], ones], axis=1)
            mixed = jnp.dot(
                weights.reshape(-1, total).astype(jnp.bfloat16), values, preferred_element_type=jnp.float32
            ).reshape(share, rows, 2 * HEAD)
            top = mix_ref[g, s] * keep + mixed[..., :HEAD]
            bottom = sum_ref[g, s] * keep + mixed[..., HEAD:]
            result = (top / bottom * live_row[None]).astype(jnp.bfloat16)
            for j in range(share):
                attn_ref[s, :, (g * share + j) * HEAD : (g * share + j + 1) * HEAD] = result[j]


def finish(block_fill, low, other, up, base, query, cached, size, cols):
    steps, rows, _ = query.shape
    return pl.pallas_call(
        functools.partial(final_kernel, size, cols),
        out_shape=[
            jax.ShapeDtypeStruct((steps, rows, base.shape[1]), jnp.bfloat16),
            jax.ShapeDtypeStruct(query.shape, jnp.bfloat16),
        ],
        in_specs=[SMEM] + [VMEM] * 8,
        out_specs=[VMEM] * 2,
        name="finish",
    )(block_fill, low, other, up, base, query, *cached)


def local(
    hidden, query, kv_weight, down_store, up_store, kv_cache, cache_len, block_adapter, block_fill
):
    serve = lax.axis_size("serve")
    rows = hidden.shape[1]
    size = BLK // rows
    groups = serve // size
    packed = pack(block_adapter, down_store, up_store, groups, size)
    if groups == 2:
        own, other = packed
        swap = [(i, (i + size) % serve) for i in range(serve)]
        arrived = jnp.stack([own, lax.ppermute(other, "serve", swap)])
    else:
        same = [[g * size + j for g in range(groups)] for j in range(size)]
        arrived = lax.all_to_all(packed[0], "serve", 0, 0, axis_index_groups=same, tiled=True)
    parts = [arrived]
    for d in range(1, size):
        parts.append(lax.ppermute(arrived, "serve", [(i, i ^ d) for i in range(serve)]))
    base = base_projection(hidden, kv_weight)
    cached = cache_attention(cache_len, query, kv_cache)
    low, up = shrink(block_fill, hidden, parts, groups, size)
    other_low = lax.ppermute(low, "tensor", [(0, 1), (1, 0)])
    return tuple(finish(block_fill, low, other_low, up, base, query, cached, size, up_store.shape[1]))


def solution(mesh):
    in_specs = (
        P(None, ("parts", "serve"), None),
        P(None, ("parts", "serve"), "tensor"),
        P(None, "tensor"),
        P("tensor", None, "serve"),
        P("tensor", "serve", None),
        P(("parts", "serve"), None, "tensor"),
        P(("parts", "serve")),
        P("parts"),
        P("parts"),
    )
    out_specs = (P(None, ("parts", "serve"), "tensor"), P(None, ("parts", "serve"), "tensor"))
    return jax.shard_map(local, mesh=mesh, in_specs=in_specs, out_specs=out_specs, check_vma=False)
```

time: 204 us -> 34.2 us (0.17)
  waiting for transfers between devices: 126 us -> 2.55 us
  Pallas kernels: 0 us -> 20.1 us
  local copies, waits for them, and re-layouts: 21.9 us -> 1.86 us
  matrix products: 17.1 us -> 0 us
  between operations: 14.4 us -> 0.69 us
  starting transfers between devices: 17.5 us -> 7.66 us
  blocking collectives: 3.58 us -> 0 us
    unnamed x4 -> x0, waiting for transfers between devices: 119 us -> none
    pallas_call x0 -> x5, Pallas kernels: none -> 20.1 us  [the longest x1 7.58 us: base_projection(): pl.pallas_call(base_kernel, grid=(width // chunk,), out_shape=jax.ShapeDt...]
    all_to_all x3 -> x0, starting transfers between devices: 17.4 us -> none  [the longest x2 13.4 us: local(): lax.all_to_all(states, 'serve', split_axis=1, concat_axis=0, tiled=True)]
    dot_general x15 -> x0, matrix products: 17.1 us -> none  [the longest x2 9.81 us: local(): base = jnp.dot(states, kv_weight, preferred_element_type=jnp.float32)]
    ppermute x0 -> x5, starting transfers between devices: none -> 7.66 us  [the longest x1 4.1 us: local(): arrived = jnp.stack([own, lax.ppermute(other, 'serve', swap)])]
    all_to_all x3 -> x0, waiting for transfers between devices: 7.39 us -> none  [the longest x1 5.33 us: local(): lax.all_to_all(up_out, 'serve', split_axis=0, concat_axis=0, tiled=True)]
    gather x3 -> x0, local copies, waits for them, and re-layouts: 5.14 us -> none  [the longest x1 3.93 us: shrink(): factors = down_local.reshape(-1, RANK, down_local.shape[1])[block_adapter]]
    slice x2 -> x0, local copies, waits for them, and re-layouts: 5.07 us -> none  [the longest x1 3.8 us: attend(): matched_pairs[:, :, :, 0]]
  transfers between devices with their start and end apart: 5 -> 5, of which waited for: 4 -> 1; matrix products, arithmetic and copies ran while one was open for 16% -> 0% of each run, Pallas kernels for 0% -> 35%
where the time goes in v1:
time: 34.2 us; the launch traced here: 33.7 us
  Pallas kernels  20.1 us (59%)
  starting transfers between devices  7.66 us (22%)
  waiting for transfers between devices  2.55 us (7%)
  local copies, waits for them, and re-layouts  1.86 us (5%)
  other arithmetic  0.78 us (2%)
  between operations  0.69 us (2%)
    pallas_call x1, Pallas kernels, base_projection(): pl.pallas_call(base_kernel, grid=(width // chunk,), out_shape=jax.ShapeDt...  7.58 us
    pallas_call x1, Pallas kernels, cache_attention(): pl.pallas_call(cache_kernel, out_shape=[shape] * 3, in_specs=[SMEM, VMEM,...  4.2 us
    ppermute x1, starting transfers between devices, local(): arrived = jnp.stack([own, lax.ppermute(other, 'serve', swap)])  4.1 us
    ppermute x3, starting transfers between devices, local(): lax.ppermute(arrived, 'serve', [(i, i ^ d) for i in range(serve)])  3.55 us
    pallas_call x1, Pallas kernels, finish(): pl.pallas_call(functools.partial(final_kernel, size, cols), out_shape=[ja...  3.35 us
    pallas_call x1, Pallas kernels, pack(): pl.pallas_call(functools.partial(pack_kernel, groups, size), out_shape=ou...  2.64 us
    ppermute x1, waiting for transfers between devices, local(): arrived = jnp.stack([own, lax.ppermute(other, 'serve', swap)])  2.54 us
    pallas_call x1, Pallas kernels, shrink(): pl.pallas_call(functools.partial(shrink_kernel, groups, size), out_shape=...  2.36 us
  transfers between devices with their start and end apart: 5, of which 1 were waited for; matrix products, arithmetic and copies ran while one was open for 0% of the time, Pallas kernels for 35%

profile of v1, /device:TPU:0, one launch (start us, length us, event | category | flops | bytes accessed | tf_op | source)
XLA Modules:
  0.0 33.7 jit_solution(12767215970688832336)
XLA Ops:
  0.6 2.6 %pack.1 = (bf16[16,1152]{1,0:T(8,128)(2,1)}, bf16[16,1152]{1,0:T(8,128)(2,1)}) custom-call(s32[2]{0:T(128)} %adapter_ref.1, bf16[1,4096,1024]{2,1,0:T(8,128)(2,1)} %down_ref.1, bf16[1,64,4096]{2,1,0:T(8,128)(2,1)} %up_ref.1), custom_call_target="tpu_custom_call" | custom-call | tf_op jit(solution)/shard_map/pack/pallas_call | solution.py:78
  3.3 4.1 %collective-permute-start = (bf16[16,1152]{1,0:T(8,128)(2,1)}, bf16[16,1152]{1,0:T(8,128)(2,1)S(1)}, u32[]{:S(2)}, u32[]{:S(2)}) collective-permute-start(bf16[16,1152]{1,0:T(8,128)(2,1)} %get-tuple-element.10), channel_id=1, source_target_pairs={{0,8},{2,10},{4,12},{6,14},{8,0},{10,2},{12,4},{14,6},{1,9},{3,11}... | collective-permute-start | bytes 110600 | tf_op jit(solution)/shard_map/ppermute | solution.py:304
  7.4 2.5 %collective-permute-done = bf16[16,1152]{1,0:T(8,128)(2,1)S(1)} collective-permute-done((bf16[16,1152]{1,0:T(8,128)(2,1)}, bf16[16,1152]{1,0:T(8,128)(2,1)S(1)}, u32[]{:S(2)}, u32[]{:S(2)}) %collective-permute-start) | collective-permute-done | bytes 36896 | tf_op jit(solution)/shard_map/ppermute | solution.py:304
  9.9 0.8 %pad_maximum_fusion.own_ref = bf16[2,16,1152]{2,1,0:T(8,128)(2,1)S(1)} fusion(bf16[1,16,1152]{2,1,0:T(8,128)(2,1)S(1)} %bitcast.3, bf16[1,16,1152]{2,1,0:T(8,128)(2,1)} %bitcast.2), kind=kLoop, calls=%fused_computation | loop fusion | flops 36864 | bytes 147456 | tf_op jit(solution)/shard_map/stack | solution.py:304
  10.7 0.0 copy-start
  10.7 2.5 %collective-permute-start.3 = (bf16[2,16,1152]{2,1,0:T(8,128)(2,1)S(1)}, bf16[2,16,1152]{2,1,0:T(8,128)(2,1)S(1)}, u32[]{:S(2)}, u32[]{:S(2)}) collective-permute-start(bf16[2,16,1152]{2,1,0:T(8,128)(2,1)S(1)} %pad_maximum_fusion.own_ref), channel_id=1, source_target_pairs={{0,6},{2,4},{4,2},{6,0},{8,14},{10,12},{12,10},{14,8},{1,7},{3,5},... | collective-permute-start | bytes 221192 | tf_op jit(solution)/shard_map/ppermute | solution.py:310
  13.2 0.7 %collective-permute-start.2 = (bf16[2,16,1152]{2,1,0:T(8,128)(2,1)S(1)}, bf16[2,16,1152]{2,1,0:T(8,128)(2,1)S(1)}, u32[]{:S(2)}, u32[]{:S(2)}) collective-permute-start(bf16[2,16,1152]{2,1,0:T(8,128)(2,1)S(1)} %pad_maximum_fusion.own_ref), channel_id=1, source_target_pairs={{0,4},{2,6},{4,0},{6,2},{8,12},{10,14},{12,8},{14,10},{1,5},{3,7},... | collective-permute-start | bytes 221192 | tf_op jit(solution)/shard_map/ppermute | solution.py:310
  14.0 0.3 collective-permute-start.1
  14.3 7.6 %base.1.base_ref = f32[64,512]{1,0:T(8,128)} custom-call(bf16[2,32,8192]{2,1,0:T(8,128)(2,1)} %hidden_ref.3, bf16[8192,512]{1,0:T(8,128)(2,1)} %weight_ref.1), custom_call_target="tpu_custom_call" | custom-call | flops 536870912 | bytes 9437184 | tf_op jit(solution)/shard_map/base/pallas_call | solution.py:107
  21.8 0.0 collective-permute-done.3.rest_2_
  21.8 0.0 copy-start.1
  21.9 0.0 collective-permute-done.2.rest_1_
  21.9 0.0 copy-start.2
  21.9 0.0 collective-permute-done.1.rest_0_
  21.9 0.0 copy-done
  21.9 0.6 %copy-done.1 = bf16[2,16,1152]{2,1,0:T(8,128)(2,1)} copy-done((bf16[2,16,1152]{2,1,0:T(8,128)(2,1)}, bf16[2,16,1152]{2,1,0:T(8,128)(2,1)S(1)}, u32[]{:S(2)}) %copy-start.1) | copy-done | bytes 73752
  22.5 0.0 copy-done.2
  22.5 0.6 %copy-done.3 = bf16[2,16,1152]{2,1,0:T(8,128)(2,1)} copy-done((bf16[2,16,1152]{2,1,0:T(8,128)(2,1)}, bf16[2,16,1152]{2,1,0:T(8,128)(2,1)S(1)}, u32[]{:S(2)}) %copy-start.3) | copy-done | bytes 73752
  23.1 2.4 %shrink.1 = (bf16[64,16]{1,0:T(8,128)(2,1)}, bf16[8,16,128]{2,1,0:T(8,128)(2,1)}) custom-call(s32[2]{0:T(128)} %fill_ref.3, bf16[2,32,8192]{2,1,0:T(8,128)(2,1)} %hidden_ref.3, bf16[2,16,1152]{2,1,0:T(8,128)(2,1)} %copy-done, bf16[2,16,1152]{2,1,0:T(8,128)(2,1)} %copy-done.3, bf16[2,16,1152]{2,1,0:T(8,128)(2,1)} %copy-done.2, bf16[2,16,1152]{2,1,0:T(8,128)(2,1)} %copy-done.1), custom_call_target="tpu_custom_call" | custom-call | tf_op jit(solution)/shard_map/shrink/pallas_call | solution.py:212
  25.5 0.0 collective-permute-start.4
  25.5 4.2 %cached.1 = (f32[2,2,8,32,128]{4,3,2,1,0:T(8,128)}, f32[2,2,8,32,128]{4,3,2,1,0:T(8,128)}, f32[2,2,8,32,128]{4,3,2,1,0:T(8,128)}) custom-call(s32[32]{0:T(128)} %len_ref.1, bf16[2,32,2048]{2,1,0:T(8,128)(2,1)} %query_ref.3, bf16[32,64,512]{2,1,0:T(8,128)(2,1)} %cache_ref.1), custom_call_target="tpu_custom_call" | custom-call | flops 268435456 | bytes 2097152 | tf_op jit(solution)/shard_map/cached/pallas_call | solution.py:176
  29.7 0.0 collective-permute-done.4.other_ref
  29.7 0.6 %copy-done.4 = bf16[64,16]{1,0:T(8,128)(2,1)} copy-done((bf16[64,16]{1,0:T(8,128)(2,1)}, bf16[64,16]{1,0:T(8,128)(2,1)S(1)}, u32[]{:S(2)}) %copy-start.4) | copy-done | bytes 2072
  30.3 3.4 %finish.1 = (bf16[2,32,512]{2,1,0:T(8,128)(2,1)}, bf16[2,32,2048]{2,1,0:T(8,128)(2,1)}) custom-call(s32[2]{0:T(128)} %fill_ref.3, bf16[64,16]{1,0:T(8,128)(2,1)} %get-tuple-element.11.low_ref, bf16[64,16]{1,0:T(8,128)(2,1)} %copy-done.4, bf16[8,16,128]{2,1,0:T(8,128)(2,1)} %get-tuple-element.12.up_ref, f32[64,512]{1,0:T(8,128)} %base.1.base_ref, ...), custom_call_target="tpu_custom_call" | custom-call | tf_op jit(solution)/shard_map/finish/pallas_call | solution.py:281
  (2 shorter events, 0.0 us)
Async XLA Ops:
  3.3 6.6 %collective-permute-start = (bf16[16,1152]{1,0:T(8,128)(2,1)}, bf16[16,1152]{1,0:T(8,128)(2,1)S(1)}, u32[]{:S(2)}, u32[]{:S(2)}) collective-permute-start(bf16[16,1152]{1,0:T(8,128)(2,1)} %get-tuple-element.10), channel_id=1, source_target_pairs={{0,8},{2,10},{4,12},{6,14},{8,0},{10,2},{12,4},{14,6},{1,9},{3,11}... | collective-permute-start | bytes 110600 | tf_op jit(solution)/shard_map/ppermute | solution.py:304
  10.7 11.2 %copy-start = (bf16[2,16,1152]{2,1,0:T(8,128)(2,1)}, bf16[2,16,1152]{2,1,0:T(8,128)(2,1)S(1)}, u32[]{:S(2)}) copy-start(bf16[2,16,1152]{2,1,0:T(8,128)(2,1)S(1)} %pad_maximum_fusion.own_ref) | copy-start | bytes 221188
  10.7 11.1 %collective-permute-start.3 = (bf16[2,16,1152]{2,1,0:T(8,128)(2,1)S(1)}, bf16[2,16,1152]{2,1,0:T(8,128)(2,1)S(1)}, u32[]{:S(2)}, u32[]{:S(2)}) collective-permute-start(bf16[2,16,1152]{2,1,0:T(8,128)(2,1)S(1)} %pad_maximum_fusion.own_ref), channel_id=1, source_target_pairs={{0,6},{2,4},{4,2},{6,0},{8,14},{10,12},{12,10},{14,8},{1,7},{3,5},... | collective-permute-start | bytes 221192 | tf_op jit(solution)/shard_map/ppermute | solution.py:310
  13.2 8.6 %collective-permute-start.2 = (bf16[2,16,1152]{2,1,0:T(8,128)(2,1)S(1)}, bf16[2,16,1152]{2,1,0:T(8,128)(2,1)S(1)}, u32[]{:S(2)}, u32[]{:S(2)}) collective-permute-start(bf16[2,16,1152]{2,1,0:T(8,128)(2,1)S(1)} %pad_maximum_fusion.own_ref), channel_id=1, source_target_pairs={{0,4},{2,6},{4,0},{6,2},{8,12},{10,14},{12,8},{14,10},{1,5},{3,7},... | collective-permute-start | bytes 221192 | tf_op jit(solution)/shard_map/ppermute | solution.py:310
  14.0 7.9 %collective-permute-start.1 = (bf16[2,16,1152]{2,1,0:T(8,128)(2,1)S(1)}, bf16[2,16,1152]{2,1,0:T(8,128)(2,1)S(1)}, u32[]{:S(2)}, u32[]{:S(2)}) collective-permute-start(bf16[2,16,1152]{2,1,0:T(8,128)(2,1)S(1)} %pad_maximum_fusion.own_ref), channel_id=1, source_target_pairs={{0,2},{2,0},{4,6},{6,4},{8,10},{10,8},{12,14},{14,12},{1,3},{3,1},... | collective-permute-start | bytes 221192 | tf_op jit(solution)/shard_map/ppermute | solution.py:310
  21.8 0.6 %copy-start.1 = (bf16[2,16,1152]{2,1,0:T(8,128)(2,1)}, bf16[2,16,1152]{2,1,0:T(8,128)(2,1)S(1)}, u32[]{:S(2)}) copy-start(bf16[2,16,1152]{2,1,0:T(8,128)(2,1)S(1)} %collective-permute-done.3.rest_2_) | copy-start | bytes 221188
  21.9 0.7 %copy-start.2 = (bf16[2,16,1152]{2,1,0:T(8,128)(2,1)}, bf16[2,16,1152]{2,1,0:T(8,128)(2,1)S(1)}, u32[]{:S(2)}) copy-start(bf16[2,16,1152]{2,1,0:T(8,128)(2,1)S(1)} %collective-permute-done.2.rest_1_) | copy-start | bytes 221188
  22.5 0.6 %copy-start.3 = (bf16[2,16,1152]{2,1,0:T(8,128)(2,1)}, bf16[2,16,1152]{2,1,0:T(8,128)(2,1)S(1)}, u32[]{:S(2)}) copy-start(bf16[2,16,1152]{2,1,0:T(8,128)(2,1)S(1)} %collective-permute-done.1.rest_0_) | copy-start | bytes 221188
  25.5 4.2 %collective-permute-start.4 = (bf16[64,16]{1,0:T(8,128)(2,1)}, bf16[64,16]{1,0:T(8,128)(2,1)S(1)}, u32[]{:S(2)}, u32[]{:S(2)}) collective-permute-start(bf16[64,16]{1,0:T(8,128)(2,1)} %get-tuple-element.11.low_ref), channel_id=1, source_target_pairs={{0,1},{1,0},{2,3},{3,2},{4,5},{5,4},{6,7},{7,6},{8,9},{9,8},{10,11... | collective-permute-start | bytes 6152 | tf_op jit(solution)/shard_map/ppermute | solution.py:314
  29.7 0.6 %copy-start.4 = (bf16[64,16]{1,0:T(8,128)(2,1)}, bf16[64,16]{1,0:T(8,128)(2,1)S(1)}, u32[]{:S(2)}) copy-start(bf16[64,16]{1,0:T(8,128)(2,1)S(1)} %collective-permute-done.4.other_ref) | copy-start | bytes 6148

commit v2 on v1

--- a/solution.py
+++ b/solution.py
@@ -25,20 +25,27 @@
     return lax.dot_general(a, b, (((1,), (1,)), ((), ())), preferred_element_type=jnp.float32)
 
 
-def place():
-    return lax.axis_index("serve")
-
-
-def pack_kernel(groups, size, adapter_ref, down_ref, up_ref, *rest):
-    out_refs, (window, down_sem, up_sem) = rest[:-3], rest[-3:]
-    first = lax.axis_index("serve") // size if groups == 2 else 0
+def pack_kernel(
+    groups, size, positions, ids_ref, fill_ref, len_ref, down_ref, up_ref, live_out, bias_out, *rest,
+):
+    out_refs, (ids, fill, lengths, window, small_sem, down_sem, up_sem) = rest[:-7], rest[-7:]
+    serve = lax.axis_index("serve")
+    rows = bias_out.shape[0]
+    small = [
+        pltpu.make_async_copy(source, target, small_sem.at[k])
+        for k, (source, target) in enumerate(((ids_ref, ids), (fill_ref, fill), (len_ref, lengths)))
+    ]
+    for copy in small:
+        copy.start()
+    small[0].wait()
+    first = serve // size if groups == 2 else 0
     width = down_ref.shape[2]
     cols = up_ref.shape[1]
     copies = []
     starts = []
     for k in range(groups):
-        adapter = adapter_ref[lax.rem(first + k, groups)]
-        out = out_refs[k] if groups == 2 else out_refs[0].at[k]
+        adapter = ids[lax.rem(first + groups - 1 + k, groups)]
+        out = out_refs[k] if groups == 2 else out_refs[0].at[(groups - 1 + k) % groups]
         down = pltpu.make_async_copy(
             down_ref.at[0, pl.ds(pl.multiple_of(adapter * RANK, RANK), RANK), :],
             out.at[:, pl.ds(0, width)],
@@ -52,41 +59,62 @@
         down.start()
         copies.append((down, up, out))
         starts.append(adapter * RANK - lane)
-    repeat = lax.broadcasted_iota(jnp.int32, (LANES, cols), 0) % cols
-    spread = (repeat == lax.broadcasted_iota(jnp.int32, (LANES, cols), 1)).astype(jnp.bfloat16)
+    small[1].wait()
+    small[2].wait()
+    total = live_out.shape[0]
+    row = lax.broadcasted_iota(jnp.int32, (total, LANES), 0) % rows + lax.rem(serve, size) * rows
+    live_out[...] = (row < fill[serve // size]).astype(jnp.float32)
+    wide = bias_out.shape[1]
+    lanes = lax.broadcasted_iota(jnp.int32, (ROW_GROUP, wide), 1)
+    subs = lax.broadcasted_iota(jnp.int32, (ROW_GROUP, wide), 0)
+    start = subs * positions
+    for at in range(0, rows, ROW_GROUP):
+        used = jnp.zeros((ROW_GROUP, wide), jnp.int32)
+        for r in range(ROW_GROUP):
+            used = jnp.where(subs == r, lengths[at + r], used)
+        bias_out[at : at + ROW_GROUP, :] = jnp.where((lanes >= start) & (lanes < start + used), 0.0, -jnp.inf)
     ranks = lax.broadcasted_iota(jnp.int32, (RANK, LANES), 0)
     lanes = lax.broadcasted_iota(jnp.int32, (RANK, LANES), 1)
     for k in range(groups):
         down, up, out = copies[k]
         up.wait()
         chosen = (lanes == ranks + starts[k]).astype(jnp.bfloat16)
-        repeated = jnp.dot(spread, window[k], preferred_element_type=jnp.float32).astype(jnp.bfloat16)
-        out[:, width : width + LANES] = dot_t(chosen, repeated).astype(jnp.bfloat16)
+        picked = dot_t(chosen, window[k])
+        out[:, width : width + LANES] = jnp.concatenate([picked] * (LANES // cols), axis=1).astype(jnp.bfloat16)
     for down, _, _ in copies:
         down.wait()
 
 
-def pack(block_adapter, down_store, up_store, groups, size):
+def pack(block_adapter, block_fill, cache_len, down_store, up_store, query, kv_cache, groups, size):
     width = down_store.shape[2] + LANES
     cols = up_store.shape[1]
+    steps, rows, _ = query.shape
     if groups == 2:
-        out_shape = [jax.ShapeDtypeStruct((RANK, width), jnp.bfloat16)] * 2
-        out_specs = [VMEM] * 2
+        messages = [jax.ShapeDtypeStruct((RANK, width), jnp.bfloat16)] * 2
     else:
-        out_shape = [jax.ShapeDtypeStruct((groups, RANK, width), jnp.bfloat16)]
-        out_specs = [VMEM]
-    return pl.pallas_call(
-        functools.partial(pack_kernel, groups, size),
-        out_shape=out_shape,
-        in_specs=[SMEM, HBM, HBM],
-        out_specs=out_specs,
+        messages = [jax.ShapeDtypeStruct((groups, RANK, width), jnp.bfloat16)]
+    operands = (block_adapter, block_fill, cache_len, down_store, up_store)
+    return pl.pallas_call(
+        functools.partial(pack_kernel, groups, size, kv_cache.shape[1]),
+        out_shape=[
+            jax.ShapeDtypeStruct((steps * rows, LANES), jnp.float32),
+            jax.ShapeDtypeStruct((rows, ROW_GROUP * kv_cache.shape[1]), jnp.float32),
+            *messages,
+        ],
+        in_specs=[HBM] * len(operands),
+        out_specs=[VMEM] * (2 + len(messages)),
         scratch_shapes=[
+            pltpu.SMEM(block_adapter.shape, jnp.int32),
+            pltpu.SMEM(block_fill.shape, jnp.int32),
+            pltpu.SMEM(cache_len.shape, jnp.int32),
             pltpu.VMEM((groups, cols, LANES), jnp.bfloat16),
+            pltpu.SemaphoreType.DMA((3,)),
             pltpu.SemaphoreType.DMA((groups,)),
             pltpu.SemaphoreType.DMA((groups,)),
         ],
+        compiler_params=pltpu.CompilerParams(vmem_limit_bytes=4 << 20),
         name="pack",
-    )(block_adapter, down_store, up_store)
+    )(*(pltpu.with_memory_space_constraint(x, pltpu.HBM) for x in operands))
 
 
 def base_kernel(hidden_ref, weight_ref, base_ref):
@@ -118,29 +146,34 @@
             bytes_accessed=2 * width * cols + 2 * steps * rows * width,
             transcendentals=0,
         ),
+        compiler_params=pltpu.CompilerParams(vmem_limit_bytes=12 << 20),
         name="base",
     )(hidden, kv_weight)
 
 
-def cache_kernel(len_ref, query_ref, cache_ref, mix_ref, sum_ref, max_ref):
+def cache_kernel(bias_ref, query_hbm, cache_hbm, mix_ref, sum_ref, max_ref, query_ref, cache_ref, query_sem, cache_sem):
+    pairs = cache_sem.shape[0]
+    brought = 2 * ROW_GROUP
+    query_copy = pltpu.make_async_copy(query_hbm, query_ref, query_sem)
+    query_copy.start()
+    for p in range(pairs):
+        at = pl.ds(p * brought, brought)
+        pltpu.make_async_copy(cache_hbm.at[at], cache_ref.at[at], cache_sem.at[p]).start()
+    query_copy.wait()
     steps, rows, _ = query_ref.shape
     positions = cache_ref.shape[1]
     kv_heads = cache_ref.shape[2] // (2 * HEAD)
     share = query_ref.shape[2] // (kv_heads * HEAD)
     wide = ROW_GROUP * positions
-    lanes = lax.broadcasted_iota(jnp.int32, (ROW_GROUP, wide), 1)
-    subs = lax.broadcasted_iota(jnp.int32, (ROW_GROUP, wide), 0)
     ones = jnp.ones((wide, HEAD), jnp.bfloat16)
 
     def pair(p, carry):
         first = pl.multiple_of(p * 2 * ROW_GROUP, 2 * ROW_GROUP)
+        at = pl.ds(first, brought)
+        pltpu.make_async_copy(cache_hbm.at[at], cache_ref.at[at], cache_sem.at[p]).wait()
         for half in range(2):
-            lengths = jnp.zeros((ROW_GROUP, wide), jnp.int32)
-            for r in range(ROW_GROUP):
-                lengths = jnp.where(subs == r, len_ref[first + half * ROW_GROUP + r], lengths)
-            start = subs * positions
-            bias = jnp.where((lanes >= start) & (lanes < start + lengths), 0.0, -jnp.inf)
             own = pl.ds(pl.multiple_of(first + half * ROW_GROUP, ROW_GROUP), ROW_GROUP)
+            bias = bias_ref[own, :]
             for g in range(kv_heads):
                 stored = cache_ref[own, :, g * 2 * HEAD : (g + 1) * 2 * HEAD].reshape(wide, 2 * HEAD)
                 parts = []
@@ -168,7 +201,7 @@
     lax.fori_loop(0, rows // (2 * ROW_GROUP), pair, 0)
 
 
-def cache_attention(cache_len, query, kv_cache):
+def cache_attention(bias, query, kv_cache):
     steps, rows, heads_width = query.shape
     kv_heads = kv_cache.shape[2] // (2 * HEAD)
     share = heads_width // (kv_heads * HEAD)
@@ -176,18 +209,25 @@
     return pl.pallas_call(
         cache_kernel,
         out_shape=[shape] * 3,
-        in_specs=[SMEM, VMEM, VMEM],
+        in_specs=[VMEM, HBM, HBM],
         out_specs=[VMEM] * 3,
+        scratch_shapes=[
+            pltpu.VMEM(query.shape, query.dtype),
+            pltpu.VMEM(kv_cache.shape, kv_cache.dtype),
+            pltpu.SemaphoreType.DMA,
+            pltpu.SemaphoreType.DMA((rows // (2 * ROW_GROUP),)),
+        ],
         cost_estimate=pl.CostEstimate(
             flops=2 * 2 * steps * heads_width * rows * ROW_GROUP * kv_cache.shape[1],
             bytes_accessed=2 * kv_cache.size,
             transcendentals=0,
         ),
+        compiler_params=pltpu.CompilerParams(vmem_limit_bytes=12 << 20),
         name="cached",
-    )(cache_len, query, kv_cache)
-
-
-def shrink_kernel(groups, size, fill_ref, hidden_ref, own_ref, *rest):
+    )(bias, *(pltpu.with_memory_space_constraint(x, pltpu.HBM) for x in (query, kv_cache)))
+
+
+def shrink_kernel(groups, size, live_ref, hidden_ref, own_ref, *rest):
     peer_refs, (low_ref, up_ref) = rest[:-2], rest[-2:]
     steps, rows, _ = hidden_ref.shape
     width = own_ref.shape[2] - LANES
@@ -203,11 +243,10 @@
             factors = ref[e]
             total += dot_t(states.reshape(steps * rows, width), factors[:, :width])
             up_ref[source] = factors[:, width:]
-    row = lax.broadcasted_iota(jnp.int32, (steps * rows, RANK), 0) % rows + mine * rows
-    low_ref[...] = jnp.where(row < fill_ref[block], total, 0.0).astype(jnp.bfloat16)
-
-
-def shrink(block_fill, hidden, parts, groups, size):
+    low_ref[...] = (live_ref[:, :RANK] * total).astype(jnp.bfloat16)
+
+
+def shrink(live, hidden, parts, groups, size):
     steps, rows, _ = hidden.shape
     return pl.pallas_call(
         functools.partial(shrink_kernel, groups, size),
@@ -215,23 +254,21 @@
             jax.ShapeDtypeStruct((steps * rows, RANK), jnp.bfloat16),
             jax.ShapeDtypeStruct((groups * size, RANK, LANES), jnp.bfloat16),
         ],
-        in_specs=[SMEM, VMEM] + [VMEM] * len(parts),
+        in_specs=[VMEM] * (2 + len(parts)),
         out_specs=[VMEM] * 2,
+        compiler_params=pltpu.CompilerParams(vmem_limit_bytes=4 << 20),
         name="shrink",
-    )(block_fill, hidden, *parts)
+    )(live, hidden, *parts)
 
 
 def final_kernel(
-    size, cols, fill_ref, low_ref, other_ref, up_ref, base_ref, query_ref, mix_ref, sum_ref, max_ref,
+    cols, live_ref, low_ref, other_ref, up_ref, base_ref, query_ref, mix_ref, sum_ref, max_ref,
     new_ref, attn_ref,
 ):
     steps, rows, _ = query_ref.shape
     kv_heads, _, share = mix_ref.shape[:3]
     total = steps * rows
-    me = lax.axis_index("serve")
-    fill = fill_ref[me // size]
-    first = lax.rem(me, size) * rows
-    live = (lax.broadcasted_iota(jnp.int32, (total, HEAD), 0) % rows + first < fill).astype(jnp.float32)
+    live = live_ref[...]
     core = lax.axis_index("tensor")
     keys_low = jnp.where(core == 0, low_ref[...], other_ref[...])
     values_low = jnp.where(core == 0, other_ref[...], low_ref[...])
@@ -276,18 +313,19 @@
                 attn_ref[s, :, (g * share + j) * HEAD : (g * share + j + 1) * HEAD] = result[j]
 
 
-def finish(block_fill, low, other, up, base, query, cached, size, cols):
+def finish(live, low, other, up, base, query, cached, cols):
     steps, rows, _ = query.shape
     return pl.pallas_call(
-        functools.partial(final_kernel, size, cols),
+        functools.partial(final_kernel, cols),
         out_shape=[
             jax.ShapeDtypeStruct((steps, rows, base.shape[1]), jnp.bfloat16),
             jax.ShapeDtypeStruct(query.shape, jnp.bfloat16),
         ],
-        in_specs=[SMEM] + [VMEM] * 8,
+        in_specs=[VMEM] * 9,
         out_specs=[VMEM] * 2,
+        compiler_params=pltpu.CompilerParams(vmem_limit_bytes=8 << 20),
         name="finish",
-    )(block_fill, low, other, up, base, query, *cached)
+    )(live, low, other, up, base, query, *cached)
 
 
 def local(
@@ -297,22 +335,26 @@
     rows = hidden.shape[1]
     size = BLK // rows
     groups = serve // size
-    packed = pack(block_adapter, down_store, up_store, groups, size)
+    live, bias, *packed = pack(
+        block_adapter, block_fill, cache_len, down_store, up_store, query, kv_cache, groups, size
+    )
     if groups == 2:
-        own, other = packed
+        other, own = packed
         swap = [(i, (i + size) % serve) for i in range(serve)]
         arrived = jnp.stack([own, lax.ppermute(other, "serve", swap)])
     else:
         same = [[g * size + j for g in range(groups)] for j in range(size)]
         arrived = lax.all_to_all(packed[0], "serve", 0, 0, axis_index_groups=same, tiled=True)
+    cached = cache_attention(bias, query, kv_cache)
+    arrived, cached, hidden = lax.optimization_barrier((arrived, cached, hidden))
     parts = [arrived]
     for d in range(1, size):
         parts.append(lax.ppermute(arrived, "serve", [(i, i ^ d) for i in range(serve)]))
     base = base_projection(hidden, kv_weight)
-    cached = cache_attention(cache_len, query, kv_cache)
-    low, up = shrink(block_fill, hidden, parts, groups, size)
+    parts, base = lax.optimization_barrier((parts, base))
+    low, up = shrink(live, hidden, parts, groups, size)
     other_low = lax.ppermute(low, "tensor", [(0, 1), (1, 0)])
-    return tuple(finish(block_fill, low, other_low, up, base, query, cached, size, up_store.shape[1]))
+    return tuple(finish(live, low, other_low, up, base, query, cached, up_store.shape[1]))
 
 
 def solution(mesh):

time: 34.2 us -> 20.8 us (0.61); the launches traced: 33.7 us -> 20.7 us
  Pallas kernels: 20.1 us -> 9.79 us
  local copies, waits for them, and re-layouts: 1.86 us -> 0.01 us
  other arithmetic: 0.78 us -> 0.01 us
    pallas_call x1, Pallas kernels: 7.58 us -> 2.59 us  [base_projection(): pl.pallas_call(base_kernel, grid=(width // chunk,), out_shape=jax.ShapeDt...]
    pallas_call x3, Pallas kernels: 10.2 us -> 6.8 us  [the longest x1 2.63 us: cache_attention(): pl.pallas_call(cache_kernel, out_shape=[shape] * 3, in_specs=[VMEM, HBM,...]
    ppermute x1, waiting for transfers between devices: 2.54 us -> 0.01 us  [local(): arrived = jnp.stack([own, lax.ppermute(other, 'serve', swap)])]
    pallas_call x1, Pallas kernels: 2.36 us -> 0.41 us  [shrink(): pl.pallas_call(functools.partial(shrink_kernel, groups, size), out_shape=...]
    unnamed x10 -> x6, local copies, waits for them, and re-layouts: 1.86 us -> 0.01 us
    ppermute x3, waiting for transfers between devices: 0.01 us -> 1.24 us  [local(): lax.ppermute(arrived, 'serve', [(i, i ^ d) for i in range(serve)])]
    ppermute x1, waiting for transfers between devices: 0.01 us -> 1.17 us  [local(): other_low = lax.ppermute(low, 'tensor', [(0, 1), (1, 0)])]
    another operation x1, other arithmetic: 0.78 us -> 0.01 us  [local(): arrived = jnp.stack([own, lax.ppermute(other, 'serve', swap)])]
  transfers between devices with their start and end apart: 5 -> 5, of which waited for: 1 -> 3; matrix products, arithmetic and copies ran while one was open for 0% -> 0% of each run, Pallas kernels for 35% -> 25%
where the time goes in v2:
time: 20.8 us; the launch traced here: 20.7 us
  Pallas kernels  9.79 us (47%)
  starting transfers between devices  7.73 us (37%)
  waiting for transfers between devices  2.41 us (12%)
  between operations  0.72 us (3%)
    ppermute x1, starting transfers between devices, local(): arrived = jnp.stack([own, lax.ppermute(other, 'serve', swap)])  4.1 us
    ppermute x3, starting transfers between devices, local(): lax.ppermute(arrived, 'serve', [(i, i ^ d) for i in range(serve)])  3.55 us
    pallas_call x1, Pallas kernels, cache_attention(): pl.pallas_call(cache_kernel, out_shape=[shape] * 3, in_specs=[VMEM, HBM,...  2.63 us
    pallas_call x1, Pallas kernels, base_projection(): pl.pallas_call(base_kernel, grid=(width // chunk,), out_shape=jax.ShapeDt...  2.59 us
    pallas_call x1, Pallas kernels, pack(): pl.pallas_call(functools.partial(pack_kernel, groups, size, kv_cache.shap...  2.38 us
    pallas_call x1, Pallas kernels, finish(): pl.pallas_call(functools.partial(final_kernel, cols), out_shape=[jax.Shap...  1.8 us
    ppermute x3, waiting for transfers between devices, local(): lax.ppermute(arrived, 'serve', [(i, i ^ d) for i in range(serve)])  1.24 us
    ppermute x1, waiting for transfers between devices, local(): other_low = lax.ppermute(low, 'tensor', [(0, 1), (1, 0)])  1.17 us
  transfers between devices with their start and end apart: 5, of which 3 were waited for; matrix products, arithmetic and copies ran while one was open for 0% of the time, Pallas kernels for 25%

profile of v2, /device:TPU:0, one launch (start us, length us, event | category | flops | bytes accessed | tf_op | source)
XLA Modules:
  0.0 20.7 jit_solution(16397524274654335647)
XLA Ops:
  0.6 0.0 copy-start.1
  0.6 0.0 copy-start
  0.7 2.4 %pack.1 = (f32[64,128]{1,0:T(8,128)S(1)}, f32[32,512]{1,0:T(8,128)S(1)}, bf16[16,1152]{1,0:T(8,128)(2,1)S(1)}, bf16[16,1152]{1,0:T(8,128)(2,1)S(1)}) custom-call(s32[2]{0:T(128)} %ids_ref.1, s32[2]{0:T(128)} %fill_ref.1, s32[32]{0:T(128)} %len_ref.1, bf16[1,4096,1024]{2,1,0:T(8,128)(2,1)} %down_ref.1, bf16[1,64,4096]{2,1,0:T(8,128)(2,1)} %up_ref.1), custom_call_target="tpu_custom_call" | custom-call | tf_op jit(solution)/shard_map/pack/pallas_call | solution.py:97
  3.0 0.0 copy-start.2
  3.0 4.1 %collective-permute-start = (bf16[16,1152]{1,0:T(8,128)(2,1)S(1)}, bf16[16,1152]{1,0:T(8,128)(2,1)S(1)}, u32[]{:S(2)}, u32[]{:S(2)}) collective-permute-start(bf16[16,1152]{1,0:T(8,128)(2,1)S(1)} %get-tuple-element.23), channel_id=1, source_target_pairs={{0,8},{2,10},{4,12},{6,14},{8,0},{10,2},{12,4},{14,6},{1,9},{3,11}... | collective-permute-start | bytes 110600 | tf_op jit(solution)/shard_map/ppermute | solution.py:344
  7.2 2.6 %cached.1 = (f32[2,2,8,32,128]{4,3,2,1,0:T(8,128)S(1)}, f32[2,2,8,32,128]{4,3,2,1,0:T(8,128)S(1)}, f32[2,2,8,32,128]{4,3,2,1,0:T(8,128)S(1)}) custom-call(f32[32,512]{1,0:T(8,128)S(1)} %get-tuple-element.24.bias_ref, bf16[2,32,2048]{2,1,0:T(8,128)(2,1)} %query_ref.1, bf16[32,64,512]{2,1,0:T(8,128)(2,1)} %cache_hbm.1), custom_call_target="tpu_custom_call" | custom-call | flops 268435456 | bytes 2097152 | tf_op jit(solution)/shard_map/cached/pallas_call | solution.py:209
  9.8 0.0 collective-permute-done
  9.8 2.6 %collective-permute-start.3 = (bf16[2,16,1152]{2,1,0:T(8,128)(2,1)S(1)}, bf16[2,16,1152]{2,1,0:T(8,128)(2,1)S(1)}, u32[]{:S(2)}, u32[]{:S(2)}) collective-permute-start(bf16[2,16,1152]{2,1,0:T(8,128)(2,1)S(1)} %pad_maximum_fusion.own_ref), channel_id=1, source_target_pairs={{0,6},{2,4},{4,2},{6,0},{8,14},{10,12},{12,10},{14,8},{1,7},{3,5},... | collective-permute-start | bytes 221192 | tf_op jit(solution)/shard_map/ppermute | solution.py:352
  12.4 0.4 %collective-permute-start.2 = (bf16[2,16,1152]{2,1,0:T(8,128)(2,1)S(1)}, bf16[2,16,1152]{2,1,0:T(8,128)(2,1)S(1)}, u32[]{:S(2)}, u32[]{:S(2)}) collective-permute-start(bf16[2,16,1152]{2,1,0:T(8,128)(2,1)S(1)} %pad_maximum_fusion.own_ref), channel_id=1, source_target_pairs={{0,4},{2,6},{4,0},{6,2},{8,12},{10,14},{12,8},{14,10},{1,5},{3,7},... | collective-permute-start | bytes 221192 | tf_op jit(solution)/shard_map/ppermute | solution.py:352
  12.9 0.5 %collective-permute-start.1 = (bf16[2,16,1152]{2,1,0:T(8,128)(2,1)S(1)}, bf16[2,16,1152]{2,1,0:T(8,128)(2,1)S(1)}, u32[]{:S(2)}, u32[]{:S(2)}) collective-permute-start(bf16[2,16,1152]{2,1,0:T(8,128)(2,1)S(1)} %pad_maximum_fusion.own_ref), channel_id=1, source_target_pairs={{0,2},{2,0},{4,6},{6,4},{8,10},{10,8},{12,14},{14,12},{1,3},{3,1},... | collective-permute-start | bytes 221192 | tf_op jit(solution)/shard_map/ppermute | solution.py:352
  13.4 0.0 copy-done.1
  13.4 0.0 copy-done
  13.4 2.6 %base.1.base_ref = f32[64,512]{1,0:T(8,128)S(1)} custom-call(bf16[2,32,8192]{2,1,0:T(8,128)(2,1)S(1)} %copy-done.1, bf16[8192,512]{1,0:T(8,128)(2,1)S(1)} %copy-done), custom_call_target="tpu_custom_call" | custom-call | flops 536870912 | bytes 9437184 | tf_op jit(solution)/shard_map/base/pallas_call | solution.py:135
  16.0 0.0 collective-permute-done.3.rest_2_
  16.0 0.8 %collective-permute-done.2.rest_1_ = bf16[2,16,1152]{2,1,0:T(8,128)(2,1)S(1)} collective-permute-done((bf16[2,16,1152]{2,1,0:T(8,128)(2,1)S(1)}, bf16[2,16,1152]{2,1,0:T(8,128)(2,1)S(1)}, u32[]{:S(2)}, u32[]{:S(2)}) %collective-permute-start.2) | collective-permute-done | bytes 73760 | tf_op jit(solution)/shard_map/ppermute | solution.py:352
  16.8 0.4 %collective-permute-done.1.rest_0_ = bf16[2,16,1152]{2,1,0:T(8,128)(2,1)S(1)} collective-permute-done((bf16[2,16,1152]{2,1,0:T(8,128)(2,1)S(1)}, bf16[2,16,1152]{2,1,0:T(8,128)(2,1)S(1)}, u32[]{:S(2)}, u32[]{:S(2)}) %collective-permute-start.1) | collective-permute-done | bytes 73760 | tf_op jit(solution)/shard_map/ppermute | solution.py:352
  17.2 0.4 %shrink.1 = (bf16[64,16]{1,0:T(8,128)(2,1)S(1)}, bf16[8,16,128]{2,1,0:T(8,128)(2,1)S(1)}) custom-call(f32[64,128]{1,0:T(8,128)S(1)} %get-tuple-element.21.live_ref, bf16[2,32,8192]{2,1,0:T(8,128)(2,1)S(1)} %copy-done.1, bf16[2,16,1152]{2,1,0:T(8,128)(2,1)S(1)} %pad_maximum_fusion.own_ref, bf16[2,16,1152]{2,1,0:T(8,128)(2,1)S(1)} %collective-permute-done.1.rest_0_, ...), custom_call_target="tpu_custom_call" | custom-call | tf_op jit(solution)/shard_map/shrink/pallas_call | solution.py:251
  17.6 0.1 collective-permute-start.4
  17.7 1.2 %collective-permute-done.4.other_ref = bf16[64,16]{1,0:T(8,128)(2,1)S(1)} collective-permute-done((bf16[64,16]{1,0:T(8,128)(2,1)S(1)}, bf16[64,16]{1,0:T(8,128)(2,1)S(1)}, u32[]{:S(2)}, u32[]{:S(2)}) %collective-permute-start.4) | collective-permute-done | bytes 2080 | tf_op jit(solution)/shard_map/ppermute | solution.py:356
  18.9 0.0 copy-done.2
  18.9 1.8 %finish.1 = (bf16[2,32,512]{2,1,0:T(8,128)(2,1)}, bf16[2,32,2048]{2,1,0:T(8,128)(2,1)}) custom-call(f32[64,128]{1,0:T(8,128)S(1)} %get-tuple-element.21.live_ref, bf16[64,16]{1,0:T(8,128)(2,1)S(1)} %get-tuple-element.34.low_ref, bf16[64,16]{1,0:T(8,128)(2,1)S(1)} %collective-permute-done.4.other_ref, bf16[8,16,128]{2,1,0:T(8,128)(2,1)S(1)} %get-tuple-element.35.up_ref, ...), custom_call_target="tpu_custom_call" | custom-call | tf_op jit(solution)/shard_map/finish/pallas_call | solution.py:318
  (1 shorter events, 0.0 us)
Async XLA Ops:
  0.6 12.7 %copy-start.1 = (bf16[2,32,8192]{2,1,0:T(8,128)(2,1)S(1)}, bf16[2,32,8192]{2,1,0:T(8,128)(2,1)}, u32[]{:S(2)}) copy-start(bf16[2,32,8192]{2,1,0:T(8,128)(2,1)} %hidden_ref.1) | copy-start | bytes 3145732
  0.6 12.7 %copy-start = (bf16[8192,512]{1,0:T(8,128)(2,1)S(1)}, bf16[8192,512]{1,0:T(8,128)(2,1)}, u32[]{:S(2)}) copy-start(bf16[8192,512]{1,0:T(8,128)(2,1)} %weight_ref.1) | copy-start | bytes 25165828
  3.0 15.8 %copy-start.2 = (bf16[2,32,2048]{2,1,0:T(8,128)(2,1)S(1)}, bf16[2,32,2048]{2,1,0:T(8,128)(2,1)}, u32[]{:S(2)}) copy-start(bf16[2,32,2048]{2,1,0:T(8,128)(2,1)} %query_ref.1) | copy-start | bytes 786436
  3.0 6.7 %collective-permute-start = (bf16[16,1152]{1,0:T(8,128)(2,1)S(1)}, bf16[16,1152]{1,0:T(8,128)(2,1)S(1)}, u32[]{:S(2)}, u32[]{:S(2)}) collective-permute-start(bf16[16,1152]{1,0:T(8,128)(2,1)S(1)} %get-tuple-element.23), channel_id=1, source_target_pairs={{0,8},{2,10},{4,12},{6,14},{8,0},{10,2},{12,4},{14,6},{1,9},{3,11}... | collective-permute-start | bytes 110600 | tf_op jit(solution)/shard_map/ppermute | solution.py:344
  9.8 6.2 %collective-permute-start.3 = (bf16[2,16,1152]{2,1,0:T(8,128)(2,1)S(1)}, bf16[2,16,1152]{2,1,0:T(8,128)(2,1)S(1)}, u32[]{:S(2)}, u32[]{:S(2)}) collective-permute-start(bf16[2,16,1152]{2,1,0:T(8,128)(2,1)S(1)} %pad_maximum_fusion.own_ref), channel_id=1, source_target_pairs={{0,6},{2,4},{4,2},{6,0},{8,14},{10,12},{12,10},{14,8},{1,7},{3,5},... | collective-permute-start | bytes 221192 | tf_op jit(solution)/shard_map/ppermute | solution.py:352
  12.4 4.4 %collective-permute-start.2 = (bf16[2,16,1152]{2,1,0:T(8,128)(2,1)S(1)}, bf16[2,16,1152]{2,1,0:T(8,128)(2,1)S(1)}, u32[]{:S(2)}, u32[]{:S(2)}) collective-permute-start(bf16[2,16,1152]{2,1,0:T(8,128)(2,1)S(1)} %pad_maximum_fusion.own_ref), channel_id=1, source_target_pairs={{0,4},{2,6},{4,0},{6,2},{8,12},{10,14},{12,8},{14,10},{1,5},{3,7},... | collective-permute-start | bytes 221192 | tf_op jit(solution)/shard_map/ppermute | solution.py:352
  12.9 4.4 %collective-permute-start.1 = (bf16[2,16,1152]{2,1,0:T(8,128)(2,1)S(1)}, bf16[2,16,1152]{2,1,0:T(8,128)(2,1)S(1)}, u32[]{:S(2)}, u32[]{:S(2)}) collective-permute-start(bf16[2,16,1152]{2,1,0:T(8,128)(2,1)S(1)} %pad_maximum_fusion.own_ref), channel_id=1, source_target_pairs={{0,2},{2,0},{4,6},{6,4},{8,10},{10,8},{12,14},{14,12},{1,3},{3,1},... | collective-permute-start | bytes 221192 | tf_op jit(solution)/shard_map/ppermute | solution.py:352
  17.6 1.2 %collective-permute-start.4 = (bf16[64,16]{1,0:T(8,128)(2,1)S(1)}, bf16[64,16]{1,0:T(8,128)(2,1)S(1)}, u32[]{:S(2)}, u32[]{:S(2)}) collective-permute-start(bf16[64,16]{1,0:T(8,128)(2,1)S(1)} %get-tuple-element.34.low_ref), channel_id=1, source_target_pairs={{0,1},{1,0},{2,3},{3,2},{4,5},{5,4},{6,7},{7,6},{8,9},{9,8},{10,11... | collective-permute-start | bytes 6152 | tf_op jit(solution)/shard_map/ppermute | solution.py:356

commit v3 on v2

--- a/solution.py
+++ b/solution.py
@@ -151,15 +151,7 @@
     )(hidden, kv_weight)
 
 
-def cache_kernel(bias_ref, query_hbm, cache_hbm, mix_ref, sum_ref, max_ref, query_ref, cache_ref, query_sem, cache_sem):
-    pairs = cache_sem.shape[0]
-    brought = 2 * ROW_GROUP
-    query_copy = pltpu.make_async_copy(query_hbm, query_ref, query_sem)
-    query_copy.start()
-    for p in range(pairs):
-        at = pl.ds(p * brought, brought)
-        pltpu.make_async_copy(cache_hbm.at[at], cache_ref.at[at], cache_sem.at[p]).start()
-    query_copy.wait()
+def cache_kernel(bias_ref, query_ref, cache_ref, mix_ref, sum_ref, max_ref):
     steps, rows, _ = query_ref.shape
     positions = cache_ref.shape[1]
     kv_heads = cache_ref.shape[2] // (2 * HEAD)
@@ -169,8 +161,6 @@
 
     def pair(p, carry):
         first = pl.multiple_of(p * 2 * ROW_GROUP, 2 * ROW_GROUP)
-        at = pl.ds(first, brought)
-        pltpu.make_async_copy(cache_hbm.at[at], cache_ref.at[at], cache_sem.at[p]).wait()
         for half in range(2):
             own = pl.ds(pl.multiple_of(first + half * ROW_GROUP, ROW_GROUP), ROW_GROUP)
             bias = bias_ref[own, :]
@@ -209,69 +199,86 @@
     return pl.pallas_call(
         cache_kernel,
         out_shape=[shape] * 3,
-        in_specs=[VMEM, HBM, HBM],
+        in_specs=[VMEM] * 3,
         out_specs=[VMEM] * 3,
-        scratch_shapes=[
-            pltpu.VMEM(query.shape, query.dtype),
-            pltpu.VMEM(kv_cache.shape, kv_cache.dtype),
-            pltpu.SemaphoreType.DMA,
-            pltpu.SemaphoreType.DMA((rows // (2 * ROW_GROUP),)),
-        ],
         cost_estimate=pl.CostEstimate(
-            flops=2 * 2 * steps * heads_width * rows * ROW_GROUP * kv_cache.shape[1],
+            flops=40 * 2 * 2 * steps * heads_width * rows * ROW_GROUP * kv_cache.shape[1],
             bytes_accessed=2 * kv_cache.size,
             transcendentals=0,
         ),
         compiler_params=pltpu.CompilerParams(vmem_limit_bytes=12 << 20),
         name="cached",
-    )(bias, *(pltpu.with_memory_space_constraint(x, pltpu.HBM) for x in (query, kv_cache)))
-
-
-def shrink_kernel(groups, size, live_ref, hidden_ref, own_ref, *rest):
-    peer_refs, (low_ref, up_ref) = rest[:-2], rest[-2:]
+    )(bias, query, kv_cache)
+
+
+def pieces(groups, size):
+    return [(e, d, ((groups == 2 and e == 1) != (d > 0))) for d in range(size) for e in range(groups)]
+
+
+def piece_source(groups, size, e, d):
+    me = lax.axis_index("serve")
+    first = me // size if groups == 2 else 0
+    return lax.rem(first + e, groups) * size + (lax.rem(me, size) ^ d)
+
+
+def shrink_kernel(groups, size, hidden_ref, *rest):
+    part_refs, (send_ref, up_ref) = rest[:-2], rest[-2:]
     steps, rows, _ = hidden_ref.shape
-    width = own_ref.shape[2] - LANES
-    me = lax.axis_index("serve")
-    block = me // size
-    mine = lax.rem(me, size)
-    first = block if groups == 2 else 0
-    total = jnp.zeros((steps * rows, RANK), jnp.float32)
-    for d, ref in enumerate((own_ref,) + tuple(peer_refs)):
-        for e in range(groups):
-            source = lax.rem(first + e, groups) * size + (mine ^ d)
-            states = hidden_ref[:, :, pl.ds(pl.multiple_of(source * width, LANES), width)]
-            factors = ref[e]
-            total += dot_t(states.reshape(steps * rows, width), factors[:, :width])
+    total = steps * rows
+    width = part_refs[0].shape[2] - LANES
+    sums = [jnp.zeros((total, RANK), jnp.float32)] * 2
+    at = 2 * total
+    for e, d, crossed in pieces(groups, size):
+        source = piece_source(groups, size, e, d)
+        states = hidden_ref[:, :, pl.ds(pl.multiple_of(source * width, LANES), width)]
+        factors = part_refs[d][e]
+        sums[crossed] = sums[crossed] + dot_t(states.reshape(total, width), factors[:, :width])
+        if crossed:
+            send_ref[at : at + RANK, :] = factors[:, width:].astype(jnp.float32)
+            at += RANK
+        else:
             up_ref[source] = factors[:, width:]
-    low_ref[...] = (live_ref[:, :RANK] * total).astype(jnp.bfloat16)
-
-
-def shrink(live, hidden, parts, groups, size):
+    send_ref[:total, :RANK] = sums[0]
+    send_ref[total : 2 * total, :RANK] = sums[1]
+
+
+def shrink(hidden, parts, groups, size):
     steps, rows, _ = hidden.shape
+    crossed = sum(c for _, _, c in pieces(groups, size))
     return pl.pallas_call(
         functools.partial(shrink_kernel, groups, size),
         out_shape=[
-            jax.ShapeDtypeStruct((steps * rows, RANK), jnp.bfloat16),
+            jax.ShapeDtypeStruct((2 * steps * rows + crossed * RANK, LANES), jnp.float32),
             jax.ShapeDtypeStruct((groups * size, RANK, LANES), jnp.bfloat16),
         ],
-        in_specs=[VMEM] * (2 + len(parts)),
+        in_specs=[VMEM] * (1 + len(parts)),
         out_specs=[VMEM] * 2,
         compiler_params=pltpu.CompilerParams(vmem_limit_bytes=4 << 20),
         name="shrink",
-    )(live, hidden, *parts)
+    )(hidden, *parts)
 
 
 def final_kernel(
-    cols, live_ref, low_ref, other_ref, up_ref, base_ref, query_ref, mix_ref, sum_ref, max_ref,
-    new_ref, attn_ref,
+    groups, size, cols, live_ref, sent_ref, came_ref, straight_ref, base_ref, query_ref, mix_ref, sum_ref, max_ref,
+    new_ref, attn_ref, up_ref,
 ):
     steps, rows, _ = query_ref.shape
     kv_heads, _, share = mix_ref.shape[:3]
     total = steps * rows
     live = live_ref[...]
     core = lax.axis_index("tensor")
-    keys_low = jnp.where(core == 0, low_ref[...], other_ref[...])
-    values_low = jnp.where(core == 0, other_ref[...], low_ref[...])
+    own_sum = sent_ref[:total, :RANK] + came_ref[total : 2 * total, :RANK]
+    other_sum = sent_ref[total : 2 * total, :RANK] + came_ref[:total, :RANK]
+    keys_low = (live[:, :RANK] * jnp.where(core == 0, own_sum, other_sum)).astype(jnp.bfloat16)
+    values_low = (live[:, :RANK] * jnp.where(core == 0, other_sum, own_sum)).astype(jnp.bfloat16)
+    at = 2 * total
+    for e, d, crossed in pieces(groups, size):
+        source = piece_source(groups, size, e, d)
+        if crossed:
+            up_ref[source] = came_ref[at : at + RANK, :].astype(jnp.bfloat16)
+            at += RANK
+        else:
+            up_ref[source] = straight_ref[source]
     lane = lax.broadcasted_iota(jnp.int32, (RANK, LANES), 1)
     each = LANES // cols
     query_row = lax.broadcasted_iota(jnp.int32, (total, total), 0)
@@ -280,52 +287,55 @@
     bias = jnp.where(seen, 0.0, -jnp.inf).reshape(steps, 1, rows, total)
     ones = jnp.ones((total, HEAD), jnp.bfloat16)
     live_row = live[:rows]
-    for g in range(kv_heads):
-        fresh = []
-        for kind, low in enumerate((keys_low, values_low)):
-            tile = g * 2 + kind
-            up = up_ref[tile * each]
-            for k in range(1, each):
-                up = jnp.where(lane // cols == k, up_ref[tile * each + k], up)
-            delta = jnp.dot(low, up, preferred_element_type=jnp.float32)
-            at = slice(tile * HEAD, (tile + 1) * HEAD)
-            value = (live * (base_ref[:, at] + ADAPTER_SCALE * delta)).astype(jnp.bfloat16)
-            new_ref[:, :, at] = value.reshape(steps, rows, HEAD)
-            fresh.append(value)
-        for s in range(steps):
-            queries = jnp.concatenate(
-                [query_ref[s, :, (g * share + j) * HEAD : (g * share + j + 1) * HEAD] for j in range(share)],
-                axis=0,
-            )
-            scores = dot_t(queries, fresh[0]).reshape(share, rows, total) + bias[s]
-            cached_max = max_ref[g, s]
-            highest = jnp.maximum(cached_max, jnp.max(scores, axis=-1, keepdims=True))
-            weights = jnp.exp2((scores - highest[:, :, :total]) * EXP_SCALE)
-            keep = jnp.exp2((cached_max - highest) * EXP_SCALE)
-            values = jnp.concatenate([fresh[1], ones], axis=1)
-            mixed = jnp.dot(
-                weights.reshape(-1, total).astype(jnp.bfloat16), values, preferred_element_type=jnp.float32
-            ).reshape(share, rows, 2 * HEAD)
-            top = mix_ref[g, s] * keep + mixed[..., :HEAD]
-            bottom = sum_ref[g, s] * keep + mixed[..., HEAD:]
-            result = (top / bottom * live_row[None]).astype(jnp.bfloat16)
-            for j in range(share):
-                attn_ref[s, :, (g * share + j) * HEAD : (g * share + j + 1) * HEAD] = result[j]
-
-
-def finish(live, low, other, up, base, query, cached, cols):
+    fresh = []
+    for tile in range(2 * kv_heads):
+        up = up_ref[tile * each]
+        for k in range(1, each):
+            up = jnp.where(lane // cols == k, up_ref[tile * each + k], up)
+        low = keys_low if tile % 2 == 0 else values_low
+        delta = jnp.dot(low, up, preferred_element_type=jnp.float32)
+        at = slice(tile * HEAD, (tile + 1) * HEAD)
+        value = (live * (base_ref[:, at] + ADAPTER_SCALE * delta)).astype(jnp.bfloat16)
+        new_ref[:, :, at] = value.reshape(steps, rows, HEAD)
+        fresh.append(value)
+    todo = [(g, s) for g in range(kv_heads) for s in range(steps)]
+    found = []
+    for g, s in todo:
+        queries = jnp.concatenate(
+            [query_ref[s, :, (g * share + j) * HEAD : (g * share + j + 1) * HEAD] for j in range(share)], axis=0
+        )
+        scores = dot_t(queries, fresh[2 * g]).reshape(share, rows, total) + bias[s]
+        found.append((scores, jnp.max(scores, axis=-1, keepdims=True)))
+    for (g, s), (scores, most) in zip(todo, found):
+        cached_max = max_ref[g, s]
+        highest = jnp.maximum(cached_max, most)
+        weights = jnp.exp2((scores - highest[:, :, :total]) * EXP_SCALE)
+        keep = jnp.exp2((cached_max - highest) * EXP_SCALE)
+        values = jnp.concatenate([fresh[2 * g + 1], ones], axis=1)
+        mixed = jnp.dot(
+            weights.reshape(-1, total).astype(jnp.bfloat16), values, preferred_element_type=jnp.float32
+        ).reshape(share, rows, 2 * HEAD)
+        top = mix_ref[g, s] * keep + mixed[..., :HEAD]
+        bottom = sum_ref[g, s] * keep + mixed[..., HEAD:]
+        result = (top / bottom * live_row[None]).astype(jnp.bfloat16)
+        for j in range(share):
+            attn_ref[s, :, (g * share + j) * HEAD : (g * share + j + 1) * HEAD] = result[j]
+
+
+def finish(live, sent, came, up, base, query, cached, groups, size, cols):
     steps, rows, _ = query.shape
     return pl.pallas_call(
-        functools.partial(final_kernel, cols),
+        functools.partial(final_kernel, groups, size, cols),
         out_shape=[
             jax.ShapeDtypeStruct((steps, rows, base.shape[1]), jnp.bfloat16),
             jax.ShapeDtypeStruct(query.shape, jnp.bfloat16),
         ],
         in_specs=[VMEM] * 9,
         out_specs=[VMEM] * 2,
+        scratch_shapes=[pltpu.VMEM(up.shape, up.dtype)],
         compiler_params=pltpu.CompilerParams(vmem_limit_bytes=8 << 20),
         name="finish",
-    )(live, low, other, up, base, query, *cached)
+    )(live, sent, came, up, base, query, *cached)
 
 
 def local(
@@ -335,13 +345,17 @@
     rows = hidden.shape[1]
     size = BLK // rows
     groups = serve // size
+    both = ("serve", "tensor")
+
+    def crossing(d):
+        return [(i * 2 + t, (i ^ d) * 2 + 1 - t) for i in range(serve) for t in range(2)]
+
     live, bias, *packed = pack(
         block_adapter, block_fill, cache_len, down_store, up_store, query, kv_cache, groups, size
     )
     if groups == 2:
         other, own = packed
-        swap = [(i, (i + size) % serve) for i in range(serve)]
-        arrived = jnp.stack([own, lax.ppermute(other, "serve", swap)])
+        arrived = jnp.stack([own, lax.ppermute(other, both, crossing(size))])
     else:
         same = [[g * size + j for g in range(groups)] for j in range(size)]
         arrived = lax.all_to_all(packed[0], "serve", 0, 0, axis_index_groups=same, tiled=True)
@@ -349,12 +363,12 @@
     arrived, cached, hidden = lax.optimization_barrier((arrived, cached, hidden))
     parts = [arrived]
     for d in range(1, size):
-        parts.append(lax.ppermute(arrived, "serve", [(i, i ^ d) for i in range(serve)]))
+        parts.append(lax.ppermute(arrived, both, crossing(d)))
     base = base_projection(hidden, kv_weight)
     parts, base = lax.optimization_barrier((parts, base))
-    low, up = shrink(live, hidden, parts, groups, size)
-    other_low = lax.ppermute(low, "tensor", [(0, 1), (1, 0)])
-    return tuple(finish(live, low, other_low, up, base, query, cached, up_store.shape[1]))
+    sent, up = shrink(hidden, parts, groups, size)
+    came = lax.ppermute(sent, "tensor", [(0, 1), (1, 0)])
+    return tuple(finish(live, sent, came, up, base, query, cached, groups, size, up_store.shape[1]))
 
 
 def solution(mesh):

time: 20.8 us -> 19.5 us (0.938)
  Pallas kernels: 9.79 us -> 8.16 us
  waiting for transfers between devices: 2.41 us -> 3.15 us
  starting transfers between devices: 7.73 us -> 7.26 us
    pallas_call x2, Pallas kernels: 4.42 us -> 2.76 us  [the longest x1 1.41 us: finish(): pl.pallas_call(functools.partial(final_kernel, groups, size, cols), out_s...]
    ppermute x5, waiting for transfers between devices: 2.41 us -> 3.15 us  [the longest x3 1.48 us: local(): parts.append(lax.ppermute(arrived, both, crossing(d)))]
    ppermute x5, starting transfers between devices: 7.73 us -> 7.26 us  [the longest x1 3.54 us: local(): arrived = jnp.stack([own, lax.ppermute(other, both, crossing(size))])]
  transfers between devices with their start and end apart: 5 -> 5, of which waited for: 3 -> 4; matrix products, arithmetic and copies ran while one was open for 0% -> 0% of each run, Pallas kernels for 25% -> 20%
where the time goes in v3:
time: 19.5 us; the launch traced here: 19.3 us
  Pallas kernels  8.16 us (42%)
  starting transfers between devices  7.26 us (37%)
  waiting for transfers between devices  3.15 us (16%)
  between operations  0.72 us (4%)
    ppermute x1, starting transfers between devices, local(): arrived = jnp.stack([own, lax.ppermute(other, both, crossing(size))])  3.54 us
    ppermute x3, starting transfers between devices, local(): parts.append(lax.ppermute(arrived, both, crossing(d)))  3.53 us
    pallas_call x1, Pallas kernels, base_projection(): pl.pallas_call(base_kernel, grid=(width // chunk,), out_shape=jax.ShapeDt...  2.6 us
    pallas_call x1, Pallas kernels, pack(): pl.pallas_call(functools.partial(pack_kernel, groups, size, kv_cache.shap...  2.4 us
    ppermute x3, waiting for transfers between devices, local(): parts.append(lax.ppermute(arrived, both, crossing(d)))  1.48 us
    pallas_call x1, Pallas kernels, finish(): pl.pallas_call(functools.partial(final_kernel, groups, size, cols), out_s...  1.41 us
    pallas_call x1, Pallas kernels, cache_attention(): pl.pallas_call(cache_kernel, out_shape=[shape] * 3, in_specs=[VMEM] * 3,...  1.35 us
    ppermute x1, waiting for transfers between devices, local(): came = lax.ppermute(sent, 'tensor', [(0, 1), (1, 0)])  1.17 us
  transfers between devices with their start and end apart: 5, of which 4 were waited for; matrix products, arithmetic and copies ran while one was open for 0% of the time, Pallas kernels for 20%

profile of v3, /device:TPU:0, one launch (start us, length us, event | category | flops | bytes accessed | tf_op | source)
XLA Modules:
  0.0 19.3 jit_solution(6817120623276899281)
XLA Ops:
  0.6 0.0 copy-start.1
  0.6 0.0 copy-start.2
  0.7 0.0 slice-start
  0.7 2.4 %pack.1 = (f32[64,128]{1,0:T(8,128)S(1)}, f32[32,512]{1,0:T(8,128)S(1)}, bf16[16,1152]{1,0:T(8,128)(2,1)S(1)}, bf16[16,1152]{1,0:T(8,128)(2,1)S(1)}) custom-call(s32[2]{0:T(128)} %ids_ref.1, s32[2]{0:T(128)} %fill_ref.1, s32[32]{0:T(128)} %len_ref.1, bf16[1,4096,1024]{2,1,0:T(8,128)(2,1)} %down_ref.1, bf16[1,64,4096]{2,1,0:T(8,128)(2,1)} %up_ref.1), custom_call_target="tpu_custom_call" | custom-call | tf_op jit(solution)/shard_map/pack/pallas_call | solution.py:97
  3.1 3.5 %collective-permute-start = (bf16[16,1152]{1,0:T(8,128)(2,1)S(1)}, bf16[16,1152]{1,0:T(8,128)(2,1)S(1)}, u32[]{:S(2)}, u32[]{:S(2)}) collective-permute-start(bf16[16,1152]{1,0:T(8,128)(2,1)S(1)} %get-tuple-element.23), channel_id=1, source_target_pairs={{0,9},{1,8},{2,11},{3,10},{4,13},{5,12},{6,15},{7,14},{8,1},{9,0},... | collective-permute-start | bytes 110600 | tf_op jit(solution)/shard_map/ppermute | solution.py:358
  6.6 0.0 copy-done.1
  6.6 0.0 copy-done.2
  6.6 0.0 slice-start.1
  6.6 1.4 %cached.1 = (f32[2,2,8,32,128]{4,3,2,1,0:T(8,128)S(1)}, f32[2,2,8,32,128]{4,3,2,1,0:T(8,128)S(1)}, f32[2,2,8,32,128]{4,3,2,1,0:T(8,128)S(1)}) custom-call(f32[32,512]{1,0:T(8,128)S(1)} %get-tuple-element.24.bias_ref, bf16[2,32,2048]{2,1,0:T(8,128)(2,1)S(1)} %copy-done.1, bf16[32,64,512]{2,1,0:T(8,128)(2,1)S(1)} %copy-done.2), custom_call_target="tpu_custom_call" | custom-call | flops 10737418240 | bytes 2097152 | tf_op jit(solution)/shard_map/cached/pallas_call | solution.py:199
  8.0 0.5 %collective-permute-done = bf16[16,1152]{1,0:T(8,128)(2,1)S(1)} collective-permute-done((bf16[16,1152]{1,0:T(8,128)(2,1)S(1)}, bf16[16,1152]{1,0:T(8,128)(2,1)S(1)}, u32[]{:S(2)}, u32[]{:S(2)}) %collective-permute-start) | collective-permute-done | bytes 36896 | tf_op jit(solution)/shard_map/ppermute | solution.py:358
  8.5 2.9 %collective-permute-start.3 = (bf16[2,16,1152]{2,1,0:T(8,128)(2,1)S(1)}, bf16[2,16,1152]{2,1,0:T(8,128)(2,1)S(1)}, u32[]{:S(2)}, u32[]{:S(2)}) collective-permute-start(bf16[2,16,1152]{2,1,0:T(8,128)(2,1)S(1)} %pad_maximum_fusion.rest_0_), channel_id=1, source_target_pairs={{0,7},{1,6},{2,5},{3,4},{4,3},{5,2},{6,1},{7,0},{8,15},{9,14},{10,... | collective-permute-start | bytes 221192 | tf_op jit(solution)/shard_map/ppermute | solution.py:366
  11.4 0.5 %collective-permute-start.2 = (bf16[2,16,1152]{2,1,0:T(8,128)(2,1)S(1)}, bf16[2,16,1152]{2,1,0:T(8,128)(2,1)S(1)}, u32[]{:S(2)}, u32[]{:S(2)}) collective-permute-start(bf16[2,16,1152]{2,1,0:T(8,128)(2,1)S(1)} %pad_maximum_fusion.rest_0_), channel_id=1, source_target_pairs={{0,5},{1,4},{2,7},{3,6},{4,1},{5,0},{6,3},{7,2},{8,13},{9,12},{10,... | collective-permute-start | bytes 221192 | tf_op jit(solution)/shard_map/ppermute | solution.py:366
  11.8 0.2 collective-permute-start.1
  12.0 0.0 slice-done
  12.0 0.0 slice-done.1
  12.0 0.0 copy-done
  12.0 2.6 %base.1.base_ref = f32[64,512]{1,0:T(8,128)S(1)} custom-call(bf16[2,32,8192]{2,1,0:T(8,128)(2,1)S(1)} %copy-done, bf16[8192,512]{1,0:T(8,128)(2,1)S(1)} %bitcast.3), custom_call_target="tpu_custom_call" | custom-call | flops 536870912 | bytes 9437184 | tf_op jit(solution)/shard_map/base/pallas_call | solution.py:135
  14.7 0.0 collective-permute-done.3.rest_3_
  14.7 1.2 %collective-permute-done.2.rest_2_ = bf16[2,16,1152]{2,1,0:T(8,128)(2,1)S(1)} collective-permute-done((bf16[2,16,1152]{2,1,0:T(8,128)(2,1)S(1)}, bf16[2,16,1152]{2,1,0:T(8,128)(2,1)S(1)}, u32[]{:S(2)}, u32[]{:S(2)}) %collective-permute-start.2) | collective-permute-done | bytes 73760 | tf_op jit(solution)/shard_map/ppermute | solution.py:366
  15.9 0.3 %collective-permute-done.1.rest_1_ = bf16[2,16,1152]{2,1,0:T(8,128)(2,1)S(1)} collective-permute-done((bf16[2,16,1152]{2,1,0:T(8,128)(2,1)S(1)}, bf16[2,16,1152]{2,1,0:T(8,128)(2,1)S(1)}, u32[]{:S(2)}, u32[]{:S(2)}) %collective-permute-start.1) | collective-permute-done | bytes 73760 | tf_op jit(solution)/shard_map/ppermute | solution.py:366
  16.1 0.4 %shrink.1 = (f32[192,128]{1,0:T(8,128)S(1)}, bf16[8,16,128]{2,1,0:T(8,128)(2,1)S(1)}) custom-call(bf16[2,32,8192]{2,1,0:T(8,128)(2,1)S(1)} %copy-done, bf16[2,16,1152]{2,1,0:T(8,128)(2,1)S(1)} %pad_maximum_fusion.rest_0_, bf16[2,16,1152]{2,1,0:T(8,128)(2,1)S(1)} %collective-permute-done.1.rest_1_, bf16[2,16,1152]{2,1,0:T(8,128)(2,1)S(1)} %collective-permute-done.2.rest_2_, ...), custom_call_target="tpu_custom_call" | custom-call | tf_op jit(solution)/shard_map/shrink/pallas_call | solution.py:248
  16.5 0.2 %collective-permute-start.4 = (f32[192,128]{1,0:T(8,128)S(1)}, f32[192,128]{1,0:T(8,128)S(1)}, u32[]{:S(2)}, u32[]{:S(2)}) collective-permute-start(f32[192,128]{1,0:T(8,128)S(1)} %get-tuple-element.34.sent_ref), channel_id=1, source_target_pairs={{0,1},{1,0},{2,3},{3,2},{4,5},{5,4},{6,7},{7,6},{8,9},{9,8},{10,11... | collective-permute-start | bytes 294920 | tf_op jit(solution)/shard_map/ppermute | solution.py:370
  16.7 1.2 %collective-permute-done.4.came_ref = f32[192,128]{1,0:T(8,128)S(1)} collective-permute-done((f32[192,128]{1,0:T(8,128)S(1)}, f32[192,128]{1,0:T(8,128)S(1)}, u32[]{:S(2)}, u32[]{:S(2)}) %collective-permute-start.4) | collective-permute-done | bytes 98336 | tf_op jit(solution)/shard_map/ppermute | solution.py:370
  17.9 1.4 %finish.1 = (bf16[2,32,512]{2,1,0:T(8,128)(2,1)}, bf16[2,32,2048]{2,1,0:T(8,128)(2,1)}) custom-call(f32[64,128]{1,0:T(8,128)S(1)} %get-tuple-element.21.live_ref, f32[192,128]{1,0:T(8,128)S(1)} %get-tuple-element.34.sent_ref, f32[192,128]{1,0:T(8,128)S(1)} %collective-permute-done.4.came_ref, bf16[8,16,128]{2,1,0:T(8,128)(2,1)S(1)} %get-tuple-element.35.straight_ref, ...), custom_call_target="tpu_custom_call" | custom-call | tf_op jit(solution)/shard_map/finish/pallas_call | solution.py:327
  (3 shorter events, 0.0 us)
Async XLA Ops:
  0.6 6.0 %copy-start.1 = (bf16[2,32,2048]{2,1,0:T(8,128)(2,1)S(1)}, bf16[2,32,2048]{2,1,0:T(8,128)(2,1)}, u32[]{:S(2)}) copy-start(bf16[2,32,2048]{2,1,0:T(8,128)(2,1)} %query_ref.3) | copy-start | bytes 786436
  0.6 6.0 %copy-start.2 = (bf16[32,64,512]{2,1,0:T(8,128)(2,1)S(1)}, bf16[32,64,512]{2,1,0:T(8,128)(2,1)}, u32[]{:S(2)}) copy-start(bf16[32,64,512]{2,1,0:T(8,128)(2,1)} %cache_ref.1) | copy-start | bytes 6291460
  0.7 11.4 %slice-start = ((s8[8388608]{0:T(1024)(128)(4,1)}), s8[4194304]{0:T(1024)(128)(4,1)S(1)}, s32[]{:S(2)}) async-start(s8[8388608]{0:T(1024)(128)(4,1)} %bitcast.2), calls=%async_computation | async-start | bytes 8388608
  3.1 5.4 %collective-permute-start = (bf16[16,1152]{1,0:T(8,128)(2,1)S(1)}, bf16[16,1152]{1,0:T(8,128)(2,1)S(1)}, u32[]{:S(2)}, u32[]{:S(2)}) collective-permute-start(bf16[16,1152]{1,0:T(8,128)(2,1)S(1)} %get-tuple-element.23), channel_id=1, source_target_pairs={{0,9},{1,8},{2,11},{3,10},{4,13},{5,12},{6,15},{7,14},{8,1},{9,0},... | collective-permute-start | bytes 110600 | tf_op jit(solution)/shard_map/ppermute | solution.py:358
  6.6 5.4 %slice-start.1 = ((s8[8388608]{0:T(1024)(128)(4,1)}), s8[4194304]{0:T(1024)(128)(4,1)S(1)}, s32[]{:S(2)}) async-start(s8[8388608]{0:T(1024)(128)(4,1)} %bitcast.2), calls=%async_computation.1 | async-start | bytes 8388608
  6.6 5.4 %copy-start = (bf16[2,32,8192]{2,1,0:T(8,128)(2,1)S(1)}, bf16[2,32,8192]{2,1,0:T(8,128)(2,1)}, u32[]{:S(2)}) copy-start(bf16[2,32,8192]{2,1,0:T(8,128)(2,1)} %hidden_ref.1) | copy-start | bytes 3145732
  8.5 6.2 %collective-permute-start.3 = (bf16[2,16,1152]{2,1,0:T(8,128)(2,1)S(1)}, bf16[2,16,1152]{2,1,0:T(8,128)(2,1)S(1)}, u32[]{:S(2)}, u32[]{:S(2)}) collective-permute-start(bf16[2,16,1152]{2,1,0:T(8,128)(2,1)S(1)} %pad_maximum_fusion.rest_0_), channel_id=1, source_target_pairs={{0,7},{1,6},{2,5},{3,4},{4,3},{5,2},{6,1},{7,0},{8,15},{9,14},{10,... | collective-permute-start | bytes 221192 | tf_op jit(solution)/shard_map/ppermute | solution.py:366
  11.4 4.5 %collective-permute-start.2 = (bf16[2,16,1152]{2,1,0:T(8,128)(2,1)S(1)}, bf16[2,16,1152]{2,1,0:T(8,128)(2,1)S(1)}, u32[]{:S(2)}, u32[]{:S(2)}) collective-permute-start(bf16[2,16,1152]{2,1,0:T(8,128)(2,1)S(1)} %pad_maximum_fusion.rest_0_), channel_id=1, source_target_pairs={{0,5},{1,4},{2,7},{3,6},{4,1},{5,0},{6,3},{7,2},{8,13},{9,12},{10,... | collective-permute-start | bytes 221192 | tf_op jit(solution)/shard_map/ppermute | solution.py:366
  11.8 4.3 %collective-permute-start.1 = (bf16[2,16,1152]{2,1,0:T(8,128)(2,1)S(1)}, bf16[2,16,1152]{2,1,0:T(8,128)(2,1)S(1)}, u32[]{:S(2)}, u32[]{:S(2)}) collective-permute-start(bf16[2,16,1152]{2,1,0:T(8,128)(2,1)S(1)} %pad_maximum_fusion.rest_0_), channel_id=1, source_target_pairs={{0,3},{1,2},{2,1},{3,0},{4,7},{5,6},{6,5},{7,4},{8,11},{9,10},{10,... | collective-permute-start | bytes 221192 | tf_op jit(solution)/shard_map/ppermute | solution.py:366
  16.5 1.4 %collective-permute-start.4 = (f32[192,128]{1,0:T(8,128)S(1)}, f32[192,128]{1,0:T(8,128)S(1)}, u32[]{:S(2)}, u32[]{:S(2)}) collective-permute-start(f32[192,128]{1,0:T(8,128)S(1)} %get-tuple-element.34.sent_ref), channel_id=1, source_target_pairs={{0,1},{1,0},{2,3},{3,2},{4,5},{5,4},{6,7},{7,6},{8,9},{9,8},{10,11... | collective-permute-start | bytes 294920 | tf_op jit(solution)/shard_map/ppermute | solution.py:370

commit v4 on v3

--- a/solution.py
+++ b/solution.py
@@ -14,6 +14,8 @@
 LANES = 128
 ADAPTER_SCALE = 2.0
 ROW_GROUP = 8
+CHUNK = 1024
+HEAD_CHUNKS = 3
 EXP_SCALE = HEAD ** (-0.5) * math.log2(math.e)
 
 HBM = pl.BlockSpec(memory_space=pl.ANY)
@@ -75,12 +77,12 @@
         bias_out[at : at + ROW_GROUP, :] = jnp.where((lanes >= start) & (lanes < start + used), 0.0, -jnp.inf)
     ranks = lax.broadcasted_iota(jnp.int32, (RANK, LANES), 0)
     lanes = lax.broadcasted_iota(jnp.int32, (RANK, LANES), 1)
+    chosen = [(lanes == ranks + start).astype(jnp.bfloat16) for start in starts]
+    for _, up, _ in copies:
+        up.wait()
+    picked = [dot_t(chosen[k], jnp.concatenate([window[k]] * (LANES // cols), axis=0)) for k in range(groups)]
     for k in range(groups):
-        down, up, out = copies[k]
-        up.wait()
-        chosen = (lanes == ranks + starts[k]).astype(jnp.bfloat16)
-        picked = dot_t(chosen, window[k])
-        out[:, width : width + LANES] = jnp.concatenate([picked] * (LANES // cols), axis=1).astype(jnp.bfloat16)
+        copies[k][2][:, width : width + LANES] = picked[k].astype(jnp.bfloat16)
     for down, _, _ in copies:
         down.wait()
 
@@ -117,41 +119,57 @@
     )(*(pltpu.with_memory_space_constraint(x, pltpu.HBM) for x in operands))
 
 
-def base_kernel(hidden_ref, weight_ref, base_ref):
-    steps, rows, width = hidden_ref.shape
-
-    @pl.when(pl.program_id(0) == 0)
-    def _():
-        base_ref[...] = jnp.zeros_like(base_ref)
-
-    states = hidden_ref[...].reshape(steps * rows, width)
-    base_ref[...] += jnp.dot(states, weight_ref[...], preferred_element_type=jnp.float32)
-
-
-def base_projection(hidden, kv_weight):
+def base_kernel(hidden_ref, head_ref, weight_hbm, base_ref, tail_ref, tail_sem):
+    steps, rows, _ = hidden_ref.shape
+    head = head_ref.shape[0]
+    chunks = tail_sem.shape[0]
+
+    def tail(i):
+        at = pl.multiple_of(i * CHUNK, CHUNK)
+        source = weight_hbm.at[pl.ds(pl.multiple_of(head + i * CHUNK, CHUNK), CHUNK)]
+        return pltpu.make_async_copy(source, tail_ref.at[pl.ds(at, CHUNK)], tail_sem.at[i])
+
+    for i in range(chunks):
+        tail(i).start()
+    states = hidden_ref[:, :, :head].reshape(steps * rows, head)
+    base_ref[...] = jnp.dot(states, head_ref[...], preferred_element_type=jnp.float32)
+
+    def step(i, carry):
+        tail(i).wait()
+        states = hidden_ref[:, :, pl.ds(pl.multiple_of(head + i * CHUNK, CHUNK), CHUNK)]
+        part = tail_ref[pl.ds(pl.multiple_of(i * CHUNK, CHUNK), CHUNK), :]
+        base_ref[...] += jnp.dot(states.reshape(steps * rows, CHUNK), part, preferred_element_type=jnp.float32)
+        return carry
+
+    lax.fori_loop(0, chunks, step, 0)
+
+
+def base_projection(hidden, head, kv_weight):
     steps, rows, width = hidden.shape
     cols = kv_weight.shape[1]
-    chunk = 1024
+    chunks = (width - head.shape[0]) // CHUNK
     return pl.pallas_call(
         base_kernel,
-        grid=(width // chunk,),
         out_shape=jax.ShapeDtypeStruct((steps * rows, cols), jnp.float32),
-        in_specs=[
-            pl.BlockSpec((steps, rows, chunk), lambda i: (0, 0, i)),
-            pl.BlockSpec((chunk, cols), lambda i: (i, 0)),
+        in_specs=[VMEM, VMEM, HBM],
+        out_specs=VMEM,
+        scratch_shapes=[
+            pltpu.VMEM((chunks * CHUNK, cols), kv_weight.dtype),
+            pltpu.SemaphoreType.DMA((chunks,)),
         ],
-        out_specs=pl.BlockSpec((steps * rows, cols), lambda i: (0, 0)),
         cost_estimate=pl.CostEstimate(
             flops=2 * steps * rows * width * cols,
             bytes_accessed=2 * width * cols + 2 * steps * rows * width,
             transcendentals=0,
         ),
-        compiler_params=pltpu.CompilerParams(vmem_limit_bytes=12 << 20),
+        compiler_params=pltpu.CompilerParams(vmem_limit_bytes=14 << 20),
         name="base",
-    )(hidden, kv_weight)
-
-
-def cache_kernel(bias_ref, query_ref, cache_ref, mix_ref, sum_ref, max_ref):
+    )(hidden, head, pltpu.with_memory_space_constraint(kv_weight, pltpu.HBM))
+
+
+def cache_kernel(bias_ref, query_ref, cache_ref, weight_hbm, mix_ref, sum_ref, max_ref, head_ref, head_sem):
+    head_copy = pltpu.make_async_copy(weight_hbm.at[pl.ds(0, head_ref.shape[0])], head_ref, head_sem)
+    head_copy.start()
     steps, rows, _ = query_ref.shape
     positions = cache_ref.shape[1]
     kv_heads = cache_ref.shape[2] // (2 * HEAD)
@@ -189,18 +207,21 @@
         return carry
 
     lax.fori_loop(0, rows // (2 * ROW_GROUP), pair, 0)
-
-
-def cache_attention(bias, query, kv_cache):
+    head_copy.wait()
+
+
+def cache_attention(bias, query, kv_cache, kv_weight):
     steps, rows, heads_width = query.shape
     kv_heads = kv_cache.shape[2] // (2 * HEAD)
     share = heads_width // (kv_heads * HEAD)
+    head = jax.ShapeDtypeStruct((HEAD_CHUNKS * CHUNK, kv_weight.shape[1]), kv_weight.dtype)
     shape = jax.ShapeDtypeStruct((kv_heads, steps, share, rows, HEAD), jnp.float32)
     return pl.pallas_call(
         cache_kernel,
-        out_shape=[shape] * 3,
-        in_specs=[VMEM] * 3,
-        out_specs=[VMEM] * 3,
+        out_shape=[shape] * 3 + [head],
+        in_specs=[VMEM] * 3 + [HBM],
+        out_specs=[VMEM] * 4,
+        scratch_shapes=[pltpu.SemaphoreType.DMA],
         cost_estimate=pl.CostEstimate(
             flops=40 * 2 * 2 * steps * heads_width * rows * ROW_GROUP * kv_cache.shape[1],
             bytes_accessed=2 * kv_cache.size,
@@ -208,7 +229,7 @@
         ),
         compiler_params=pltpu.CompilerParams(vmem_limit_bytes=12 << 20),
         name="cached",
-    )(bias, query, kv_cache)
+    )(bias, query, kv_cache, pltpu.with_memory_space_constraint(kv_weight, pltpu.HBM))
 
 
 def pieces(groups, size):
@@ -359,12 +380,12 @@
     else:
         same = [[g * size + j for g in range(groups)] for j in range(size)]
         arrived = lax.all_to_all(packed[0], "serve", 0, 0, axis_index_groups=same, tiled=True)
-    cached = cache_attention(bias, query, kv_cache)
-    arrived, cached, hidden = lax.optimization_barrier((arrived, cached, hidden))
+    *cached, head = cache_attention(bias, query, kv_cache, kv_weight)
+    arrived, cached, head, hidden = lax.optimization_barrier((arrived, cached, head, hidden))
     parts = [arrived]
     for d in range(1, size):
         parts.append(lax.ppermute(arrived, both, crossing(d)))
-    base = base_projection(hidden, kv_weight)
+    base = base_projection(hidden, head, kv_weight)
     parts, base = lax.optimization_barrier((parts, base))
     sent, up = shrink(hidden, parts, groups, size)
     came = lax.ppermute(sent, "tensor", [(0, 1), (1, 0)])

time: 19.5 us -> 18.7 us (0.959)
  waiting for transfers between devices: 3.15 us -> 1.98 us
  Pallas kernels: 8.16 us -> 8.42 us
    pallas_call x2, Pallas kernels: 3.95 us -> 4.83 us  [the longest x1 2.84 us: base_projection(): pl.pallas_call(base_kernel, out_shape=jax.ShapeDtypeStruct((steps * rows,...]
    pallas_call x1, Pallas kernels: 2.4 us -> 1.79 us  [pack(): pl.pallas_call(functools.partial(pack_kernel, groups, size, kv_cache.shap...]
    ppermute x3, waiting for transfers between devices: 1.48 us -> 0.89 us  [local(): parts.append(lax.ppermute(arrived, both, crossing(d)))]
    ppermute x1, waiting for transfers between devices: 0.49 us -> 0.01 us  [local(): arrived = jnp.stack([own, lax.ppermute(other, both, crossing(size))])]
  transfers between devices with their start and end apart: 5 -> 5, of which waited for: 4 -> 3; matrix products, arithmetic and copies ran while one was open for 0% -> 0% of each run, Pallas kernels for 20% -> 26%
where the time goes in v4:
time: 18.7 us; the launch traced here: 18.5 us
  Pallas kernels  8.42 us (45%)
  starting transfers between devices  7.39 us (40%)
  waiting for transfers between devices  1.98 us (11%)
  between operations  0.71 us (4%)
    ppermute x3, starting transfers between devices, local(): parts.append(lax.ppermute(arrived, both, crossing(d)))  3.57 us
    ppermute x1, starting transfers between devices, local(): arrived = jnp.stack([own, lax.ppermute(other, both, crossing(size))])  3.54 us
    pallas_call x1, Pallas kernels, base_projection(): pl.pallas_call(base_kernel, out_shape=jax.ShapeDtypeStruct((steps * rows,...  2.84 us
    pallas_call x1, Pallas kernels, cache_attention(): pl.pallas_call(cache_kernel, out_shape=[shape] * 3 + [head], in_specs=[VM...  1.99 us
    pallas_call x1, Pallas kernels, pack(): pl.pallas_call(functools.partial(pack_kernel, groups, size, kv_cache.shap...  1.79 us
    pallas_call x1, Pallas kernels, finish(): pl.pallas_call(functools.partial(final_kernel, groups, size, cols), out_s...  1.4 us
    ppermute x1, waiting for transfers between devices, local(): came = lax.ppermute(sent, 'tensor', [(0, 1), (1, 0)])  1.09 us
    ppermute x3, waiting for transfers between devices, local(): parts.append(lax.ppermute(arrived, both, crossing(d)))  0.89 us
  transfers between devices with their start and end apart: 5, of which 3 were waited for; matrix products, arithmetic and copies ran while one was open for 0% of the time, Pallas kernels for 26%

profile of v4, /device:TPU:0, one launch (start us, length us, event | category | flops | bytes accessed | tf_op | source)
XLA Modules:
  0.0 18.5 jit_solution(14425889438780206907)
XLA Ops:
  0.6 0.0 copy-start.1
  0.6 0.0 copy-start.2
  0.7 1.8 %pack.1 = (f32[64,128]{1,0:T(8,128)S(1)}, f32[32,512]{1,0:T(8,128)S(1)}, bf16[16,1152]{1,0:T(8,128)(2,1)S(1)}, bf16[16,1152]{1,0:T(8,128)(2,1)S(1)}) custom-call(s32[2]{0:T(128)} %ids_ref.1, s32[2]{0:T(128)} %fill_ref.1, s32[32]{0:T(128)} %len_ref.1, bf16[1,4096,1024]{2,1,0:T(8,128)(2,1)} %down_ref.1, bf16[1,64,4096]{2,1,0:T(8,128)(2,1)} %up_ref.1), custom_call_target="tpu_custom_call" | custom-call | tf_op jit(solution)/shard_map/pack/pallas_call | solution.py:99
  2.5 3.5 %collective-permute-start = (bf16[16,1152]{1,0:T(8,128)(2,1)S(1)}, bf16[16,1152]{1,0:T(8,128)(2,1)S(1)}, u32[]{:S(2)}, u32[]{:S(2)}) collective-permute-start(bf16[16,1152]{1,0:T(8,128)(2,1)S(1)} %get-tuple-element.25), channel_id=1, source_target_pairs={{0,9},{1,8},{2,11},{3,10},{4,13},{5,12},{6,15},{7,14},{8,1},{9,0},... | collective-permute-start | bytes 110600 | tf_op jit(solution)/shard_map/ppermute | solution.py:379
  6.0 0.0 copy-done.1
  6.0 0.0 copy-done.2
  6.0 0.0 copy-start
  6.0 2.0 %cached.1 = (f32[2,2,8,32,128]{4,3,2,1,0:T(8,128)S(1)}, f32[2,2,8,32,128]{4,3,2,1,0:T(8,128)S(1)}, f32[2,2,8,32,128]{4,3,2,1,0:T(8,128)S(1)}, bf16[3072,512]{1,0:T(8,128)(2,1)S(1)}) custom-call(f32[32,512]{1,0:T(8,128)S(1)} %get-tuple-element.26.bias_ref, bf16[2,32,2048]{2,1,0:T(8,128)(2,1)S(1)} %copy-done.1, bf16[32,64,512]{2,1,0:T(8,128)(2,1)S(1)} %copy-done.2, ...), custom_call_target="tpu_custom_call" | custom-call | flops 10737418240 | bytes 2097152 | tf_op jit(solution)/shard_map/cached/pallas_call | solution.py:219
  8.0 0.0 collective-permute-done
  8.0 2.9 %collective-permute-start.3 = (bf16[2,16,1152]{2,1,0:T(8,128)(2,1)S(1)}, bf16[2,16,1152]{2,1,0:T(8,128)(2,1)S(1)}, u32[]{:S(2)}, u32[]{:S(2)}) collective-permute-start(bf16[2,16,1152]{2,1,0:T(8,128)(2,1)S(1)} %pad_maximum_fusion.rest_0_), channel_id=1, source_target_pairs={{0,7},{1,6},{2,5},{3,4},{4,3},{5,2},{6,1},{7,0},{8,15},{9,14},{10,... | collective-permute-start | bytes 221192 | tf_op jit(solution)/shard_map/ppermute | solution.py:387
  10.9 0.3 %collective-permute-start.2 = (bf16[2,16,1152]{2,1,0:T(8,128)(2,1)S(1)}, bf16[2,16,1152]{2,1,0:T(8,128)(2,1)S(1)}, u32[]{:S(2)}, u32[]{:S(2)}) collective-permute-start(bf16[2,16,1152]{2,1,0:T(8,128)(2,1)S(1)} %pad_maximum_fusion.rest_0_), channel_id=1, source_target_pairs={{0,5},{1,4},{2,7},{3,6},{4,1},{5,0},{6,3},{7,2},{8,13},{9,12},{10,... | collective-permute-start | bytes 221192 | tf_op jit(solution)/shard_map/ppermute | solution.py:387
  11.2 0.4 %collective-permute-start.1 = (bf16[2,16,1152]{2,1,0:T(8,128)(2,1)S(1)}, bf16[2,16,1152]{2,1,0:T(8,128)(2,1)S(1)}, u32[]{:S(2)}, u32[]{:S(2)}) collective-permute-start(bf16[2,16,1152]{2,1,0:T(8,128)(2,1)S(1)} %pad_maximum_fusion.rest_0_), channel_id=1, source_target_pairs={{0,3},{1,2},{2,1},{3,0},{4,7},{5,6},{6,5},{7,4},{8,11},{9,10},{10,... | collective-permute-start | bytes 221192 | tf_op jit(solution)/shard_map/ppermute | solution.py:387
  11.6 0.0 copy-done
  11.6 2.8 %base.1.base_ref = f32[64,512]{1,0:T(8,128)S(1)} custom-call(bf16[2,32,8192]{2,1,0:T(8,128)(2,1)S(1)} %copy-done, bf16[3072,512]{1,0:T(8,128)(2,1)S(1)} %get-tuple-element.33.head_ref, bf16[8192,512]{1,0:T(8,128)(2,1)} %weight_hbm.3), custom_call_target="tpu_custom_call" | custom-call | flops 536870912 | bytes 9437184 | tf_op jit(solution)/shard_map/base/pallas_call | solution.py:151
  14.5 0.0 collective-permute-done.3.rest_3_
  14.5 0.8 %collective-permute-done.2.rest_2_ = bf16[2,16,1152]{2,1,0:T(8,128)(2,1)S(1)} collective-permute-done((bf16[2,16,1152]{2,1,0:T(8,128)(2,1)S(1)}, bf16[2,16,1152]{2,1,0:T(8,128)(2,1)S(1)}, u32[]{:S(2)}, u32[]{:S(2)}) %collective-permute-start.2) | collective-permute-done | bytes 73760 | tf_op jit(solution)/shard_map/ppermute | solution.py:387
  15.3 0.1 collective-permute-done.1.rest_1_
  15.4 0.4 %shrink.1 = (f32[192,128]{1,0:T(8,128)S(1)}, bf16[8,16,128]{2,1,0:T(8,128)(2,1)S(1)}) custom-call(bf16[2,32,8192]{2,1,0:T(8,128)(2,1)S(1)} %copy-done, bf16[2,16,1152]{2,1,0:T(8,128)(2,1)S(1)} %pad_maximum_fusion.rest_0_, bf16[2,16,1152]{2,1,0:T(8,128)(2,1)S(1)} %collective-permute-done.1.rest_1_, bf16[2,16,1152]{2,1,0:T(8,128)(2,1)S(1)} %collective-permute-done.2.rest_2_, ...), custom_call_target="tpu_custom_call" | custom-call | tf_op jit(solution)/shard_map/shrink/pallas_call | solution.py:269
  15.8 0.3 %collective-permute-start.4 = (f32[192,128]{1,0:T(8,128)S(1)}, f32[192,128]{1,0:T(8,128)S(1)}, u32[]{:S(2)}, u32[]{:S(2)}) collective-permute-start(f32[192,128]{1,0:T(8,128)S(1)} %get-tuple-element.38.sent_ref), channel_id=1, source_target_pairs={{0,1},{1,0},{2,3},{3,2},{4,5},{5,4},{6,7},{7,6},{8,9},{9,8},{10,11... | collective-permute-start | bytes 294920 | tf_op jit(solution)/shard_map/ppermute | solution.py:391
  16.0 1.1 %collective-permute-done.4.came_ref = f32[192,128]{1,0:T(8,128)S(1)} collective-permute-done((f32[192,128]{1,0:T(8,128)S(1)}, f32[192,128]{1,0:T(8,128)S(1)}, u32[]{:S(2)}, u32[]{:S(2)}) %collective-permute-start.4) | collective-permute-done | bytes 98336 | tf_op jit(solution)/shard_map/ppermute | solution.py:391
  17.1 1.4 %finish.1 = (bf16[2,32,512]{2,1,0:T(8,128)(2,1)}, bf16[2,32,2048]{2,1,0:T(8,128)(2,1)}) custom-call(f32[64,128]{1,0:T(8,128)S(1)} %get-tuple-element.23.live_ref, f32[192,128]{1,0:T(8,128)S(1)} %get-tuple-element.38.sent_ref, f32[192,128]{1,0:T(8,128)S(1)} %collective-permute-done.4.came_ref, bf16[8,16,128]{2,1,0:T(8,128)(2,1)S(1)} %get-tuple-element.39.straight_ref, ...), custom_call_target="tpu_custom_call" | custom-call | tf_op jit(solution)/shard_map/finish/pallas_call | solution.py:348
  (1 shorter events, 0.0 us)
Async XLA Ops:
  0.6 5.4 %copy-start.1 = (bf16[2,32,2048]{2,1,0:T(8,128)(2,1)S(1)}, bf16[2,32,2048]{2,1,0:T(8,128)(2,1)}, u32[]{:S(2)}) copy-start(bf16[2,32,2048]{2,1,0:T(8,128)(2,1)} %query_ref.3) | copy-start | bytes 786436
  0.6 5.4 %copy-start.2 = (bf16[32,64,512]{2,1,0:T(8,128)(2,1)S(1)}, bf16[32,64,512]{2,1,0:T(8,128)(2,1)}, u32[]{:S(2)}) copy-start(bf16[32,64,512]{2,1,0:T(8,128)(2,1)} %cache_ref.1) | copy-start | bytes 6291460
  2.5 5.5 %collective-permute-start = (bf16[16,1152]{1,0:T(8,128)(2,1)S(1)}, bf16[16,1152]{1,0:T(8,128)(2,1)S(1)}, u32[]{:S(2)}, u32[]{:S(2)}) collective-permute-start(bf16[16,1152]{1,0:T(8,128)(2,1)S(1)} %get-tuple-element.25), channel_id=1, source_target_pairs={{0,9},{1,8},{2,11},{3,10},{4,13},{5,12},{6,15},{7,14},{8,1},{9,0},... | collective-permute-start | bytes 110600 | tf_op jit(solution)/shard_map/ppermute | solution.py:379
  6.0 5.6 %copy-start = (bf16[2,32,8192]{2,1,0:T(8,128)(2,1)S(1)}, bf16[2,32,8192]{2,1,0:T(8,128)(2,1)}, u32[]{:S(2)}) copy-start(bf16[2,32,8192]{2,1,0:T(8,128)(2,1)} %hidden_ref.1) | copy-start | bytes 3145732
  8.0 6.4 %collective-permute-start.3 = (bf16[2,16,1152]{2,1,0:T(8,128)(2,1)S(1)}, bf16[2,16,1152]{2,1,0:T(8,128)(2,1)S(1)}, u32[]{:S(2)}, u32[]{:S(2)}) collective-permute-start(bf16[2,16,1152]{2,1,0:T(8,128)(2,1)S(1)} %pad_maximum_fusion.rest_0_), channel_id=1, source_target_pairs={{0,7},{1,6},{2,5},{3,4},{4,3},{5,2},{6,1},{7,0},{8,15},{9,14},{10,... | collective-permute-start | bytes 221192 | tf_op jit(solution)/shard_map/ppermute | solution.py:387
  10.9 4.4 %collective-permute-start.2 = (bf16[2,16,1152]{2,1,0:T(8,128)(2,1)S(1)}, bf16[2,16,1152]{2,1,0:T(8,128)(2,1)S(1)}, u32[]{:S(2)}, u32[]{:S(2)}) collective-permute-start(bf16[2,16,1152]{2,1,0:T(8,128)(2,1)S(1)} %pad_maximum_fusion.rest_0_), channel_id=1, source_target_pairs={{0,5},{1,4},{2,7},{3,6},{4,1},{5,0},{6,3},{7,2},{8,13},{9,12},{10,... | collective-permute-start | bytes 221192 | tf_op jit(solution)/shard_map/ppermute | solution.py:387
  11.2 4.2 %collective-permute-start.1 = (bf16[2,16,1152]{2,1,0:T(8,128)(2,1)S(1)}, bf16[2,16,1152]{2,1,0:T(8,128)(2,1)S(1)}, u32[]{:S(2)}, u32[]{:S(2)}) collective-permute-start(bf16[2,16,1152]{2,1,0:T(8,128)(2,1)S(1)} %pad_maximum_fusion.rest_0_), channel_id=1, source_target_pairs={{0,3},{1,2},{2,1},{3,0},{4,7},{5,6},{6,5},{7,4},{8,11},{9,10},{10,... | collective-permute-start | bytes 221192 | tf_op jit(solution)/shard_map/ppermute | solution.py:387
  15.8 1.4 %collective-permute-start.4 = (f32[192,128]{1,0:T(8,128)S(1)}, f32[192,128]{1,0:T(8,128)S(1)}, u32[]{:S(2)}, u32[]{:S(2)}) collective-permute-start(f32[192,128]{1,0:T(8,128)S(1)} %get-tuple-element.38.sent_ref), channel_id=1, source_target_pairs={{0,1},{1,0},{2,3},{3,2},{4,5},{5,4},{6,7},{7,6},{8,9},{9,8},{10,11... | collective-permute-start | bytes 294920 | tf_op jit(solution)/shard_map/ppermute | solution.py:391

commit v5 on v4

--- a/solution.py
+++ b/solution.py
@@ -242,32 +242,34 @@
     return lax.rem(first + e, groups) * size + (lax.rem(me, size) ^ d)
 
 
-def shrink_kernel(groups, size, hidden_ref, *rest):
+def shrink_kernel(groups, size, cols, hidden_ref, *rest):
     part_refs, (send_ref, up_ref) = rest[:-2], rest[-2:]
     steps, rows, _ = hidden_ref.shape
     total = steps * rows
-    width = part_refs[0].shape[2] - LANES
+    width = (part_refs[0].shape[1] - LANES) // groups
     sums = [jnp.zeros((total, RANK), jnp.float32)] * 2
     at = 2 * total
     for e, d, crossed in pieces(groups, size):
         source = piece_source(groups, size, e, d)
         states = hidden_ref[:, :, pl.ds(pl.multiple_of(source * width, LANES), width)]
-        factors = part_refs[d][e]
-        sums[crossed] = sums[crossed] + dot_t(states.reshape(total, width), factors[:, :width])
+        factors = part_refs[d][:, e * width : (e + 1) * width]
+        sums[crossed] = sums[crossed] + dot_t(states.reshape(total, width), factors)
+        shift = lax.rem((lax.rem(source, LANES // cols) - e) * cols + LANES, LANES)
+        up = pltpu.roll(part_refs[d][:, groups * width :].astype(jnp.float32), shift, 1)
         if crossed:
-            send_ref[at : at + RANK, :] = factors[:, width:].astype(jnp.float32)
+            send_ref[at : at + RANK, :] = up
             at += RANK
         else:
-            up_ref[source] = factors[:, width:]
+            up_ref[source] = up.astype(jnp.bfloat16)
     send_ref[:total, :RANK] = sums[0]
     send_ref[total : 2 * total, :RANK] = sums[1]
 
 
-def shrink(hidden, parts, groups, size):
+def shrink(hidden, parts, groups, size, cols):
     steps, rows, _ = hidden.shape
     crossed = sum(c for _, _, c in pieces(groups, size))
     return pl.pallas_call(
-        functools.partial(shrink_kernel, groups, size),
+        functools.partial(shrink_kernel, groups, size, cols),
         out_shape=[
             jax.ShapeDtypeStruct((2 * steps * rows + crossed * RANK, LANES), jnp.float32),
             jax.ShapeDtypeStruct((groups * size, RANK, LANES), jnp.bfloat16),
@@ -359,6 +361,14 @@
     )(live, sent, came, up, base, query, *cached)
 
 
+def join(slices, cols):
+    run = jnp.arange(LANES)[None, :] // cols
+    up = slices[0][:, -LANES:]
+    for e, part in enumerate(slices[1:], 1):
+        up = jnp.where(run == e, part[:, -LANES:], up)
+    return jnp.concatenate([part[:, :-LANES] for part in slices] + [up], axis=1)
+
+
 def local(
     hidden, query, kv_weight, down_store, up_store, kv_cache, cache_len, block_adapter, block_fill
 ):
@@ -376,10 +386,11 @@
     )
     if groups == 2:
         other, own = packed
-        arrived = jnp.stack([own, lax.ppermute(other, both, crossing(size))])
+        slices = [own, lax.ppermute(other, both, crossing(size))]
     else:
         same = [[g * size + j for g in range(groups)] for j in range(size)]
-        arrived = lax.all_to_all(packed[0], "serve", 0, 0, axis_index_groups=same, tiled=True)
+        slices = list(lax.all_to_all(packed[0], "serve", 0, 0, axis_index_groups=same, tiled=True))
+    arrived = join(slices, up_store.shape[1])
     *cached, head = cache_attention(bias, query, kv_cache, kv_weight)
     arrived, cached, head, hidden = lax.optimization_barrier((arrived, cached, head, hidden))
     parts = [arrived]
@@ -387,7 +398,7 @@
         parts.append(lax.ppermute(arrived, both, crossing(d)))
     base = base_projection(hidden, head, kv_weight)
     parts, base = lax.optimization_barrier((parts, base))
-    sent, up = shrink(hidden, parts, groups, size)
+    sent, up = shrink(hidden, parts, groups, size, up_store.shape[1])
     came = lax.ppermute(sent, "tensor", [(0, 1), (1, 0)])
     return tuple(finish(live, sent, came, up, base, query, cached, groups, size, up_store.shape[1]))
 

time: 18.7 us -> 18.6 us (level)
  waiting for transfers between devices: 1.98 us -> 1.77 us
where the time goes in v5:
time: 18.6 us; the launch traced here: 18.4 us
  Pallas kernels  8.44 us (45%)
  starting transfers between devices  7.43 us (40%)
  waiting for transfers between devices  1.77 us (10%)
  between operations  0.74 us (4%)
    ppermute x3, starting transfers between devices, local(): parts.append(lax.ppermute(arrived, both, crossing(d)))  3.57 us
    ppermute x1, starting transfers between devices, local(): slices = [own, lax.ppermute(other, both, crossing(size))]  3.54 us
    pallas_call x1, Pallas kernels, base_projection(): pl.pallas_call(base_kernel, out_shape=jax.ShapeDtypeStruct((steps * rows,...  2.84 us
    pallas_call x1, Pallas kernels, cache_attention(): pl.pallas_call(cache_kernel, out_shape=[shape] * 3 + [head], in_specs=[VM...  1.99 us
    pallas_call x1, Pallas kernels, pack(): pl.pallas_call(functools.partial(pack_kernel, groups, size, kv_cache.shap...  1.79 us
    pallas_call x1, Pallas kernels, finish(): pl.pallas_call(functools.partial(final_kernel, groups, size, cols), out_s...  1.41 us
    ppermute x1, waiting for transfers between devices, local(): came = lax.ppermute(sent, 'tensor', [(0, 1), (1, 0)])  1.04 us
    ppermute x3, waiting for transfers between devices, local(): parts.append(lax.ppermute(arrived, both, crossing(d)))  0.73 us
  transfers between devices with their start and end apart: 5, of which 3 were waited for; matrix products, arithmetic and copies ran while one was open for 0% of the time, Pallas kernels for 26%

profile of v5, /device:TPU:0, one launch (start us, length us, event | category | flops | bytes accessed | tf_op | source)
XLA Modules:
  0.0 18.4 jit_solution(864680539055211930)
XLA Ops:
  0.6 0.0 copy-start.1
  0.6 0.0 copy-start.2
  0.7 1.8 %pack.1 = (f32[64,128]{1,0:T(8,128)S(1)}, f32[32,512]{1,0:T(8,128)S(1)}, bf16[16,1152]{1,0:T(8,128)(2,1)S(1)}, bf16[16,1152]{1,0:T(8,128)(2,1)S(1)}) custom-call(s32[2]{0:T(128)} %ids_ref.1, s32[2]{0:T(128)} %fill_ref.1, s32[32]{0:T(128)} %len_ref.1, bf16[1,4096,1024]{2,1,0:T(8,128)(2,1)} %down_ref.1, bf16[1,64,4096]{2,1,0:T(8,128)(2,1)} %up_ref.1), custom_call_target="tpu_custom_call" | custom-call | tf_op jit(solution)/shard_map/pack/pallas_call | solution.py:99
  2.5 3.5 %collective-permute-start = (bf16[16,1152]{1,0:T(8,128)(2,1)S(1)}, bf16[16,1152]{1,0:T(8,128)(2,1)S(1)}, u32[]{:S(2)}, u32[]{:S(2)}) collective-permute-start(bf16[16,1152]{1,0:T(8,128)(2,1)S(1)} %get-tuple-element.25), channel_id=1, source_target_pairs={{0,9},{1,8},{2,11},{3,10},{4,13},{5,12},{6,15},{7,14},{8,1},{9,0},... | collective-permute-start | bytes 110600 | tf_op jit(solution)/shard_map/ppermute | solution.py:389
  6.0 0.0 copy-done.1
  6.0 0.0 copy-done.2
  6.0 0.0 copy-start
  6.0 2.0 %cached.1 = (f32[2,2,8,32,128]{4,3,2,1,0:T(8,128)S(1)}, f32[2,2,8,32,128]{4,3,2,1,0:T(8,128)S(1)}, f32[2,2,8,32,128]{4,3,2,1,0:T(8,128)S(1)}, bf16[3072,512]{1,0:T(8,128)(2,1)S(1)}) custom-call(f32[32,512]{1,0:T(8,128)S(1)} %get-tuple-element.26.bias_ref, bf16[2,32,2048]{2,1,0:T(8,128)(2,1)S(1)} %copy-done.1, bf16[32,64,512]{2,1,0:T(8,128)(2,1)S(1)} %copy-done.2, ...), custom_call_target="tpu_custom_call" | custom-call | flops 10737418240 | bytes 2097152 | tf_op jit(solution)/shard_map/cached/pallas_call | solution.py:219
  8.0 0.0 collective-permute-done
  8.1 2.9 %collective-permute-start.3 = (bf16[16,2176]{1,0:T(8,128)(2,1)S(1)}, bf16[16,2176]{1,0:T(8,128)(2,1)S(1)}, u32[]{:S(2)}, u32[]{:S(2)}) collective-permute-start(bf16[16,2176]{1,0:T(8,128)(2,1)S(1)} %pad_maximum_fusion.rest_0_), channel_id=1, source_target_pairs={{0,7},{1,6},{2,5},{3,4},{4,3},{5,2},{6,1},{7,0},{8,15},{9,14},{10,... | collective-permute-start | bytes 208904 | tf_op jit(solution)/shard_map/ppermute | solution.py:398
  11.0 0.2 %collective-permute-start.2 = (bf16[16,2176]{1,0:T(8,128)(2,1)S(1)}, bf16[16,2176]{1,0:T(8,128)(2,1)S(1)}, u32[]{:S(2)}, u32[]{:S(2)}) collective-permute-start(bf16[16,2176]{1,0:T(8,128)(2,1)S(1)} %pad_maximum_fusion.rest_0_), channel_id=1, source_target_pairs={{0,5},{1,4},{2,7},{3,6},{4,1},{5,0},{6,3},{7,2},{8,13},{9,12},{10,... | collective-permute-start | bytes 208904 | tf_op jit(solution)/shard_map/ppermute | solution.py:398
  11.2 0.5 %collective-permute-start.1 = (bf16[16,2176]{1,0:T(8,128)(2,1)S(1)}, bf16[16,2176]{1,0:T(8,128)(2,1)S(1)}, u32[]{:S(2)}, u32[]{:S(2)}) collective-permute-start(bf16[16,2176]{1,0:T(8,128)(2,1)S(1)} %pad_maximum_fusion.rest_0_), channel_id=1, source_target_pairs={{0,3},{1,2},{2,1},{3,0},{4,7},{5,6},{6,5},{7,4},{8,11},{9,10},{10,... | collective-permute-start | bytes 208904 | tf_op jit(solution)/shard_map/ppermute | solution.py:398
  11.6 0.0 copy-done
  11.6 2.8 %base.1.base_ref = f32[64,512]{1,0:T(8,128)S(1)} custom-call(bf16[2,32,8192]{2,1,0:T(8,128)(2,1)S(1)} %copy-done, bf16[3072,512]{1,0:T(8,128)(2,1)S(1)} %get-tuple-element.33.head_ref, bf16[8192,512]{1,0:T(8,128)(2,1)} %weight_hbm.3), custom_call_target="tpu_custom_call" | custom-call | flops 536870912 | bytes 9437184 | tf_op jit(solution)/shard_map/base/pallas_call | solution.py:151
  14.5 0.0 collective-permute-done.3.rest_3_
  14.5 0.6 %collective-permute-done.2.rest_2_ = bf16[16,2176]{1,0:T(8,128)(2,1)S(1)} collective-permute-done((bf16[16,2176]{1,0:T(8,128)(2,1)S(1)}, bf16[16,2176]{1,0:T(8,128)(2,1)S(1)}, u32[]{:S(2)}, u32[]{:S(2)}) %collective-permute-start.2) | collective-permute-done | bytes 69664 | tf_op jit(solution)/shard_map/ppermute | solution.py:398
  15.2 0.1 collective-permute-done.1.rest_1_
  15.2 0.4 %shrink.1 = (f32[192,128]{1,0:T(8,128)S(1)}, bf16[8,16,128]{2,1,0:T(8,128)(2,1)S(1)}) custom-call(bf16[2,32,8192]{2,1,0:T(8,128)(2,1)S(1)} %copy-done, bf16[16,2176]{1,0:T(8,128)(2,1)S(1)} %pad_maximum_fusion.rest_0_, bf16[16,2176]{1,0:T(8,128)(2,1)S(1)} %collective-permute-done.1.rest_1_, bf16[16,2176]{1,0:T(8,128)(2,1)S(1)} %collective-permute-done.2.rest_2_, ...), custom_call_target="tpu_custom_call" | custom-call | tf_op jit(solution)/shard_map/shrink/pallas_call | solution.py:271
  15.6 0.3 %collective-permute-start.4 = (f32[192,128]{1,0:T(8,128)S(1)}, f32[192,128]{1,0:T(8,128)S(1)}, u32[]{:S(2)}, u32[]{:S(2)}) collective-permute-start(f32[192,128]{1,0:T(8,128)S(1)} %get-tuple-element.38.sent_ref), channel_id=1, source_target_pairs={{0,1},{1,0},{2,3},{3,2},{4,5},{5,4},{6,7},{7,6},{8,9},{9,8},{10,11... | collective-permute-start | bytes 294920 | tf_op jit(solution)/shard_map/ppermute | solution.py:402
  16.0 1.0 %collective-permute-done.4.came_ref = f32[192,128]{1,0:T(8,128)S(1)} collective-permute-done((f32[192,128]{1,0:T(8,128)S(1)}, f32[192,128]{1,0:T(8,128)S(1)}, u32[]{:S(2)}, u32[]{:S(2)}) %collective-permute-start.4) | collective-permute-done | bytes 98336 | tf_op jit(solution)/shard_map/ppermute | solution.py:402
  17.0 1.4 %finish.1 = (bf16[2,32,512]{2,1,0:T(8,128)(2,1)}, bf16[2,32,2048]{2,1,0:T(8,128)(2,1)}) custom-call(f32[64,128]{1,0:T(8,128)S(1)} %get-tuple-element.23.live_ref, f32[192,128]{1,0:T(8,128)S(1)} %get-tuple-element.38.sent_ref, f32[192,128]{1,0:T(8,128)S(1)} %collective-permute-done.4.came_ref, bf16[8,16,128]{2,1,0:T(8,128)(2,1)S(1)} %get-tuple-element.39.straight_ref, ...), custom_call_target="tpu_custom_call" | custom-call | tf_op jit(solution)/shard_map/finish/pallas_call | solution.py:350
  (5 shorter events, 0.0 us)
Async XLA Ops:
  0.6 5.4 %copy-start.1 = (bf16[2,32,2048]{2,1,0:T(8,128)(2,1)S(1)}, bf16[2,32,2048]{2,1,0:T(8,128)(2,1)}, u32[]{:S(2)}) copy-start(bf16[2,32,2048]{2,1,0:T(8,128)(2,1)} %query_ref.3) | copy-start | bytes 786436
  0.6 5.4 %copy-start.2 = (bf16[32,64,512]{2,1,0:T(8,128)(2,1)S(1)}, bf16[32,64,512]{2,1,0:T(8,128)(2,1)}, u32[]{:S(2)}) copy-start(bf16[32,64,512]{2,1,0:T(8,128)(2,1)} %cache_ref.1) | copy-start | bytes 6291460
  2.5 5.6 %collective-permute-start = (bf16[16,1152]{1,0:T(8,128)(2,1)S(1)}, bf16[16,1152]{1,0:T(8,128)(2,1)S(1)}, u32[]{:S(2)}, u32[]{:S(2)}) collective-permute-start(bf16[16,1152]{1,0:T(8,128)(2,1)S(1)} %get-tuple-element.25), channel_id=1, source_target_pairs={{0,9},{1,8},{2,11},{3,10},{4,13},{5,12},{6,15},{7,14},{8,1},{9,0},... | collective-permute-start | bytes 110600 | tf_op jit(solution)/shard_map/ppermute | solution.py:389
  6.0 5.6 %copy-start = (bf16[2,32,8192]{2,1,0:T(8,128)(2,1)S(1)}, bf16[2,32,8192]{2,1,0:T(8,128)(2,1)}, u32[]{:S(2)}) copy-start(bf16[2,32,8192]{2,1,0:T(8,128)(2,1)} %hidden_ref.1) | copy-start | bytes 3145732
  8.1 6.4 %collective-permute-start.3 = (bf16[16,2176]{1,0:T(8,128)(2,1)S(1)}, bf16[16,2176]{1,0:T(8,128)(2,1)S(1)}, u32[]{:S(2)}, u32[]{:S(2)}) collective-permute-start(bf16[16,2176]{1,0:T(8,128)(2,1)S(1)} %pad_maximum_fusion.rest_0_), channel_id=1, source_target_pairs={{0,7},{1,6},{2,5},{3,4},{4,3},{5,2},{6,1},{7,0},{8,15},{9,14},{10,... | collective-permute-start | bytes 208904 | tf_op jit(solution)/shard_map/ppermute | solution.py:398
  11.0 4.2 %collective-permute-start.2 = (bf16[16,2176]{1,0:T(8,128)(2,1)S(1)}, bf16[16,2176]{1,0:T(8,128)(2,1)S(1)}, u32[]{:S(2)}, u32[]{:S(2)}) collective-permute-start(bf16[16,2176]{1,0:T(8,128)(2,1)S(1)} %pad_maximum_fusion.rest_0_), channel_id=1, source_target_pairs={{0,5},{1,4},{2,7},{3,6},{4,1},{5,0},{6,3},{7,2},{8,13},{9,12},{10,... | collective-permute-start | bytes 208904 | tf_op jit(solution)/shard_map/ppermute | solution.py:398
  11.2 4.0 %collective-permute-start.1 = (bf16[16,2176]{1,0:T(8,128)(2,1)S(1)}, bf16[16,2176]{1,0:T(8,128)(2,1)S(1)}, u32[]{:S(2)}, u32[]{:S(2)}) collective-permute-start(bf16[16,2176]{1,0:T(8,128)(2,1)S(1)} %pad_maximum_fusion.rest_0_), channel_id=1, source_target_pairs={{0,3},{1,2},{2,1},{3,0},{4,7},{5,6},{6,5},{7,4},{8,11},{9,10},{10,... | collective-permute-start | bytes 208904 | tf_op jit(solution)/shard_map/ppermute | solution.py:398
  15.6 1.4 %collective-permute-start.4 = (f32[192,128]{1,0:T(8,128)S(1)}, f32[192,128]{1,0:T(8,128)S(1)}, u32[]{:S(2)}, u32[]{:S(2)}) collective-permute-start(f32[192,128]{1,0:T(8,128)S(1)} %get-tuple-element.38.sent_ref), channel_id=1, source_target_pairs={{0,1},{1,0},{2,3},{3,2},{4,5},{5,4},{6,7},{7,6},{8,9},{9,8},{10,11... | collective-permute-start | bytes 294920 | tf_op jit(solution)/shard_map/ppermute | solution.py:402

commit v6 on v5

--- a/solution.py
+++ b/solution.py
@@ -223,7 +223,7 @@
         out_specs=[VMEM] * 4,
         scratch_shapes=[pltpu.SemaphoreType.DMA],
         cost_estimate=pl.CostEstimate(
-            flops=40 * 2 * 2 * steps * heads_width * rows * ROW_GROUP * kv_cache.shape[1],
+            flops=14 * 2 * 2 * steps * heads_width * rows * ROW_GROUP * kv_cache.shape[1],
             bytes_accessed=2 * kv_cache.size,
             transcendentals=0,
         ),

time: 18.6 us -> 18.7 us (level)
  waiting for transfers between devices: 1.77 us -> 2.12 us
    ppermute x3, waiting for transfers between devices: 0.73 us -> 0.95 us  [local(): parts.append(lax.ppermute(arrived, both, crossing(d)))]
  transfers between devices with their start and end apart: 5 -> 5, of which waited for: 3 -> 3; matrix products, arithmetic and copies ran while one was open for 0% -> 0% of each run, Pallas kernels for 26% -> 25%
where the time goes in v6:
time: 18.7 us; the launch traced here: 18.6 us
  Pallas kernels  8.34 us (45%)
  starting transfers between devices  7.31 us (39%)
  waiting for transfers between devices  2.12 us (11%)
  between operations  0.75 us (4%)
    ppermute x3, starting transfers between devices, local(): parts.append(lax.ppermute(arrived, both, crossing(d)))  3.57 us
    ppermute x1, starting transfers between devices, local(): slices = [own, lax.ppermute(other, both, crossing(size))]  3.53 us
    pallas_call x1, Pallas kernels, base_projection(): pl.pallas_call(base_kernel, out_shape=jax.ShapeDtypeStruct((steps * rows,...  2.84 us
    pallas_call x1, Pallas kernels, cache_attention(): pl.pallas_call(cache_kernel, out_shape=[shape] * 3 + [head], in_specs=[VM...  1.9 us
    pallas_call x1, Pallas kernels, pack(): pl.pallas_call(functools.partial(pack_kernel, groups, size, kv_cache.shap...  1.8 us
    pallas_call x1, Pallas kernels, finish(): pl.pallas_call(functools.partial(final_kernel, groups, size, cols), out_s...  1.4 us
    ppermute x1, waiting for transfers between devices, local(): came = lax.ppermute(sent, 'tensor', [(0, 1), (1, 0)])  1.16 us
    ppermute x3, waiting for transfers between devices, local(): parts.append(lax.ppermute(arrived, both, crossing(d)))  0.95 us
  transfers between devices with their start and end apart: 5, of which 3 were waited for; matrix products, arithmetic and copies ran while one was open for 0% of the time, Pallas kernels for 25%

profile of v6, /device:TPU:0, one launch (start us, length us, event | category | flops | bytes accessed | tf_op | source)
XLA Modules:
  0.0 18.6 jit_solution(14053169927789637264)
XLA Ops:
  0.6 0.0 copy-start.1
  0.6 0.0 copy-start.2
  0.7 1.8 %pack.1 = (f32[64,128]{1,0:T(8,128)S(1)}, f32[32,512]{1,0:T(8,128)S(1)}, bf16[16,1152]{1,0:T(8,128)(2,1)S(1)}, bf16[16,1152]{1,0:T(8,128)(2,1)S(1)}) custom-call(s32[2]{0:T(128)} %ids_ref.1, s32[2]{0:T(128)} %fill_ref.1, s32[32]{0:T(128)} %len_ref.1, bf16[1,4096,1024]{2,1,0:T(8,128)(2,1)} %down_ref.1, bf16[1,64,4096]{2,1,0:T(8,128)(2,1)} %up_ref.1), custom_call_target="tpu_custom_call" | custom-call | tf_op jit(solution)/shard_map/pack/pallas_call | solution.py:99
  2.5 0.0 copy-start
  2.5 3.5 %collective-permute-start = (bf16[16,1152]{1,0:T(8,128)(2,1)S(1)}, bf16[16,1152]{1,0:T(8,128)(2,1)S(1)}, u32[]{:S(2)}, u32[]{:S(2)}) collective-permute-start(bf16[16,1152]{1,0:T(8,128)(2,1)S(1)} %get-tuple-element.25), channel_id=1, source_target_pairs={{0,9},{1,8},{2,11},{3,10},{4,13},{5,12},{6,15},{7,14},{8,1},{9,0},... | collective-permute-start | bytes 110600 | tf_op jit(solution)/shard_map/ppermute | solution.py:389
  6.0 0.0 copy-done.1
  6.0 0.0 copy-done.2
  6.0 1.9 %cached.1 = (f32[2,2,8,32,128]{4,3,2,1,0:T(8,128)S(1)}, f32[2,2,8,32,128]{4,3,2,1,0:T(8,128)S(1)}, f32[2,2,8,32,128]{4,3,2,1,0:T(8,128)S(1)}, bf16[3072,512]{1,0:T(8,128)(2,1)S(1)}) custom-call(f32[32,512]{1,0:T(8,128)S(1)} %get-tuple-element.26.bias_ref, bf16[2,32,2048]{2,1,0:T(8,128)(2,1)S(1)} %copy-done.1, bf16[32,64,512]{2,1,0:T(8,128)(2,1)S(1)} %copy-done.2, ...), custom_call_target="tpu_custom_call" | custom-call | flops 3758096384 | bytes 2097152 | tf_op jit(solution)/shard_map/cached/pallas_call | solution.py:219
  7.9 0.0 collective-permute-done
  8.0 2.9 %collective-permute-start.3 = (bf16[16,2176]{1,0:T(8,128)(2,1)S(1)}, bf16[16,2176]{1,0:T(8,128)(2,1)S(1)}, u32[]{:S(2)}, u32[]{:S(2)}) collective-permute-start(bf16[16,2176]{1,0:T(8,128)(2,1)S(1)} %pad_maximum_fusion.rest_0_), channel_id=1, source_target_pairs={{0,7},{1,6},{2,5},{3,4},{4,3},{5,2},{6,1},{7,0},{8,15},{9,14},{10,... | collective-permute-start | bytes 208904 | tf_op jit(solution)/shard_map/ppermute | solution.py:398
  10.9 0.3 %collective-permute-start.2 = (bf16[16,2176]{1,0:T(8,128)(2,1)S(1)}, bf16[16,2176]{1,0:T(8,128)(2,1)S(1)}, u32[]{:S(2)}, u32[]{:S(2)}) collective-permute-start(bf16[16,2176]{1,0:T(8,128)(2,1)S(1)} %pad_maximum_fusion.rest_0_), channel_id=1, source_target_pairs={{0,5},{1,4},{2,7},{3,6},{4,1},{5,0},{6,3},{7,2},{8,13},{9,12},{10,... | collective-permute-start | bytes 208904 | tf_op jit(solution)/shard_map/ppermute | solution.py:398
  11.2 0.3 %collective-permute-start.1 = (bf16[16,2176]{1,0:T(8,128)(2,1)S(1)}, bf16[16,2176]{1,0:T(8,128)(2,1)S(1)}, u32[]{:S(2)}, u32[]{:S(2)}) collective-permute-start(bf16[16,2176]{1,0:T(8,128)(2,1)S(1)} %pad_maximum_fusion.rest_0_), channel_id=1, source_target_pairs={{0,3},{1,2},{2,1},{3,0},{4,7},{5,6},{6,5},{7,4},{8,11},{9,10},{10,... | collective-permute-start | bytes 208904 | tf_op jit(solution)/shard_map/ppermute | solution.py:398
  11.6 0.0 copy-done
  11.6 2.8 %base.1.base_ref = f32[64,512]{1,0:T(8,128)S(1)} custom-call(bf16[2,32,8192]{2,1,0:T(8,128)(2,1)S(1)} %copy-done, bf16[3072,512]{1,0:T(8,128)(2,1)S(1)} %get-tuple-element.33.head_ref, bf16[8192,512]{1,0:T(8,128)(2,1)} %weight_hbm.3), custom_call_target="tpu_custom_call" | custom-call | flops 536870912 | bytes 9437184 | tf_op jit(solution)/shard_map/base/pallas_call | solution.py:151
  14.4 0.0 collective-permute-done.3.rest_3_
  14.4 0.7 %collective-permute-done.2.rest_2_ = bf16[16,2176]{1,0:T(8,128)(2,1)S(1)} collective-permute-done((bf16[16,2176]{1,0:T(8,128)(2,1)S(1)}, bf16[16,2176]{1,0:T(8,128)(2,1)S(1)}, u32[]{:S(2)}, u32[]{:S(2)}) %collective-permute-start.2) | collective-permute-done | bytes 69664 | tf_op jit(solution)/shard_map/ppermute | solution.py:398
  15.1 0.2 %collective-permute-done.1.rest_1_ = bf16[16,2176]{1,0:T(8,128)(2,1)S(1)} collective-permute-done((bf16[16,2176]{1,0:T(8,128)(2,1)S(1)}, bf16[16,2176]{1,0:T(8,128)(2,1)S(1)}, u32[]{:S(2)}, u32[]{:S(2)}) %collective-permute-start.1) | collective-permute-done | bytes 69664 | tf_op jit(solution)/shard_map/ppermute | solution.py:398
  15.4 0.4 %shrink.1 = (f32[192,128]{1,0:T(8,128)S(1)}, bf16[8,16,128]{2,1,0:T(8,128)(2,1)S(1)}) custom-call(bf16[2,32,8192]{2,1,0:T(8,128)(2,1)S(1)} %copy-done, bf16[16,2176]{1,0:T(8,128)(2,1)S(1)} %pad_maximum_fusion.rest_0_, bf16[16,2176]{1,0:T(8,128)(2,1)S(1)} %collective-permute-done.1.rest_1_, bf16[16,2176]{1,0:T(8,128)(2,1)S(1)} %collective-permute-done.2.rest_2_, ...), custom_call_target="tpu_custom_call" | custom-call | tf_op jit(solution)/shard_map/shrink/pallas_call | solution.py:271
  15.8 0.2 %collective-permute-start.4 = (f32[192,128]{1,0:T(8,128)S(1)}, f32[192,128]{1,0:T(8,128)S(1)}, u32[]{:S(2)}, u32[]{:S(2)}) collective-permute-start(f32[192,128]{1,0:T(8,128)S(1)} %get-tuple-element.38.sent_ref), channel_id=1, source_target_pairs={{0,1},{1,0},{2,3},{3,2},{4,5},{5,4},{6,7},{7,6},{8,9},{9,8},{10,11... | collective-permute-start | bytes 294920 | tf_op jit(solution)/shard_map/ppermute | solution.py:402
  16.0 1.2 %collective-permute-done.4.came_ref = f32[192,128]{1,0:T(8,128)S(1)} collective-permute-done((f32[192,128]{1,0:T(8,128)S(1)}, f32[192,128]{1,0:T(8,128)S(1)}, u32[]{:S(2)}, u32[]{:S(2)}) %collective-permute-start.4) | collective-permute-done | bytes 98336 | tf_op jit(solution)/shard_map/ppermute | solution.py:402
  17.2 1.4 %finish.1 = (bf16[2,32,512]{2,1,0:T(8,128)(2,1)}, bf16[2,32,2048]{2,1,0:T(8,128)(2,1)}) custom-call(f32[64,128]{1,0:T(8,128)S(1)} %get-tuple-element.23.live_ref, f32[192,128]{1,0:T(8,128)S(1)} %get-tuple-element.38.sent_ref, f32[192,128]{1,0:T(8,128)S(1)} %collective-permute-done.4.came_ref, bf16[8,16,128]{2,1,0:T(8,128)(2,1)S(1)} %get-tuple-element.39.straight_ref, ...), custom_call_target="tpu_custom_call" | custom-call | tf_op jit(solution)/shard_map/finish/pallas_call | solution.py:350
  (5 shorter events, 0.0 us)
Async XLA Ops:
  0.6 5.4 %copy-start.1 = (bf16[2,32,2048]{2,1,0:T(8,128)(2,1)S(1)}, bf16[2,32,2048]{2,1,0:T(8,128)(2,1)}, u32[]{:S(2)}) copy-start(bf16[2,32,2048]{2,1,0:T(8,128)(2,1)} %query_ref.3) | copy-start | bytes 786436
  0.6 5.4 %copy-start.2 = (bf16[32,64,512]{2,1,0:T(8,128)(2,1)S(1)}, bf16[32,64,512]{2,1,0:T(8,128)(2,1)}, u32[]{:S(2)}) copy-start(bf16[32,64,512]{2,1,0:T(8,128)(2,1)} %cache_ref.1) | copy-start | bytes 6291460
  2.5 9.1 %copy-start = (bf16[2,32,8192]{2,1,0:T(8,128)(2,1)S(1)}, bf16[2,32,8192]{2,1,0:T(8,128)(2,1)}, u32[]{:S(2)}) copy-start(bf16[2,32,8192]{2,1,0:T(8,128)(2,1)} %hidden_ref.1) | copy-start | bytes 3145732
  2.5 5.5 %collective-permute-start = (bf16[16,1152]{1,0:T(8,128)(2,1)S(1)}, bf16[16,1152]{1,0:T(8,128)(2,1)S(1)}, u32[]{:S(2)}, u32[]{:S(2)}) collective-permute-start(bf16[16,1152]{1,0:T(8,128)(2,1)S(1)} %get-tuple-element.25), channel_id=1, source_target_pairs={{0,9},{1,8},{2,11},{3,10},{4,13},{5,12},{6,15},{7,14},{8,1},{9,0},... | collective-permute-start | bytes 110600 | tf_op jit(solution)/shard_map/ppermute | solution.py:389
  8.0 6.4 %collective-permute-start.3 = (bf16[16,2176]{1,0:T(8,128)(2,1)S(1)}, bf16[16,2176]{1,0:T(8,128)(2,1)S(1)}, u32[]{:S(2)}, u32[]{:S(2)}) collective-permute-start(bf16[16,2176]{1,0:T(8,128)(2,1)S(1)} %pad_maximum_fusion.rest_0_), channel_id=1, source_target_pairs={{0,7},{1,6},{2,5},{3,4},{4,3},{5,2},{6,1},{7,0},{8,15},{9,14},{10,... | collective-permute-start | bytes 208904 | tf_op jit(solution)/shard_map/ppermute | solution.py:398
  10.9 4.3 %collective-permute-start.2 = (bf16[16,2176]{1,0:T(8,128)(2,1)S(1)}, bf16[16,2176]{1,0:T(8,128)(2,1)S(1)}, u32[]{:S(2)}, u32[]{:S(2)}) collective-permute-start(bf16[16,2176]{1,0:T(8,128)(2,1)S(1)} %pad_maximum_fusion.rest_0_), channel_id=1, source_target_pairs={{0,5},{1,4},{2,7},{3,6},{4,1},{5,0},{6,3},{7,2},{8,13},{9,12},{10,... | collective-permute-start | bytes 208904 | tf_op jit(solution)/shard_map/ppermute | solution.py:398
  11.2 4.2 %collective-permute-start.1 = (bf16[16,2176]{1,0:T(8,128)(2,1)S(1)}, bf16[16,2176]{1,0:T(8,128)(2,1)S(1)}, u32[]{:S(2)}, u32[]{:S(2)}) collective-permute-start(bf16[16,2176]{1,0:T(8,128)(2,1)S(1)} %pad_maximum_fusion.rest_0_), channel_id=1, source_target_pairs={{0,3},{1,2},{2,1},{3,0},{4,7},{5,6},{6,5},{7,4},{8,11},{9,10},{10,... | collective-permute-start | bytes 208904 | tf_op jit(solution)/shard_map/ppermute | solution.py:398
  15.8 1.4 %collective-permute-start.4 = (f32[192,128]{1,0:T(8,128)S(1)}, f32[192,128]{1,0:T(8,128)S(1)}, u32[]{:S(2)}, u32[]{:S(2)}) collective-permute-start(f32[192,128]{1,0:T(8,128)S(1)} %get-tuple-element.38.sent_ref), channel_id=1, source_target_pairs={{0,1},{1,0},{2,3},{3,2},{4,5},{5,4},{6,7},{7,6},{8,9},{9,8},{10,11... | collective-permute-start | bytes 294920 | tf_op jit(solution)/shard_map/ppermute | solution.py:402

commit v7 on v5

--- a/solution.py
+++ b/solution.py
@@ -283,7 +283,7 @@
 
 def final_kernel(
     groups, size, cols, live_ref, sent_ref, came_ref, straight_ref, base_ref, query_ref, mix_ref, sum_ref, max_ref,
-    new_ref, attn_ref, up_ref,
+    new_hbm, attn_hbm, up_ref, new_ref, attn_ref, out_sem,
 ):
     steps, rows, _ = query_ref.shape
     kv_heads, _, share = mix_ref.shape[:3]
@@ -321,6 +321,8 @@
         value = (live * (base_ref[:, at] + ADAPTER_SCALE * delta)).astype(jnp.bfloat16)
         new_ref[:, :, at] = value.reshape(steps, rows, HEAD)
         fresh.append(value)
+    copies = [pltpu.make_async_copy(new_ref, new_hbm, out_sem.at[0])]
+    copies[0].start()
     todo = [(g, s) for g in range(kv_heads) for s in range(steps)]
     found = []
     for g, s in todo:
@@ -343,6 +345,13 @@
         result = (top / bottom * live_row[None]).astype(jnp.bfloat16)
         for j in range(share):
             attn_ref[s, :, (g * share + j) * HEAD : (g * share + j + 1) * HEAD] = result[j]
+        span = pl.ds(g * share * HEAD, share * HEAD)
+        copies.append(
+            pltpu.make_async_copy(attn_ref.at[s, :, span], attn_hbm.at[s, :, span], out_sem.at[1 + g * steps + s])
+        )
+        copies[-1].start()
+    for copy in copies:
+        copy.wait()
 
 
 def finish(live, sent, came, up, base, query, cached, groups, size, cols):
@@ -354,8 +363,13 @@
             jax.ShapeDtypeStruct(query.shape, jnp.bfloat16),
         ],
         in_specs=[VMEM] * 9,
-        out_specs=[VMEM] * 2,
-        scratch_shapes=[pltpu.VMEM(up.shape, up.dtype)],
+        out_specs=[HBM] * 2,
+        scratch_shapes=[
+            pltpu.VMEM(up.shape, up.dtype),
+            pltpu.VMEM((steps, rows, base.shape[1]), jnp.bfloat16),
+            pltpu.VMEM(query.shape, jnp.bfloat16),
+            pltpu.SemaphoreType.DMA((1 + steps * cached[0].shape[0],)),
+        ],
         compiler_params=pltpu.CompilerParams(vmem_limit_bytes=8 << 20),
         name="finish",
     )(live, sent, came, up, base, query, *cached)

time: 18.6 us -> 18.6 us (level)
  no operation moved by 1% of the time
where the time goes in v7:
time: 18.6 us; the launch traced here: 18.4 us
  Pallas kernels  8.41 us (45%)
  starting transfers between devices  7.43 us (40%)
  waiting for transfers between devices  1.77 us (10%)
  between operations  0.74 us (4%)
    ppermute x3, starting transfers between devices, local(): parts.append(lax.ppermute(arrived, both, crossing(d)))  3.57 us
    ppermute x1, starting transfers between devices, local(): slices = [own, lax.ppermute(other, both, crossing(size))]  3.54 us
    pallas_call x1, Pallas kernels, base_projection(): pl.pallas_call(base_kernel, out_shape=jax.ShapeDtypeStruct((steps * rows,...  2.84 us
    pallas_call x1, Pallas kernels, cache_attention(): pl.pallas_call(cache_kernel, out_shape=[shape] * 3 + [head], in_specs=[VM...  1.99 us
    pallas_call x1, Pallas kernels, pack(): pl.pallas_call(functools.partial(pack_kernel, groups, size, kv_cache.shap...  1.79 us
    pallas_call x1, Pallas kernels, finish(): pl.pallas_call(functools.partial(final_kernel, groups, size, cols), out_s...  1.39 us
    ppermute x1, waiting for transfers between devices, local(): came = lax.ppermute(sent, 'tensor', [(0, 1), (1, 0)])  1.04 us
    ppermute x3, waiting for transfers between devices, local(): parts.append(lax.ppermute(arrived, both, crossing(d)))  0.73 us
  transfers between devices with their start and end apart: 5, of which 3 were waited for; matrix products, arithmetic and copies ran while one was open for 0% of the time, Pallas kernels for 26%

profile of v7, /device:TPU:0, one launch (start us, length us, event | category | flops | bytes accessed | tf_op | source)
XLA Modules:
  0.0 18.4 jit_solution(11085034433698078887)
XLA Ops:
  0.6 0.0 copy-start.1
  0.6 0.0 copy-start.2
  0.7 1.8 %pack.1 = (f32[64,128]{1,0:T(8,128)S(1)}, f32[32,512]{1,0:T(8,128)S(1)}, bf16[16,1152]{1,0:T(8,128)(2,1)S(1)}, bf16[16,1152]{1,0:T(8,128)(2,1)S(1)}) custom-call(s32[2]{0:T(128)} %ids_ref.1, s32[2]{0:T(128)} %fill_ref.1, s32[32]{0:T(128)} %len_ref.1, bf16[1,4096,1024]{2,1,0:T(8,128)(2,1)} %down_ref.1, bf16[1,64,4096]{2,1,0:T(8,128)(2,1)} %up_ref.1), custom_call_target="tpu_custom_call" | custom-call | tf_op jit(solution)/shard_map/pack/pallas_call | solution.py:99
  2.5 3.5 %collective-permute-start = (bf16[16,1152]{1,0:T(8,128)(2,1)S(1)}, bf16[16,1152]{1,0:T(8,128)(2,1)S(1)}, u32[]{:S(2)}, u32[]{:S(2)}) collective-permute-start(bf16[16,1152]{1,0:T(8,128)(2,1)S(1)} %get-tuple-element.25), channel_id=1, source_target_pairs={{0,9},{1,8},{2,11},{3,10},{4,13},{5,12},{6,15},{7,14},{8,1},{9,0},... | collective-permute-start | bytes 110600 | tf_op jit(solution)/shard_map/ppermute | solution.py:403
  6.0 0.0 copy-done.1
  6.0 0.0 copy-done.2
  6.0 0.0 copy-start
  6.0 2.0 %cached.1 = (f32[2,2,8,32,128]{4,3,2,1,0:T(8,128)S(1)}, f32[2,2,8,32,128]{4,3,2,1,0:T(8,128)S(1)}, f32[2,2,8,32,128]{4,3,2,1,0:T(8,128)S(1)}, bf16[3072,512]{1,0:T(8,128)(2,1)S(1)}) custom-call(f32[32,512]{1,0:T(8,128)S(1)} %get-tuple-element.26.bias_ref, bf16[2,32,2048]{2,1,0:T(8,128)(2,1)S(1)} %copy-done.1, bf16[32,64,512]{2,1,0:T(8,128)(2,1)S(1)} %copy-done.2, ...), custom_call_target="tpu_custom_call" | custom-call | flops 10737418240 | bytes 2097152 | tf_op jit(solution)/shard_map/cached/pallas_call | solution.py:219
  8.0 0.0 collective-permute-done
  8.1 2.9 %collective-permute-start.3 = (bf16[16,2176]{1,0:T(8,128)(2,1)S(1)}, bf16[16,2176]{1,0:T(8,128)(2,1)S(1)}, u32[]{:S(2)}, u32[]{:S(2)}) collective-permute-start(bf16[16,2176]{1,0:T(8,128)(2,1)S(1)} %pad_maximum_fusion.rest_0_), channel_id=1, source_target_pairs={{0,7},{1,6},{2,5},{3,4},{4,3},{5,2},{6,1},{7,0},{8,15},{9,14},{10,... | collective-permute-start | bytes 208904 | tf_op jit(solution)/shard_map/ppermute | solution.py:412
  11.0 0.2 %collective-permute-start.2 = (bf16[16,2176]{1,0:T(8,128)(2,1)S(1)}, bf16[16,2176]{1,0:T(8,128)(2,1)S(1)}, u32[]{:S(2)}, u32[]{:S(2)}) collective-permute-start(bf16[16,2176]{1,0:T(8,128)(2,1)S(1)} %pad_maximum_fusion.rest_0_), channel_id=1, source_target_pairs={{0,5},{1,4},{2,7},{3,6},{4,1},{5,0},{6,3},{7,2},{8,13},{9,12},{10,... | collective-permute-start | bytes 208904 | tf_op jit(solution)/shard_map/ppermute | solution.py:412
  11.2 0.5 %collective-permute-start.1 = (bf16[16,2176]{1,0:T(8,128)(2,1)S(1)}, bf16[16,2176]{1,0:T(8,128)(2,1)S(1)}, u32[]{:S(2)}, u32[]{:S(2)}) collective-permute-start(bf16[16,2176]{1,0:T(8,128)(2,1)S(1)} %pad_maximum_fusion.rest_0_), channel_id=1, source_target_pairs={{0,3},{1,2},{2,1},{3,0},{4,7},{5,6},{6,5},{7,4},{8,11},{9,10},{10,... | collective-permute-start | bytes 208904 | tf_op jit(solution)/shard_map/ppermute | solution.py:412
  11.6 0.0 copy-done
  11.6 2.8 %base.1.base_ref = f32[64,512]{1,0:T(8,128)S(1)} custom-call(bf16[2,32,8192]{2,1,0:T(8,128)(2,1)S(1)} %copy-done, bf16[3072,512]{1,0:T(8,128)(2,1)S(1)} %get-tuple-element.33.head_ref, bf16[8192,512]{1,0:T(8,128)(2,1)} %weight_hbm.3), custom_call_target="tpu_custom_call" | custom-call | flops 536870912 | bytes 9437184 | tf_op jit(solution)/shard_map/base/pallas_call | solution.py:151
  14.5 0.0 collective-permute-done.3.rest_3_
  14.5 0.6 %collective-permute-done.2.rest_2_ = bf16[16,2176]{1,0:T(8,128)(2,1)S(1)} collective-permute-done((bf16[16,2176]{1,0:T(8,128)(2,1)S(1)}, bf16[16,2176]{1,0:T(8,128)(2,1)S(1)}, u32[]{:S(2)}, u32[]{:S(2)}) %collective-permute-start.2) | collective-permute-done | bytes 69664 | tf_op jit(solution)/shard_map/ppermute | solution.py:412
  15.2 0.1 collective-permute-done.1.rest_1_
  15.2 0.4 %shrink.1 = (f32[192,128]{1,0:T(8,128)S(1)}, bf16[8,16,128]{2,1,0:T(8,128)(2,1)S(1)}) custom-call(bf16[2,32,8192]{2,1,0:T(8,128)(2,1)S(1)} %copy-done, bf16[16,2176]{1,0:T(8,128)(2,1)S(1)} %pad_maximum_fusion.rest_0_, bf16[16,2176]{1,0:T(8,128)(2,1)S(1)} %collective-permute-done.1.rest_1_, bf16[16,2176]{1,0:T(8,128)(2,1)S(1)} %collective-permute-done.2.rest_2_, ...), custom_call_target="tpu_custom_call" | custom-call | tf_op jit(solution)/shard_map/shrink/pallas_call | solution.py:271
  15.6 0.3 %collective-permute-start.4 = (f32[192,128]{1,0:T(8,128)S(1)}, f32[192,128]{1,0:T(8,128)S(1)}, u32[]{:S(2)}, u32[]{:S(2)}) collective-permute-start(f32[192,128]{1,0:T(8,128)S(1)} %get-tuple-element.38.sent_ref), channel_id=1, source_target_pairs={{0,1},{1,0},{2,3},{3,2},{4,5},{5,4},{6,7},{7,6},{8,9},{9,8},{10,11... | collective-permute-start | bytes 294920 | tf_op jit(solution)/shard_map/ppermute | solution.py:416
  16.0 1.0 %collective-permute-done.4.came_ref = f32[192,128]{1,0:T(8,128)S(1)} collective-permute-done((f32[192,128]{1,0:T(8,128)S(1)}, f32[192,128]{1,0:T(8,128)S(1)}, u32[]{:S(2)}, u32[]{:S(2)}) %collective-permute-start.4) | collective-permute-done | bytes 98336 | tf_op jit(solution)/shard_map/ppermute | solution.py:416
  17.0 1.4 %finish.1 = (bf16[2,32,512]{2,1,0:T(8,128)(2,1)}, bf16[2,32,2048]{2,1,0:T(8,128)(2,1)}) custom-call(f32[64,128]{1,0:T(8,128)S(1)} %get-tuple-element.23.live_ref, f32[192,128]{1,0:T(8,128)S(1)} %get-tuple-element.38.sent_ref, f32[192,128]{1,0:T(8,128)S(1)} %collective-permute-done.4.came_ref, bf16[8,16,128]{2,1,0:T(8,128)(2,1)S(1)} %get-tuple-element.39.straight_ref, ...), custom_call_target="tpu_custom_call" | custom-call | tf_op jit(solution)/shard_map/finish/pallas_call | solution.py:359
  (5 shorter events, 0.0 us)
Async XLA Ops:
  0.6 5.4 %copy-start.1 = (bf16[2,32,2048]{2,1,0:T(8,128)(2,1)S(1)}, bf16[2,32,2048]{2,1,0:T(8,128)(2,1)}, u32[]{:S(2)}) copy-start(bf16[2,32,2048]{2,1,0:T(8,128)(2,1)} %query_ref.3) | copy-start | bytes 786436
  0.6 5.4 %copy-start.2 = (bf16[32,64,512]{2,1,0:T(8,128)(2,1)S(1)}, bf16[32,64,512]{2,1,0:T(8,128)(2,1)}, u32[]{:S(2)}) copy-start(bf16[32,64,512]{2,1,0:T(8,128)(2,1)} %cache_ref.1) | copy-start | bytes 6291460
  2.5 5.6 %collective-permute-start = (bf16[16,1152]{1,0:T(8,128)(2,1)S(1)}, bf16[16,1152]{1,0:T(8,128)(2,1)S(1)}, u32[]{:S(2)}, u32[]{:S(2)}) collective-permute-start(bf16[16,1152]{1,0:T(8,128)(2,1)S(1)} %get-tuple-element.25), channel_id=1, source_target_pairs={{0,9},{1,8},{2,11},{3,10},{4,13},{5,12},{6,15},{7,14},{8,1},{9,0},... | collective-permute-start | bytes 110600 | tf_op jit(solution)/shard_map/ppermute | solution.py:403
  6.0 5.6 %copy-start = (bf16[2,32,8192]{2,1,0:T(8,128)(2,1)S(1)}, bf16[2,32,8192]{2,1,0:T(8,128)(2,1)}, u32[]{:S(2)}) copy-start(bf16[2,32,8192]{2,1,0:T(8,128)(2,1)} %hidden_ref.1) | copy-start | bytes 3145732
  8.1 6.4 %collective-permute-start.3 = (bf16[16,2176]{1,0:T(8,128)(2,1)S(1)}, bf16[16,2176]{1,0:T(8,128)(2,1)S(1)}, u32[]{:S(2)}, u32[]{:S(2)}) collective-permute-start(bf16[16,2176]{1,0:T(8,128)(2,1)S(1)} %pad_maximum_fusion.rest_0_), channel_id=1, source_target_pairs={{0,7},{1,6},{2,5},{3,4},{4,3},{5,2},{6,1},{7,0},{8,15},{9,14},{10,... | collective-permute-start | bytes 208904 | tf_op jit(solution)/shard_map/ppermute | solution.py:412
  11.0 4.2 %collective-permute-start.2 = (bf16[16,2176]{1,0:T(8,128)(2,1)S(1)}, bf16[16,2176]{1,0:T(8,128)(2,1)S(1)}, u32[]{:S(2)}, u32[]{:S(2)}) collective-permute-start(bf16[16,2176]{1,0:T(8,128)(2,1)S(1)} %pad_maximum_fusion.rest_0_), channel_id=1, source_target_pairs={{0,5},{1,4},{2,7},{3,6},{4,1},{5,0},{6,3},{7,2},{8,13},{9,12},{10,... | collective-permute-start | bytes 208904 | tf_op jit(solution)/shard_map/ppermute | solution.py:412
  11.2 4.0 %collective-permute-start.1 = (bf16[16,2176]{1,0:T(8,128)(2,1)S(1)}, bf16[16,2176]{1,0:T(8,128)(2,1)S(1)}, u32[]{:S(2)}, u32[]{:S(2)}) collective-permute-start(bf16[16,2176]{1,0:T(8,128)(2,1)S(1)} %pad_maximum_fusion.rest_0_), channel_id=1, source_target_pairs={{0,3},{1,2},{2,1},{3,0},{4,7},{5,6},{6,5},{7,4},{8,11},{9,10},{10,... | collective-permute-start | bytes 208904 | tf_op jit(solution)/shard_map/ppermute | solution.py:412
  15.6 1.4 %collective-permute-start.4 = (f32[192,128]{1,0:T(8,128)S(1)}, f32[192,128]{1,0:T(8,128)S(1)}, u32[]{:S(2)}, u32[]{:S(2)}) collective-permute-start(f32[192,128]{1,0:T(8,128)S(1)} %get-tuple-element.38.sent_ref), channel_id=1, source_target_pairs={{0,1},{1,0},{2,3},{3,2},{4,5},{5,4},{6,7},{7,6},{8,9},{9,8},{10,11... | collective-permute-start | bytes 294920 | tf_op jit(solution)/shard_map/ppermute | solution.py:416

commit v8 on v5

--- a/solution.py
+++ b/solution.py
@@ -38,7 +38,7 @@
         for k, (source, target) in enumerate(((ids_ref, ids), (fill_ref, fill), (len_ref, lengths)))
     ]
     for copy in small:
-        copy.start()
+        copy.start(priority=1)
     small[0].wait()
     first = serve // size if groups == 2 else 0
     width = down_ref.shape[2]
@@ -57,8 +57,8 @@
         up = pltpu.make_async_copy(
             up_ref.at[0, :, pl.ds(pl.multiple_of(lane, LANES), LANES)], window.at[k], up_sem.at[k]
         )
-        up.start()
-        down.start()
+        up.start(priority=1)
+        down.start(priority=1)
         copies.append((down, up, out))
         starts.append(adapter * RANK - lane)
     small[1].wait()

time: 18.6 us -> 18.6 us (level)
  no operation moved by 1% of the time
where the time goes in v8:
time: 18.6 us; the launch traced here: 18.4 us
  Pallas kernels  8.44 us (45%)
  starting transfers between devices  7.43 us (40%)
  waiting for transfers between devices  1.77 us (10%)
  between operations  0.74 us (4%)
    ppermute x3, starting transfers between devices, local(): parts.append(lax.ppermute(arrived, both, crossing(d)))  3.57 us
    ppermute x1, starting transfers between devices, local(): slices = [own, lax.ppermute(other, both, crossing(size))]  3.54 us
    pallas_call x1, Pallas kernels, base_projection(): pl.pallas_call(base_kernel, out_shape=jax.ShapeDtypeStruct((steps * rows,...  2.84 us
    pallas_call x1, Pallas kernels, cache_attention(): pl.pallas_call(cache_kernel, out_shape=[shape] * 3 + [head], in_specs=[VM...  1.99 us
    pallas_call x1, Pallas kernels, pack(): pl.pallas_call(functools.partial(pack_kernel, groups, size, kv_cache.shap...  1.79 us
    pallas_call x1, Pallas kernels, finish(): pl.pallas_call(functools.partial(final_kernel, groups, size, cols), out_s...  1.41 us
    ppermute x1, waiting for transfers between devices, local(): came = lax.ppermute(sent, 'tensor', [(0, 1), (1, 0)])  1.04 us
    ppermute x3, waiting for transfers between devices, local(): parts.append(lax.ppermute(arrived, both, crossing(d)))  0.73 us
  transfers between devices with their start and end apart: 5, of which 3 were waited for; matrix products, arithmetic and copies ran while one was open for 0% of the time, Pallas kernels for 26%

profile of v8, /device:TPU:0, one launch (start us, length us, event | category | flops | bytes accessed | tf_op | source)
XLA Modules:
  0.0 18.4 jit_solution(11297379353198760330)
XLA Ops:
  0.6 0.0 copy-start.1
  0.6 0.0 copy-start.2
  0.7 1.8 %pack.1 = (f32[64,128]{1,0:T(8,128)S(1)}, f32[32,512]{1,0:T(8,128)S(1)}, bf16[16,1152]{1,0:T(8,128)(2,1)S(1)}, bf16[16,1152]{1,0:T(8,128)(2,1)S(1)}) custom-call(s32[2]{0:T(128)} %ids_ref.1, s32[2]{0:T(128)} %fill_ref.1, s32[32]{0:T(128)} %len_ref.1, bf16[1,4096,1024]{2,1,0:T(8,128)(2,1)} %down_ref.1, bf16[1,64,4096]{2,1,0:T(8,128)(2,1)} %up_ref.1), custom_call_target="tpu_custom_call" | custom-call | tf_op jit(solution)/shard_map/pack/pallas_call | solution.py:99
  2.5 3.5 %collective-permute-start = (bf16[16,1152]{1,0:T(8,128)(2,1)S(1)}, bf16[16,1152]{1,0:T(8,128)(2,1)S(1)}, u32[]{:S(2)}, u32[]{:S(2)}) collective-permute-start(bf16[16,1152]{1,0:T(8,128)(2,1)S(1)} %get-tuple-element.25), channel_id=1, source_target_pairs={{0,9},{1,8},{2,11},{3,10},{4,13},{5,12},{6,15},{7,14},{8,1},{9,0},... | collective-permute-start | bytes 110600 | tf_op jit(solution)/shard_map/ppermute | solution.py:389
  6.0 0.0 copy-done.1
  6.0 0.0 copy-done.2
  6.0 0.0 copy-start
  6.0 2.0 %cached.1 = (f32[2,2,8,32,128]{4,3,2,1,0:T(8,128)S(1)}, f32[2,2,8,32,128]{4,3,2,1,0:T(8,128)S(1)}, f32[2,2,8,32,128]{4,3,2,1,0:T(8,128)S(1)}, bf16[3072,512]{1,0:T(8,128)(2,1)S(1)}) custom-call(f32[32,512]{1,0:T(8,128)S(1)} %get-tuple-element.26.bias_ref, bf16[2,32,2048]{2,1,0:T(8,128)(2,1)S(1)} %copy-done.1, bf16[32,64,512]{2,1,0:T(8,128)(2,1)S(1)} %copy-done.2, ...), custom_call_target="tpu_custom_call" | custom-call | flops 10737418240 | bytes 2097152 | tf_op jit(solution)/shard_map/cached/pallas_call | solution.py:219
  8.0 0.0 collective-permute-done
  8.1 2.9 %collective-permute-start.3 = (bf16[16,2176]{1,0:T(8,128)(2,1)S(1)}, bf16[16,2176]{1,0:T(8,128)(2,1)S(1)}, u32[]{:S(2)}, u32[]{:S(2)}) collective-permute-start(bf16[16,2176]{1,0:T(8,128)(2,1)S(1)} %pad_maximum_fusion.rest_0_), channel_id=1, source_target_pairs={{0,7},{1,6},{2,5},{3,4},{4,3},{5,2},{6,1},{7,0},{8,15},{9,14},{10,... | collective-permute-start | bytes 208904 | tf_op jit(solution)/shard_map/ppermute | solution.py:398
  11.0 0.2 %collective-permute-start.2 = (bf16[16,2176]{1,0:T(8,128)(2,1)S(1)}, bf16[16,2176]{1,0:T(8,128)(2,1)S(1)}, u32[]{:S(2)}, u32[]{:S(2)}) collective-permute-start(bf16[16,2176]{1,0:T(8,128)(2,1)S(1)} %pad_maximum_fusion.rest_0_), channel_id=1, source_target_pairs={{0,5},{1,4},{2,7},{3,6},{4,1},{5,0},{6,3},{7,2},{8,13},{9,12},{10,... | collective-permute-start | bytes 208904 | tf_op jit(solution)/shard_map/ppermute | solution.py:398
  11.2 0.5 %collective-permute-start.1 = (bf16[16,2176]{1,0:T(8,128)(2,1)S(1)}, bf16[16,2176]{1,0:T(8,128)(2,1)S(1)}, u32[]{:S(2)}, u32[]{:S(2)}) collective-permute-start(bf16[16,2176]{1,0:T(8,128)(2,1)S(1)} %pad_maximum_fusion.rest_0_), channel_id=1, source_target_pairs={{0,3},{1,2},{2,1},{3,0},{4,7},{5,6},{6,5},{7,4},{8,11},{9,10},{10,... | collective-permute-start | bytes 208904 | tf_op jit(solution)/shard_map/ppermute | solution.py:398
  11.6 0.0 copy-done
  11.6 2.8 %base.1.base_ref = f32[64,512]{1,0:T(8,128)S(1)} custom-call(bf16[2,32,8192]{2,1,0:T(8,128)(2,1)S(1)} %copy-done, bf16[3072,512]{1,0:T(8,128)(2,1)S(1)} %get-tuple-element.33.head_ref, bf16[8192,512]{1,0:T(8,128)(2,1)} %weight_hbm.3), custom_call_target="tpu_custom_call" | custom-call | flops 536870912 | bytes 9437184 | tf_op jit(solution)/shard_map/base/pallas_call | solution.py:151
  14.5 0.0 collective-permute-done.3.rest_3_
  14.5 0.6 %collective-permute-done.2.rest_2_ = bf16[16,2176]{1,0:T(8,128)(2,1)S(1)} collective-permute-done((bf16[16,2176]{1,0:T(8,128)(2,1)S(1)}, bf16[16,2176]{1,0:T(8,128)(2,1)S(1)}, u32[]{:S(2)}, u32[]{:S(2)}) %collective-permute-start.2) | collective-permute-done | bytes 69664 | tf_op jit(solution)/shard_map/ppermute | solution.py:398
  15.2 0.1 collective-permute-done.1.rest_1_
  15.2 0.4 %shrink.1 = (f32[192,128]{1,0:T(8,128)S(1)}, bf16[8,16,128]{2,1,0:T(8,128)(2,1)S(1)}) custom-call(bf16[2,32,8192]{2,1,0:T(8,128)(2,1)S(1)} %copy-done, bf16[16,2176]{1,0:T(8,128)(2,1)S(1)} %pad_maximum_fusion.rest_0_, bf16[16,2176]{1,0:T(8,128)(2,1)S(1)} %collective-permute-done.1.rest_1_, bf16[16,2176]{1,0:T(8,128)(2,1)S(1)} %collective-permute-done.2.rest_2_, ...), custom_call_target="tpu_custom_call" | custom-call | tf_op jit(solution)/shard_map/shrink/pallas_call | solution.py:271
  15.6 0.3 %collective-permute-start.4 = (f32[192,128]{1,0:T(8,128)S(1)}, f32[192,128]{1,0:T(8,128)S(1)}, u32[]{:S(2)}, u32[]{:S(2)}) collective-permute-start(f32[192,128]{1,0:T(8,128)S(1)} %get-tuple-element.38.sent_ref), channel_id=1, source_target_pairs={{0,1},{1,0},{2,3},{3,2},{4,5},{5,4},{6,7},{7,6},{8,9},{9,8},{10,11... | collective-permute-start | bytes 294920 | tf_op jit(solution)/shard_map/ppermute | solution.py:402
  16.0 1.0 %collective-permute-done.4.came_ref = f32[192,128]{1,0:T(8,128)S(1)} collective-permute-done((f32[192,128]{1,0:T(8,128)S(1)}, f32[192,128]{1,0:T(8,128)S(1)}, u32[]{:S(2)}, u32[]{:S(2)}) %collective-permute-start.4) | collective-permute-done | bytes 98336 | tf_op jit(solution)/shard_map/ppermute | solution.py:402
  17.0 1.4 %finish.1 = (bf16[2,32,512]{2,1,0:T(8,128)(2,1)}, bf16[2,32,2048]{2,1,0:T(8,128)(2,1)}) custom-call(f32[64,128]{1,0:T(8,128)S(1)} %get-tuple-element.23.live_ref, f32[192,128]{1,0:T(8,128)S(1)} %get-tuple-element.38.sent_ref, f32[192,128]{1,0:T(8,128)S(1)} %collective-permute-done.4.came_ref, bf16[8,16,128]{2,1,0:T(8,128)(2,1)S(1)} %get-tuple-element.39.straight_ref, ...), custom_call_target="tpu_custom_call" | custom-call | tf_op jit(solution)/shard_map/finish/pallas_call | solution.py:350
  (5 shorter events, 0.0 us)
Async XLA Ops:
  0.6 5.4 %copy-start.1 = (bf16[2,32,2048]{2,1,0:T(8,128)(2,1)S(1)}, bf16[2,32,2048]{2,1,0:T(8,128)(2,1)}, u32[]{:S(2)}) copy-start(bf16[2,32,2048]{2,1,0:T(8,128)(2,1)} %query_ref.3) | copy-start | bytes 786436
  0.6 5.4 %copy-start.2 = (bf16[32,64,512]{2,1,0:T(8,128)(2,1)S(1)}, bf16[32,64,512]{2,1,0:T(8,128)(2,1)}, u32[]{:S(2)}) copy-start(bf16[32,64,512]{2,1,0:T(8,128)(2,1)} %cache_ref.1) | copy-start | bytes 6291460
  2.5 5.6 %collective-permute-start = (bf16[16,1152]{1,0:T(8,128)(2,1)S(1)}, bf16[16,1152]{1,0:T(8,128)(2,1)S(1)}, u32[]{:S(2)}, u32[]{:S(2)}) collective-permute-start(bf16[16,1152]{1,0:T(8,128)(2,1)S(1)} %get-tuple-element.25), channel_id=1, source_target_pairs={{0,9},{1,8},{2,11},{3,10},{4,13},{5,12},{6,15},{7,14},{8,1},{9,0},... | collective-permute-start | bytes 110600 | tf_op jit(solution)/shard_map/ppermute | solution.py:389
  6.0 5.6 %copy-start = (bf16[2,32,8192]{2,1,0:T(8,128)(2,1)S(1)}, bf16[2,32,8192]{2,1,0:T(8,128)(2,1)}, u32[]{:S(2)}) copy-start(bf16[2,32,8192]{2,1,0:T(8,128)(2,1)} %hidden_ref.1) | copy-start | bytes 3145732
  8.1 6.4 %collective-permute-start.3 = (bf16[16,2176]{1,0:T(8,128)(2,1)S(1)}, bf16[16,2176]{1,0:T(8,128)(2,1)S(1)}, u32[]{:S(2)}, u32[]{:S(2)}) collective-permute-start(bf16[16,2176]{1,0:T(8,128)(2,1)S(1)} %pad_maximum_fusion.rest_0_), channel_id=1, source_target_pairs={{0,7},{1,6},{2,5},{3,4},{4,3},{5,2},{6,1},{7,0},{8,15},{9,14},{10,... | collective-permute-start | bytes 208904 | tf_op jit(solution)/shard_map/ppermute | solution.py:398
  11.0 4.2 %collective-permute-start.2 = (bf16[16,2176]{1,0:T(8,128)(2,1)S(1)}, bf16[16,2176]{1,0:T(8,128)(2,1)S(1)}, u32[]{:S(2)}, u32[]{:S(2)}) collective-permute-start(bf16[16,2176]{1,0:T(8,128)(2,1)S(1)} %pad_maximum_fusion.rest_0_), channel_id=1, source_target_pairs={{0,5},{1,4},{2,7},{3,6},{4,1},{5,0},{6,3},{7,2},{8,13},{9,12},{10,... | collective-permute-start | bytes 208904 | tf_op jit(solution)/shard_map/ppermute | solution.py:398
  11.2 4.0 %collective-permute-start.1 = (bf16[16,2176]{1,0:T(8,128)(2,1)S(1)}, bf16[16,2176]{1,0:T(8,128)(2,1)S(1)}, u32[]{:S(2)}, u32[]{:S(2)}) collective-permute-start(bf16[16,2176]{1,0:T(8,128)(2,1)S(1)} %pad_maximum_fusion.rest_0_), channel_id=1, source_target_pairs={{0,3},{1,2},{2,1},{3,0},{4,7},{5,6},{6,5},{7,4},{8,11},{9,10},{10,... | collective-permute-start | bytes 208904 | tf_op jit(solution)/shard_map/ppermute | solution.py:398
  15.6 1.4 %collective-permute-start.4 = (f32[192,128]{1,0:T(8,128)S(1)}, f32[192,128]{1,0:T(8,128)S(1)}, u32[]{:S(2)}, u32[]{:S(2)}) collective-permute-start(f32[192,128]{1,0:T(8,128)S(1)} %get-tuple-element.38.sent_ref), channel_id=1, source_target_pairs={{0,1},{1,0},{2,3},{3,2},{4,5},{5,4},{6,7},{7,6},{8,9},{9,8},{10,11... | collective-permute-start | bytes 294920 | tf_op jit(solution)/shard_map/ppermute | solution.py:402
